TPU v7x, 32 devices: a whole 2x2x4 slice. The times are simulated.
32 devices in a mesh: group: 8 (over y, x, core), local: 4 (over z).
Axes of the slice: x: 2, y: 2, z: 4, core: 2. Of those that a mesh axis runs over, the one named last changes fastest.
Arguments:
- inputs: bfloat16 [8192, 768], P(('group', 'local')), may hold values from -6 to 6
- norm_one: bfloat16 [768], P(('group', 'local')), may hold values from 0.25 to 1.75
- w_query: bfloat16 [768, 768], P(('group', 'local')), may hold values from -0.21875 to 0.21875
- w_key: bfloat16 [768, 768], P(('group', 'local')), may hold values from -0.21875 to 0.21875
- w_value: bfloat16 [768, 768], P(('group', 'local')), may hold values from -0.21875 to 0.21875
- w_output: bfloat16 [768, 768], P(('group', 'local')), may hold values from -4 to 4
- norm_two: bfloat16 [768], P(('group', 'local')), may hold values from 0.25 to 1.75
- w_router: bfloat16 [768, 32], P(('group', 'local')), may hold values from -0.109375 to 0.109375
- expert_in: bfloat16 [32, 768, 3072], P(('group', 'local')), may hold values from -0.21875 to 0.21875
- expert_out: bfloat16 [32, 3072, 768], P(('group', 'local')), may hold values from -6 to 6
- routes: int32 [8192, 1], P(('group', 'local')), may hold values from 0 to 31; in each aligned block of 256 rows (0 to 255, 256 to 511, ...) at most 16 rows name the same one
- cotangent: bfloat16 [8192, 768], P(('group', 'local')), may hold values from -6 to 6
Outputs:
- output: bfloat16 [8192, 768], P(('group', 'local'))
- grad_input: float32 [8192, 768], P(('group', 'local'))
- grad_norm_one: float32 [768], P(('group', 'local'))
- grad_w_query: float32 [768, 768], P(('group', 'local'))
- grad_w_key: float32 [768, 768], P(('group', 'local'))
- grad_w_value: float32 [768, 768], P(('group', 'local'))
- grad_w_output: float32 [768, 768], P(('group', 'local'))
- grad_norm_two: float32 [768], P(('group', 'local'))
- grad_w_router: float32 [768, 32], P(('group', 'local'))
- grad_expert_in: float32 [32, 768, 3072], P(('group', 'local'))
- grad_expert_out: float32 [32, 3072, 768], P(('group', 'local'))
Inputs may be any that keep to these rules, and one draw needn't show every extreme that they name: `routes`: in each aligned block of 256 rows (the rows of one device) no expert is named by more than 16 rows, a bound that some block reaches.
All inputs are finite; a program needn't handle non-finite values.
Results may differ from a plain program's by a relative error of at most 0.017.
Values may be sent and summed in bfloat16 or wider, within the bound.
No kernel may reach another device: no remote copies, remote signals or barrier semaphores. Data moves between devices by JAX's collectives and lax.ppermute only.
A program may use at most 128 MiB of HBM per device.

v0:
```python
import functools

import jax
import jax.numpy as jnp
from jax import lax
from jax.experimental import pallas as pl
from jax.experimental.pallas import tpu as pltpu
from jax.sharding import PartitionSpec as P

HEAD_DIM = 64
AXES = ("group", "local")
BF = jnp.bfloat16
F32 = jnp.float32
EPSILON = 1e-06
VMEM_BYTES = 58 * 2**20
SMALL_BYTES = 24 * 2**20


def dot(left, right):
    return jnp.dot(left, right, preferred_element_type=F32)


def dot_tn(left, right):
    return lax.dot_general(left, right, (((0,), (0,)), ((), ())), preferred_element_type=F32)


def dot_nt(left, right):
    return lax.dot_general(left, right, (((1,), (1,)), ((), ())), preferred_element_type=F32)


class Links:
    def __init__(self):
        self.groups = lax.axis_size("group")
        self.levels = lax.axis_size("local")
        self.group = lax.axis_index("group")
        self.level = lax.axis_index("local")
        self.core = self.group % 2

    def permute(self, array, target):
        pairs = []
        for group in range(self.groups):
            for level in range(self.levels):
                other_group, other_level = target(group, level)
                pairs.append((group * self.levels + level, other_group * self.levels + other_level))
        return lax.ppermute(array, AXES, pairs)

    def swap_core(self, array):
        return self.permute(array, lambda g, l: (g ^ 1, l))

    def swap_level(self, array, mask):
        return self.permute(array, lambda g, l: (g, l ^ mask))

    def swap_group(self, array, mask):
        return self.permute(array, lambda g, l: (g ^ (2 * mask), l))


def gate(array, *after):
    return lax.optimization_barrier((array, *after))[0]


def tie(*arrays):
    return lax.optimization_barrier(arrays)


def pick(flag, first, second):
    return jnp.where(flag == 0, first, second)


def joined(flag, mine, other, axis=0):
    return jnp.concatenate([pick(flag, mine, other), pick(flag, other, mine)], axis=axis)


def ordered(index, parts):
    count = len(parts)
    if count == 1:
        return parts[0]
    top = count.bit_length() - 2
    half = count // 2
    low = index & (half - 1)
    return joined((index >> top) & 1, ordered(low, parts[:half]), ordered(low, parts[half:]))


def rows_of(array, index, rows):
    return lax.dynamic_slice_in_dim(array, index * rows, rows, axis=0)


def gather_levels(links, pieces):
    got = tie(*[links.swap_level(pieces[b], b) for b in range(1, links.levels)])
    return ordered(links.level, [pieces[0], *got])


def gather_groups(links, block):
    return [block] + [links.swap_group(block, m) for m in range(1, links.groups // 2)]


def in_order(links, own, other):
    pairs = [joined(links.core, mine, far) for mine, far in zip(own, other)]
    return ordered(links.group >> 1, pairs)


def reduce_cores(links, keep, send):
    return keep + links.swap_core(send).astype(F32)


def reduce_groups(links, parts):
    got = [links.swap_group(parts[m].astype(BF), m) for m in range(1, len(parts))]
    total = parts[0]
    for part in tie(*got):
        total = total + part.astype(F32)
    return total


def reduce_levels(links, block):
    rows = block.shape[0] // links.levels
    parts = [rows_of(block, links.level ^ b, rows) for b in range(links.levels)]
    got = tie(*[links.swap_level(parts[b].astype(BF), b) for b in range(1, links.levels)])
    return [parts[0]] + [part.astype(F32) for part in got]


def owner_to_workers(links, array):
    half = array.shape[0] // 2
    mine = pick(links.core, array[:half], array[half:])
    other = links.swap_core(pick(links.core, array[half:], array[:half]))
    same = (links.level >> 1) ^ links.core
    return pick(same, mine, other), pick(same, other, mine)


def workers_to_owner(links, near, far):
    same = (links.level >> 1) ^ links.core
    mine = pick(same, near, far)
    other = links.swap_core(pick(same, far, near))
    return joined(links.core, mine, other)


PAIR = 2 * HEAD_DIM


def head_masks(dtype):
    lanes = lax.broadcasted_iota(jnp.int32, (1, PAIR), 1)
    return [(lanes // HEAD_DIM == head).astype(dtype) for head in range(2)]


def forward_kernel(
    query_ref, key_ref, value_ref, key_far_ref, value_far_ref, zero_ref, one_ref, two_ref, three_ref, probs_ref
):
    rows = query_ref.shape[0]
    query = query_ref[...] * BF(HEAD_DIM**-0.5)
    key = jnp.concatenate([key_ref[...], key_far_ref[...]], axis=0)
    value = jnp.concatenate([value_ref[...], value_far_ref[...]], axis=0)
    mixed = jnp.zeros((rows, PAIR), F32)
    for head, mask in enumerate(head_masks(BF)):
        scores = dot_nt(query * mask, key)
        weights = jnp.exp(scores - jnp.max(scores, axis=1, keepdims=True))
        probs = (weights * (1.0 / jnp.sum(weights, axis=1, keepdims=True))).astype(BF)
        probs_ref[head] = probs
        mixed = mixed + dot(probs, value * mask)
    mixed = mixed.astype(BF)
    part_rows = rows // 4
    for part, ref in enumerate((zero_ref, one_ref, two_ref, three_ref)):
        ref[...] = mixed[part * part_rows : (part + 1) * part_rows]


def pair_column(rows, block=0):
    return pl.BlockSpec((rows, PAIR), lambda i: (0, block + i))


def probs_block(rows):
    return pl.BlockSpec((2, rows, 2 * rows), lambda i: (i, 0, 0))


def attention_forward(queries, pair, pair_far):
    rows, half_width = queries.shape
    pairs = half_width // PAIR
    return pl.pallas_call(
        forward_kernel,
        grid=(pairs,),
        in_specs=[pair_column(rows)] + [pair_column(rows), pair_column(rows, pairs)] * 2,
        out_specs=[pair_column(rows // 4)] * 4 + [probs_block(rows)],
        out_shape=[jax.ShapeDtypeStruct((rows // 4, half_width), BF)] * 4
        + [jax.ShapeDtypeStruct((2 * pairs, rows, 2 * rows), BF)],
        compiler_params=params(),
        cost_estimate=cost(2 * 10**10, 4096),
    )(queries, pair, pair, pair_far, pair_far)


def backward_kernel(query_ref, key_ref, value_ref, key_far_ref, value_far_ref, probs_ref, *refs):
    grad_refs, mixed_refs = refs[:4], refs[4:8]
    grad_query_ref, grad_near_ref, grad_far_ref = refs[8:]
    rows = query_ref.shape[0]
    factor = BF(HEAD_DIM**-0.5)
    query = query_ref[...] * factor
    key = jnp.concatenate([key_ref[...], key_far_ref[...]], axis=0)
    value = jnp.concatenate([value_ref[...], value_far_ref[...]], axis=0)
    grad = jnp.concatenate([ref[...] for ref in grad_refs], axis=0)
    mixed = jnp.concatenate([ref[...] for ref in mixed_refs], axis=0)
    together = grad.astype(F32) * mixed.astype(F32)
    grad_query = jnp.zeros((rows, PAIR), F32)
    grad_key = jnp.zeros((2 * rows, PAIR), F32)
    grad_value = jnp.zeros((2 * rows, PAIR), F32)
    for head, (mask, mask_wide) in enumerate(zip(head_masks(BF), head_masks(F32))):
        probs = probs_ref[head]
        grad_one = grad * mask
        row_dots = jnp.sum(together * mask_wide, axis=1, keepdims=True)
        grad_probs = dot_nt(grad_one, value)
        grad_scores = (probs.astype(F32) * (grad_probs - row_dots)).astype(BF)
        grad_value = grad_value + dot_tn(probs, grad_one)
        grad_key = grad_key + dot_tn(grad_scores, query * mask)
        grad_query = grad_query + dot(grad_scores, key * (mask * factor))
    grad_query_ref[...] = grad_query.astype(BF)
    for index, total in enumerate((grad_key, grad_value)):
        grad_near_ref[index] = total[:rows].astype(BF)
        grad_far_ref[index] = total[rows:].astype(BF)


def attention_backward(queries, pair, pair_far, probs, grads, mixed):
    rows, half_width = queries.shape
    pairs = half_width // PAIR
    return pl.pallas_call(
        backward_kernel,
        grid=(pairs,),
        in_specs=[pair_column(rows)]
        + [pair_column(rows), pair_column(rows, pairs)] * 2
        + [probs_block(rows)]
        + [pair_column(rows // 4)] * 8,
        out_specs=[pair_column(rows)] + [pl.BlockSpec((2, rows, PAIR), lambda i: (0, 0, i))] * 2,
        out_shape=[jax.ShapeDtypeStruct((rows, half_width), BF)]
        + [jax.ShapeDtypeStruct((2, rows, half_width), BF)] * 2,
        compiler_params=params(),
        cost_estimate=cost(2 * 10**10, 4096),
    )(queries, pair, pair, pair_far, pair_far, probs, *grads, *mixed)


GELU_SCALE = 0.7978845608028654
GELU_CUBE = 0.044715


def gelu_and_slope(values):
    square = values * values
    bend = jnp.tanh(GELU_SCALE * values * (1.0 + GELU_CUBE * square))
    half = 0.5 + 0.5 * bend
    slope = half + 0.5 * values * (1.0 - bend * bend) * GELU_SCALE * (1.0 + 3 * GELU_CUBE * square)
    return values * half, slope


def whole(shape):
    return pl.BlockSpec(shape, lambda *_: (0,) * len(shape))


FLAGS = pl.BlockSpec(memory_space=pltpu.SMEM)
CORE, HALF, SAME, DEVICE, PLACE = range(5)


def params(size=VMEM_BYTES):
    return pltpu.CompilerParams(vmem_limit_bytes=size)


def cost(flops, size):
    return pl.CostEstimate(flops=flops, bytes_accessed=size, transcendentals=0)


def one_step(kernel, flags, operands, shapes, scratch=(), size=VMEM_BYTES):
    return pl.pallas_call(
        kernel,
        grid=(1,),
        in_specs=[FLAGS] + [whole(operand.shape) for operand in operands],
        out_specs=[whole(shape.shape) for shape in shapes],
        out_shape=shapes,
        scratch_shapes=list(scratch),
        compiler_params=params(size),
        cost_estimate=cost(0, 2**20),
    )(flags, *operands)


def low_shape(*shape):
    return jax.ShapeDtypeStruct(shape, BF)


def wide_shape(*shape):
    return jax.ShapeDtypeStruct(shape, F32)


def each_case(flags_ref, body):
    for half in range(2):
        for same in range(2):

            @pl.when((flags_ref[HALF] == half) & (flags_ref[SAME] == same))
            def _(half=half, same=same):
                body(half, same)


def project_kernel(count, flags_ref, normed_ref, *refs):
    own_refs, other_refs = refs[:count], refs[count : 2 * count]
    query_ref, pair_ref, weight_ref = refs[2 * count :]
    rows = own_refs[0].shape[0]
    core = flags_ref[CORE]
    for m in range(count):
        place = 2 * (flags_ref[PLACE] ^ m)
        for index, ref in ((place + core, own_refs[m]), (place + 1 - core, other_refs[m])):
            weight_ref[pl.ds(pl.multiple_of(index * rows, 16), rows), :] = ref[...]
    projected = dot(normed_ref[...], weight_ref[...]).astype(BF)
    query_ref[...] = projected[:, : query_ref.shape[1]]
    pair_ref[...] = projected[:, query_ref.shape[1] :]


def project(flags, normed, own, other):
    count = len(own)
    rows, width = normed.shape
    columns = own[0].shape[1]
    shapes = [
        low_shape(rows, columns // 3),
        low_shape(rows, columns * 2 // 3),
        low_shape(width, columns),
    ]
    kernel = functools.partial(project_kernel, count)
    return one_step(kernel, flags, [normed, *own, *other], shapes, size=SMALL_BYTES)


def mixed_route_kernel(flags_ref, zero_ref, one_ref, two_ref, three_ref, mine_ref, sent_ref):
    half_width = zero_ref.shape[1]

    def body(half, same):
        near_ref, far_ref = (mine_ref, sent_ref) if same == 0 else (sent_ref, mine_ref)
        for into_ref, refs in ((near_ref, (zero_ref, one_ref)), (far_ref, (two_ref, three_ref))):
            into_ref[:, :half_width] = refs[half][...]
            into_ref[:, half_width:] = refs[1 - half][...]

    each_case(flags_ref, body)


def mixed_route(flags, parts):
    rows, half_width = parts[0].shape
    shapes = [low_shape(rows, 2 * half_width)] * 2
    return one_step(mixed_route_kernel, flags, parts, shapes, size=SMALL_BYTES)


def grad_route_kernel(flags_ref, mine_ref, got_ref, zero_ref, one_ref, two_ref, three_ref):
    half_width = zero_ref.shape[1]

    def body(half, same):
        near_ref, far_ref = (mine_ref, got_ref) if same == 0 else (got_ref, mine_ref)
        for from_ref, refs in ((near_ref, (zero_ref, one_ref)), (far_ref, (two_ref, three_ref))):
            refs[half][...] = from_ref[:, :half_width]
            refs[1 - half][...] = from_ref[:, half_width:]

    each_case(flags_ref, body)


def grad_route(flags, mine, got):
    rows, width = mine.shape
    shapes = [low_shape(rows, width // 2)] * 4
    return one_step(grad_route_kernel, flags, [mine, got], shapes, size=SMALL_BYTES)


def owner_forward_kernel(
    flags_ref,
    mine_ref,
    got_ref,
    inputs_ref,
    weight_ref,
    gain_ref,
    to_slots_ref,
    mixed_ref,
    middle_ref,
    slots_ref,
):
    half_rows = mine_ref.shape[0]
    for core in range(2):

        @pl.when(flags_ref[CORE] == core)
        def _(core=core):
            refs = (mine_ref, got_ref)
            mixed_ref[:half_rows] = refs[core][...]
            mixed_ref[half_rows:] = refs[1 - core][...]

    weight = weight_ref[:, : mixed_ref.shape[1]]
    middle = inputs_ref[...].astype(F32) + dot(mixed_ref[...], weight)
    middle_ref[...] = middle
    inverse = lax.rsqrt(jnp.mean(middle * middle, axis=1, keepdims=True) + EPSILON)
    second_low = (middle * inverse * gain_ref[...]).astype(BF)
    slots_ref[...] = dot(to_slots_ref[...], second_low).astype(BF)


def owner_forward(flags, mine, got, inputs, full_extra, gain, to_slots):
    rows, width = inputs.shape
    shapes = [
        low_shape(rows, width),
        wide_shape(rows, width),
        low_shape(to_slots.shape[0], width),
    ]
    operands = [mine, got, inputs, full_extra, gain, to_slots]
    return one_step(owner_forward_kernel, flags, operands, shapes)


def expert_kernel(
    flags_ref,
    arrived_ref,
    cot_ref,
    compact_ref,
    expand_ref,
    router_ref,
    weight_in_ref,
    weight_out_ref,
    held_ref,
    grad_result_ref,
    hidden_ref,
    grad_inner_ref,
    grad_back_ref,
    taken_back_ref,
    grad_logits_ref,
    result_sum,
    grad_sum,
    cot_held,
    probs,
    gates,
):
    step = pl.program_id(0)
    experts = router_ref.shape[1]
    lanes = lax.broadcasted_iota(jnp.int32, (1, experts), 1)
    mine = (lanes == flags_ref[DEVICE]).astype(F32)

    @pl.when(step == 0)
    def _():
        held = dot(compact_ref[...], arrived_ref[...]).astype(BF)
        held_ref[...] = held
        cot = dot(compact_ref[...], cot_ref[...])
        cot_held[...] = cot
        logits = dot(held, router_ref[...])
        weights = jnp.exp(logits - jnp.max(logits, axis=1, keepdims=True))
        router_probs = weights / jnp.sum(weights, axis=1, keepdims=True)
        probs[...] = router_probs
        gate = jnp.sum(router_probs * mine, axis=1, keepdims=True)
        gates[...] = gate
        grad_result_ref[...] = (gate * cot).astype(BF)
        result_sum[...] = jnp.zeros_like(result_sum)
        grad_sum[...] = jnp.zeros_like(grad_sum)

    weight_in = weight_in_ref[0]
    weight_out = weight_out_ref[0]
    hidden, slope = gelu_and_slope(dot(held_ref[...], weight_in))
    hidden = hidden.astype(BF)
    hidden_ref[...] = hidden
    grad_inner = (dot_nt(grad_result_ref[...], weight_out) * slope).astype(BF)
    grad_inner_ref[...] = grad_inner
    result_sum[...] += dot(hidden, weight_out)
    grad_sum[...] += dot_nt(grad_inner, weight_in)

    @pl.when(step == pl.num_programs(0) - 1)
    def _():
        result = result_sum[...].astype(BF).astype(F32)
        gate = gates[...]
        grad_gate = jnp.sum(cot_held[...] * result, axis=1, keepdims=True)
        grad_logits = (grad_gate * probs[...] * (mine - gate)).astype(BF)
        grad_logits_ref[...] = grad_logits
        grad_held = grad_sum[...] + dot_nt(grad_logits, router_ref[...])
        grad_back_ref[...] = dot(expand_ref[...], grad_held.astype(BF)).astype(BF)
        taken_back_ref[...] = dot(expand_ref[...], (gate * result).astype(BF)).astype(BF)


def expert_layer(flags, arrived, cot, compact, expand, router, expert_in, expert_out):
    slots, width = arrived.shape
    capacity = compact.shape[0]
    hidden_width = expert_in.shape[2]
    experts = router.shape[1]
    tile = 1024
    wide = whole((capacity, width))
    tall = pl.BlockSpec((capacity, tile), lambda i: (0, i))
    return pl.pallas_call(
        expert_kernel,
        grid=(hidden_width // tile,),
        in_specs=[
            FLAGS,
            whole((slots, width)),
            whole((slots, width)),
            whole((capacity, slots)),
            whole((slots, capacity)),
            whole((width, experts)),
            pl.BlockSpec((1, width, tile), lambda i: (0, 0, i)),
            pl.BlockSpec((1, tile, width), lambda i: (0, i, 0)),
        ],
        out_specs=[wide, wide, tall, tall, whole((slots, width)), whole((slots, width))]
        + [whole((capacity, experts))],
        out_shape=[
            jax.ShapeDtypeStruct((capacity, width), BF),
            jax.ShapeDtypeStruct((capacity, width), BF),
            jax.ShapeDtypeStruct((capacity, hidden_width), BF),
            jax.ShapeDtypeStruct((capacity, hidden_width), BF),
            jax.ShapeDtypeStruct((slots, width), BF),
            jax.ShapeDtypeStruct((slots, width), BF),
            jax.ShapeDtypeStruct((capacity, experts), BF),
        ],
        scratch_shapes=[
            pltpu.VMEM((capacity, width), F32),
            pltpu.VMEM((capacity, width), F32),
            pltpu.VMEM((capacity, width), F32),
            pltpu.VMEM((capacity, experts), F32),
            pltpu.VMEM((capacity, 1), F32),
        ],
        compiler_params=params(),
        cost_estimate=cost(8 * capacity * width * hidden_width, 8 * width * hidden_width),
    )(flags, arrived, cot, compact, expand, router, expert_in, expert_out)


def owner_backward_kernel(
    flags_ref,
    returned_ref,
    to_tokens_ref,
    cotangent_ref,
    middle_ref,
    gain_ref,
    weight_ref,
    grad_middle_ref,
    grad_branch_ref,
    mine_ref,
    sent_ref,
    grad_gain_ref,
):
    half_rows = mine_ref.shape[0]
    middle = middle_ref[...]
    inverse = lax.rsqrt(jnp.mean(middle * middle, axis=1, keepdims=True) + EPSILON)
    normed = middle * inverse
    grad_second = dot(to_tokens_ref[...], returned_ref[...])
    grouped = (grad_second * normed).reshape(-1, GAIN_ROWS, grad_second.shape[1])
    grad_gain_ref[...] = jnp.sum(grouped, axis=0).astype(BF)
    scaled = grad_second * gain_ref[...]
    grad_middle = cotangent_ref[...].astype(F32) + inverse * (
        scaled - normed * jnp.mean(scaled * normed, axis=1, keepdims=True)
    )
    grad_middle_ref[...] = grad_middle
    grad_branch = grad_middle.astype(BF)
    grad_branch_ref[...] = grad_branch
    weight = weight_ref[:, : middle.shape[1]]
    grad_mixed = dot_nt(grad_branch, weight).astype(BF)
    for core in range(2):

        @pl.when(flags_ref[CORE] == core)
        def _(core=core):
            mine_ref[...] = grad_mixed[core * half_rows : (core + 1) * half_rows]
            sent_ref[...] = grad_mixed[(1 - core) * half_rows : (2 - core) * half_rows]


def owner_backward(flags, returned, to_tokens, cotangent, middle, gain, full_extra):
    rows, width = cotangent.shape
    shapes = [
        wide_shape(rows, width),
        low_shape(rows, width),
        low_shape(rows // 2, width),
        low_shape(rows // 2, width),
        low_shape(GAIN_ROWS, width),
    ]
    operands = [returned, to_tokens, cotangent, middle, gain, full_extra]
    return one_step(owner_backward_kernel, flags, operands, shapes)


GAIN_ROWS = 16


def deal_rows(flags_ref, total, keep_ref, send_ref, rows):
    core = flags_ref[CORE]
    for m in range(total.shape[0] // (2 * rows)):
        place = 2 * (flags_ref[PLACE] ^ m)
        keep_ref[m * rows : (m + 1) * rows, :] = total[
            pl.ds(pl.multiple_of((place + core) * rows, 8), rows), :
        ]
        send_ref[m * rows : (m + 1) * rows, :] = total[
            pl.ds(pl.multiple_of((place + 1 - core) * rows, 8), rows), :
        ].astype(BF)


def dealt(width, columns):
    return [wide_shape(width // 2, columns), low_shape(width // 2, columns)]


def output_grads_kernel(
    rows, flags_ref, mixed_ref, branch_ref, router_ref, gain_ref, keep_ref, send_ref, total
):
    width, experts = router_ref.shape
    extra = total.shape[1] - width
    total[:, :width] = dot_tn(mixed_ref[...], branch_ref[...])
    gain = dot_tn(gain_ref[...], jnp.ones((GAIN_ROWS, extra), BF))
    router = router_ref[...]
    router = jnp.concatenate([router, jnp.zeros((width, extra - experts), F32)], axis=1)
    lanes = lax.broadcasted_iota(jnp.int32, (1, extra), 1)
    total[:, width:] = jnp.where(lanes == experts, gain, router)
    deal_rows(flags_ref, total, keep_ref, send_ref, rows)


def output_grads(flags, mixed, branch, router, gain_rows, rows):
    width, experts = router.shape
    columns = width + experts + 1
    columns += -columns % 128
    return one_step(
        functools.partial(output_grads_kernel, rows),
        flags,
        [mixed, branch, router, gain_rows],
        dealt(width, columns),
        [pltpu.VMEM((width, columns), F32)],
        SMALL_BYTES,
    )


def weight_grads_kernel(
    rows,
    flags_ref,
    normed_ref,
    query_ref,
    near_ref,
    got_ref,
    projected_ref,
    keep_ref,
    send_ref,
    total,
):
    part = query_ref.shape[1]
    projected_ref[:, :part] = query_ref[...]
    for index in range(2):
        both = near_ref[index].astype(F32) + got_ref[index].astype(F32)
        projected_ref[:, (index + 1) * part : (index + 2) * part] = both.astype(BF)
    total[...] = dot_tn(normed_ref[...], projected_ref[...])
    deal_rows(flags_ref, total, keep_ref, send_ref, rows)


def weight_grads(flags, normed, query, near, got, rows):
    work_rows, width = normed.shape
    columns = 3 * query.shape[1]
    return one_step(
        functools.partial(weight_grads_kernel, rows),
        flags,
        [normed, query, near, got],
        [low_shape(work_rows, columns)] + dealt(width, columns),
        [pltpu.VMEM((width, columns), F32)],
        SMALL_BYTES,
    )


def all_to_all(array):
    return lax.all_to_all(array, AXES, split_axis=0, concat_axis=0, tiled=True)


def on_device(
    inputs,
    norm_one,
    w_query,
    w_key,
    w_value,
    w_output,
    norm_two,
    w_router,
    expert_in,
    expert_out,
    routes,
    cotangent,
):
    links = Links()
    level, core = links.level, links.core
    device = links.group * links.levels + level
    devices = links.groups * links.levels
    rows, width = inputs.shape
    half_rows = rows // 2
    half_width = width // 2
    experts = w_router.shape[1]
    own_rows = norm_one.shape[0]
    most = 2 * rows // experts
    capacity = 5 * rows // 4
    blocks = links.levels

    same = (level >> 1) ^ core
    flags = jnp.stack([core, level & 1, same, device, links.group >> 1]).astype(jnp.int32)

    mine = pick(core, inputs[:half_rows], inputs[half_rows:])
    got = links.swap_core(pick(core, inputs[half_rows:], inputs[:half_rows]))
    scale = norm_one.astype(F32)[:, None]
    scaled = [(w.astype(F32) * scale).astype(BF) for w in (w_query, w_key, w_value)]
    low = jnp.concatenate([w[:, :half_width] for w in scaled], axis=1)
    high = jnp.concatenate([w[:, half_width:] for w in scaled], axis=1)
    kept, cross = pick(level & 1, low, high), pick(level & 1, high, low)
    chosen = routes[:, 0]
    picked = (chosen[:, None] == jnp.arange(experts, dtype=jnp.int32)[None, :]).astype(jnp.int32)
    tally = jnp.sum(picked, axis=0).astype(BF)
    extra = jnp.concatenate(
        [w_output, w_router, jnp.broadcast_to(tally[None], (own_rows, experts)), norm_two[:, None]],
        axis=1,
    )
    extra = jnp.pad(extra, ((0, 0), (0, -extra.shape[1] % 128)))
    kept = jnp.concatenate([kept, extra], axis=1)
    cross = jnp.concatenate([cross, extra], axis=1)
    level_block = gather_levels(links, [kept, cross, kept, cross])
    level_rows = level_block.shape[0]
    level_weights = level_block[:, : 3 * half_width]
    got = gate(got, kept, cross)
    near, far = pick(same, mine, got), pick(same, got, mine)
    near_first = links.swap_level(near, 1)
    far_first = links.swap_level(far, 2)
    far_second = links.swap_level(far_first, 1)
    own_weights = gather_groups(links, level_weights)
    picked = gate(picked, level_block)
    rank = jnp.sum((jnp.cumsum(picked, axis=0) - picked) * picked, axis=1)
    place = chosen * most + rank
    slot_index = jnp.arange(experts * most, dtype=jnp.int32)
    to_slots = (slot_index[:, None] == place[None, :]).astype(BF)
    to_tokens = (place[:, None] == slot_index[None, :]).astype(BF)
    cot_slots = dot(to_slots, cotangent).astype(BF).reshape(experts, most, width)

    own_weights = tie(*own_weights, near_first, far_first, cot_slots)[:-3]
    other_weights = [links.swap_core(part) for part in own_weights]

    source = jnp.concatenate([near, near_first, far_first, far_second], axis=0).astype(F32)
    normed_work = (
        source * lax.rsqrt(jnp.mean(source * source, axis=-1, keepdims=True) + EPSILON)
    ).astype(BF)
    if level_rows % 16 == 0:
        queries, pair, weights = project(flags, normed_work, own_weights, other_weights)
    else:
        weights = in_order(links, own_weights, other_weights)
        projected = dot(normed_work, weights).astype(BF)
        queries, pair = projected[:, :half_width], projected[:, half_width:]
    pair_far = links.swap_core(pair)
    cot_arrived = all_to_all(gate(cot_slots, far_second, *other_weights)).reshape(-1, width)
    *mixed_parts, probs = attention_forward(queries, pair, pair_far)
    mixed_parts = tie(*mixed_parts, cot_arrived)[:-1]

    back = tie(*[links.swap_level(mixed_parts[b], b) for b in (1, 2, 3)])
    level_extra = gate(level_block[:, 3 * half_width :], queries)
    own_extra = gather_groups(links, level_extra)
    other_extra = [links.swap_core(gate(part, *back)) for part in own_extra]
    full_extra = in_order(links, own_extra, other_extra)
    full_router = full_extra[:, width : width + experts]
    gain_two = full_extra[:, width + 2 * experts].astype(F32)[None]
    tallies = full_extra[::own_rows, width + experts : width + 2 * experts].astype(F32)
    mine_only = (jnp.arange(experts, dtype=jnp.int32) == device).astype(F32)[None, :]
    counts = jnp.sum(tallies * mine_only, axis=1).astype(jnp.int32)
    offsets = jnp.cumsum(counts) - counts
    within = jnp.arange(most, dtype=jnp.int32)[None, :]
    slot_grid = offsets[:, None] + within
    usable = (within < counts[:, None]) & (slot_grid < capacity)
    slot_flat = jnp.where(usable, slot_grid, -1).reshape(-1)
    held_index = jnp.arange(capacity, dtype=jnp.int32)
    compact = (held_index[:, None] == slot_flat[None, :]).astype(BF)
    expand = (slot_flat[:, None] == held_index[None, :]).astype(BF)

    mixed_mine, mixed_sent = mixed_route(flags, [mixed_parts[0], *back])
    mixed_low, middle, second_slots = owner_forward(
        flags, mixed_mine, links.swap_core(mixed_sent), inputs, full_extra, gain_two, to_slots
    )
    arrived = all_to_all(second_slots.reshape(experts, most, width)).reshape(-1, width)

    held, grad_result, hidden, grad_inner, grad_back, taken_back, grad_logits = expert_layer(
        flags, arrived, cot_arrived, compact, expand, full_router, expert_in, expert_out
    )
    grad_returned = all_to_all(grad_back.reshape(experts, most, width)).reshape(-1, width)
    grad_router = dot_tn(held, grad_logits)
    grad_weight_out = dot_tn(hidden, grad_result)
    grad_weight_in = dot_tn(held, grad_inner)
    grad_returned = gate(grad_returned, grad_weight_in, grad_weight_out, grad_router)

    grad_middle, grad_branch, grad_mine, grad_sent, gain_rows = owner_backward(
        flags, grad_returned, to_tokens, cotangent, middle, gain_two, full_extra
    )
    routed = grad_route(flags, grad_mine, links.swap_core(grad_sent))
    got = tie(*[links.swap_level(routed[b], b) for b in (1, 2, 3)])

    keep, send = output_grads(flags, gate(mixed_low, routed[0]), grad_branch, grad_router, gain_rows, level_rows)
    summed = reduce_cores(links, keep, send)
    summed = reduce_groups(
        links, [summed[m * level_rows : (m + 1) * level_rows] for m in range(links.groups // 2)]
    )
    got = tie(*got, summed)[:-1]
    taken_back = gate(taken_back, *got).reshape(experts, most, width)
    taken_arrived = all_to_all(taken_back).reshape(-1, width)
    grad_queries, grad_near, grad_far = attention_backward(
        queries, pair, pair_far, probs, [routed[0], *got], mixed_parts
    )
    got_pair = links.swap_core(grad_far)
    grad_projected, keep, send = weight_grads(
        flags, normed_work, grad_queries, grad_near, got_pair, level_rows
    )
    grad_first_work = dot_nt(grad_projected, weights).astype(BF)
    core_sum = reduce_cores(links, keep, gate(send, taken_arrived))
    core_sum = gate(core_sum, grad_first_work)
    group_sum = reduce_groups(
        links, [core_sum[m * level_rows : (m + 1) * level_rows] for m in range(links.groups // 2)]
    )
    parts = gate(grad_first_work, core_sum).reshape(blocks, half_rows, width)
    back = tie(*[links.swap_level(parts[b], b) for b in (1, 2, 3)])
    near = (parts[0].astype(F32) + back[0].astype(F32)).astype(BF)
    far = (back[1].astype(F32) + back[2].astype(F32)).astype(BF)
    grad_first = workers_to_owner(links, near, far).astype(F32)
    source_own = inputs.astype(F32)
    inverse_one = lax.rsqrt(jnp.mean(source_own * source_own, axis=-1, keepdims=True) + EPSILON)
    normed_one = source_own * inverse_one
    grad_input = grad_middle + inverse_one * (
        grad_first - normed_one * jnp.mean(grad_first * normed_one, axis=-1, keepdims=True)
    )
    output = (middle + dot(to_tokens, taken_arrived)).astype(BF)

    columns = group_sum.shape[1]
    sums = jnp.concatenate([group_sum, summed], axis=1)
    sums = reduce_levels(links, gate(sums, *back))
    zero, one, two, three = [part[:, :columns] for part in sums]
    summed = sum(part[:, columns:] for part in sums)
    kept, cross = zero + two, one + three
    low, high = pick(level & 1, kept, cross), pick(level & 1, cross, kept)
    grad_weights = [
        jnp.concatenate(
            [part[:, i * half_width : (i + 1) * half_width] for part in (low, high)], axis=1
        )
        for i in range(3)
    ]
    grad_norm_one = sum(
        jnp.sum(w.astype(F32) * g, axis=1)
        for w, g in zip((w_query, w_key, w_value), grad_weights)
    )
    grad_weights = [g * scale for g in grad_weights]

    grad_w_output = summed[:, :width]
    grad_w_router = summed[:, width : width + experts]
    grad_norm_two = summed[:, width + experts]
    return (
        output,
        grad_input,
        grad_norm_one,
        grad_weights[0],
        grad_weights[1],
        grad_weights[2],
        grad_w_output,
        grad_norm_two,
        grad_w_router,
        grad_weight_in[None],
        grad_weight_out[None],
    )


def solution(mesh):
    return jax.shard_map(
        on_device,
        mesh=mesh,
        in_specs=(
            P(AXES, None),
            P(AXES),
            P(AXES, None),
            P(AXES, None),
            P(AXES, None),
            P(AXES, None),
            P(AXES),
            P(AXES, None),
            P(AXES, None, None),
            P(AXES, None, None),
            P(AXES, None),
            P(AXES, None),
        ),
        out_specs=(
            P(AXES, None),
            P(AXES, None),
            P(AXES),
            P(AXES, None),
            P(AXES, None),
            P(AXES, None),
            P(AXES, None),
            P(AXES),
            P(AXES, None),
            P(AXES, None, None),
            P(AXES, None, None),
        ),
        check_vma=False,
    )
```

profile of v0, /device:TPU:0, one launch (start us, length us, event | category | flops | bytes accessed | tf_op | source)
XLA Modules:
  0.0 254.7 jit_solution(6553966571610552907)
XLA Ops:
  4.8 3.1 %collective-permute-start.4 = (bf16[24,2048]{1,0:T(8,128)(2,1)S(1)}, bf16[24,2048]{1,0:T(8,128)(2,1)S(1)}, u32[]{:S(2)}, u32[]{:S(2)}) collective-permute-start(bf16[24,2048]{1,0:T(8,128)(2,1)S(1)} %get-tuple-element.233), channel_id=1, source_target_pairs={{0,1},{1,0},{2,3},{3,2},{4,5},{5,4},{6,7},{7,6},{8,9},{9,8},{10,11... | collective-permute-start | bytes 294920 | tf_op jit(solution)/shard_map/ppermute | solution.py:45
  7.9 2.5 collective-permute-start.6
  12.7 3.4 %collective-permute-done.6 = bf16[24,2048]{1,0:T(8,128)(2,1)S(1)} collective-permute-done((bf16[24,2048]{1,0:T(8,128)(2,1)S(1)}, bf16[24,2048]{1,0:T(8,128)(2,1)S(1)}, u32[]{:S(2)}, u32[]{:S(2)}) %collective-permute-start.6) | collective-permute-done | bytes 98336 | tf_op jit(solution)/shard_map/ppermute | solution.py:45
  16.0 3.3 %collective-permute-done.5 = bf16[24,2048]{1,0:T(8,128)(2,1)S(1)} collective-permute-done((bf16[24,2048]{1,0:T(8,128)(2,1)S(1)}, bf16[24,2048]{1,0:T(8,128)(2,1)S(1)}, u32[]{:S(2)}, u32[]{:S(2)}) %collective-permute-start.5) | collective-permute-done | bytes 98336 | tf_op jit(solution)/shard_map/ppermute | solution.py:45
  20.2 1.6 collective-permute-start.7
  21.7 1.5 collective-permute-start.8
  23.7 2.6 %collective-permute-start.1 = (bf16[128,768]{1,0:T(8,128)(2,1)S(1)}, bf16[128,768]{1,0:T(8,128)(2,1)S(1)}, u32[]{:S(2)}, u32[]{:S(2)}) collective-permute-start(bf16[128,768]{1,0:T(8,128)(2,1)S(1)} %get-tuple-element.203), channel_id=1, source_target_pairs={{0,1},{1,0},{2,3},{3,2},{4,5},{5,4},{6,7},{7,6},{8,9},{9,8},{10,11... | collective-permute-start | bytes 589832 | tf_op jit(solution)/shard_map/ppermute | solution.py:45
  26.4 4.4 %collective-permute-done.2 = bf16[128,768]{1,0:T(8,128)(2,1)S(1)} collective-permute-done((bf16[128,768]{1,0:T(8,128)(2,1)S(1)}, bf16[128,768]{1,0:T(8,128)(2,1)S(1)}, u32[]{:S(2)}, u32[]{:S(2)}) %collective-permute-start.2) | collective-permute-done | bytes 196640 | tf_op jit(solution)/shard_map/ppermute | solution.py:45
  34.8 3.0 %collective-permute-done.3 = bf16[128,768]{1,0:T(8,128)(2,1)S(1)} collective-permute-done((bf16[128,768]{1,0:T(8,128)(2,1)S(1)}, bf16[128,768]{1,0:T(8,128)(2,1)S(1)}, u32[]{:S(2)}, u32[]{:S(2)}) %collective-permute-start.3) | collective-permute-done | bytes 196640 | tf_op jit(solution)/shard_map/ppermute | solution.py:45
  38.3 1.9 shard_map.203
  41.4 4.0 %all-to-all-start = ((bf16[32,16,768]{2,1,0:T(8,128)(2,1)}), bf16[32,16,768]{2,1,0:T(8,128)(2,1)S(1)}, u32[]{:S(2)}, u32[]{:S(2)}) async-start(bf16[32,16,768]{2,1,0:T(8,128)(2,1)} %bitcast.9), calls=%async_computation | async-start | bytes 1572864 | tf_op jit(solution)/shard_map/all_to_all | solution.py:636
  45.4 11.0 %shard_map.204 = (bf16[128,384]{1,0:T(8,128)(2,1)}, bf16[128,384]{1,0:T(8,128)(2,1)}, bf16[128,384]{1,0:T(8,128)(2,1)}, bf16[128,384]{1,0:T(8,128)(2,1)}, bf16[6,512,1024]{2,1,0:T(8,128)(2,1)}) custom-call(bf16[512,384]{1,0:T(8,128)(2,1)} %copy-done.13, bf16[512,768]{1,0:T(8,128)(2,1)} %copy-done.12, bf16[512,768]{1,0:T(8,128)(2,1)} %copy-done.12, ...), custom_call_target="tpu_custom_call" | custom-call | flops 20000000000 | bytes 4096 | tf_op jit(solution)/shard_map/pallas_call | solution.py:174
  56.3 8.6 %all-to-all-done = bf16[32,16,768]{2,1,0:T(8,128)(2,1)S(1)} async-done(((bf16[32,16,768]{2,1,0:T(8,128)(2,1)}), bf16[32,16,768]{2,1,0:T(8,128)(2,1)S(1)}, u32[]{:S(2)}, u32[]{:S(2)}) %all-to-all-start) | async-done | bytes 786464 | tf_op jit(solution)/shard_map/all_to_all | solution.py:636
  65.0 2.9 %collective-permute-start.15 = (bf16[128,384]{1,0:T(8,128)(2,1)}, bf16[128,384]{1,0:T(8,128)(2,1)S(1)}, u32[]{:S(2)}, u32[]{:S(2)}) collective-permute-start(bf16[128,384]{1,0:T(8,128)(2,1)} %get-tuple-element.112.refs_5_), channel_id=1, source_target_pairs={{0,1},{1,0},{2,3},{3,2},{4,5},{5,4},{6,7},{7,6},{8,9},{9,8},{10,11... | collective-permute-start | bytes 294920 | tf_op jit(solution)/shard_map/ppermute | solution.py:45
  68.6 1.6 collective-permute-start.17
  70.9 1.5 collective-permute-start.22
  72.4 1.4 collective-permute-start.24
  73.8 3.7 %collective-permute-done.16.two_ref = bf16[128,384]{1,0:T(8,128)(2,1)S(1)} collective-permute-done((bf16[128,384]{1,0:T(8,128)(2,1)}, bf16[128,384]{1,0:T(8,128)(2,1)S(1)}, u32[]{:S(2)}, u32[]{:S(2)}) %collective-permute-start.16) | collective-permute-done | bytes 98336 | tf_op jit(solution)/shard_map/ppermute | solution.py:45
  78.8 2.4 collective-permute-done.22
  88.1 3.6 %shard_map.206 = (bf16[256,768]{1,0:T(8,128)(2,1)}, f32[256,768]{1,0:T(8,128)}, bf16[512,768]{1,0:T(8,128)(2,1)}) custom-call(s32[5]{0:T(128)} %copy-done.7, bf16[128,768]{1,0:T(8,128)(2,1)} %copy-done.4, bf16[128,768]{1,0:T(8,128)(2,1)} %copy-done.30, bf16[256,768]{1,0:T(8,128)(2,1)} %inputs_ref.1, bf16[768,896]{1,0:T(8,128)(2,1)} %copy-done.17, ...), custom_call_target="tpu_custom_call" | custom-call | bytes 1048576 | tf_op jit(solution)/shard_map/pallas_call | solution.py:262
  91.7 2.9 %all-to-all-start.1 = ((bf16[32,16,768]{2,1,0:T(8,128)(2,1)}), bf16[32,16,768]{2,1,0:T(8,128)(2,1)S(1)}, u32[]{:S(2)}, u32[]{:S(2)}) async-start(bf16[32,16,768]{2,1,0:T(8,128)(2,1)} %bitcast.53), calls=%async_computation.1 | async-start | bytes 1572864 | tf_op jit(solution)/shard_map/all_to_all | solution.py:636
  97.7 16.4 %all-to-all-done.1 = bf16[32,16,768]{2,1,0:T(8,128)(2,1)S(1)} async-done(((bf16[32,16,768]{2,1,0:T(8,128)(2,1)}), bf16[32,16,768]{2,1,0:T(8,128)(2,1)S(1)}, u32[]{:S(2)}, u32[]{:S(2)}) %all-to-all-start.1) | async-done | bytes 786464 | tf_op jit(solution)/shard_map/all_to_all | solution.py:636
  115.0 14.3 %shard_map.207 = (bf16[320,768]{1,0:T(8,128)(2,1)}, bf16[320,768]{1,0:T(8,128)(2,1)}, bf16[320,3072]{1,0:T(8,128)(2,1)}, bf16[320,3072]{1,0:T(8,128)(2,1)}, bf16...) custom-call(s32[5]{0:T(128)} %copy-done.7, bf16[512,768]{1,0:T(8,128)(2,1)} %bitcast.52, ...), custom_call_target="tpu_custom_call" | custom-call | flops 6039797760 | bytes 18874368 | tf_op jit(solution)/shard_map/pallas_call | solution.py:467
  129.3 4.4 %all-to-all-start.2 = ((bf16[32,16,768]{2,1,0:T(8,128)(2,1)}), bf16[32,16,768]{2,1,0:T(8,128)(2,1)S(1)}, u32[]{:S(2)}, u32[]{:S(2)}) async-start(bf16[32,16,768]{2,1,0:T(8,128)(2,1)} %bitcast.54), calls=%async_computation.2 | async-start | bytes 1572864 | tf_op jit(solution)/shard_map/all_to_all | solution.py:636
  134.8 6.9 %fusion.43 = f32[768,3072]{1,0:T(8,128)} fusion(bf16[320,768]{1,0:T(8,128)(2,1)S(1)} %copy-done.23, bf16[320,3072]{1,0:T(8,128)(2,1)} %get-tuple-element.130), kind=kOutput, calls=%fused_computation.159 | convolution fusion | flops 1509949440 | bytes 11894784 | tf_op jit(solution)/shard_map/dot_general | solution.py:24
  141.7 5.2 %fusion.44 = f32[3072,768]{1,0:T(8,128)} fusion(bf16[320,3072]{1,0:T(8,128)(2,1)S(1)} %copy-done.22, bf16[320,768]{1,0:T(8,128)(2,1)S(1)} %copy-done.29), kind=kOutput, calls=%fused_computation.160 | convolution fusion | flops 1509949440 | bytes 11894784 | tf_op jit(solution)/shard_map/dot_general | solution.py:24
  146.8 6.5 %all-to-all-done.2 = bf16[32,16,768]{2,1,0:T(8,128)(2,1)S(1)} async-done(((bf16[32,16,768]{2,1,0:T(8,128)(2,1)}), bf16[32,16,768]{2,1,0:T(8,128)(2,1)S(1)}, u32[]{:S(2)}, u32[]{:S(2)}) %all-to-all-start.2) | async-done | bytes 786464 | tf_op jit(solution)/shard_map/all_to_all | solution.py:636
  154.2 4.5 %shard_map.208 = (f32[256,768]{1,0:T(8,128)}, bf16[256,768]{1,0:T(8,128)(2,1)}, bf16[128,768]{1,0:T(8,128)(2,1)}, bf16[128,768]{1,0:T(8,128)(2,1)}, bf16[16,768]{1,0:T(8,128)(2,1)}) custom-call(s32[5]{0:T(128)} %copy-done.7, bf16[512,768]{1,0:T(8,128)(2,1)} %bitcast.50, bf16[256,512]{1,0:T(8,128)(2,1)} %fusion.10.to_tokens_ref, ...), custom_call_target="tpu_custom_call" | custom-call | bytes 1048576 | tf_op jit(solution)/shard_map/pallas_call | solution.py:262
  158.7 1.5 collective-permute-start.26
  167.0 1.6 collective-permute-start.27
  169.0 1.6 collective-permute-start.31
  171.1 1.5 collective-permute-start.33
  173.7 3.1 %collective-permute-start.29 = (bf16[128,384]{1,0:T(8,128)(2,1)S(1)}, bf16[128,384]{1,0:T(8,128)(2,1)S(1)}, u32[]{:S(2)}, u32[]{:S(2)}) collective-permute-start(bf16[128,384]{1,0:T(8,128)(2,1)S(1)} %get-tuple-element.139), channel_id=1, source_target_pairs={{0,3},{1,2},{2,1},{3,0},{4,7},{5,6},{6,5},{7,4},{8,11},{9,10},{10,... | collective-permute-start | bytes 294920 | tf_op jit(solution)/shard_map/ppermute | solution.py:45
  176.8 6.2 %collective-permute-done.28.refs_2_ = bf16[128,384]{1,0:T(8,128)(2,1)S(1)} collective-permute-done((bf16[128,384]{1,0:T(8,128)(2,1)S(1)}, bf16[128,384]{1,0:T(8,128)(2,1)S(1)}, u32[]{:S(2)}, u32[]{:S(2)}) %collective-permute-start.28) | collective-permute-done | bytes 98336 | tf_op jit(solution)/shard_map/ppermute | solution.py:45
  183.8 3.6 %all-to-all-start.3 = ((bf16[32,16,768]{2,1,0:T(8,128)(2,1)}), bf16[32,16,768]{2,1,0:T(8,128)(2,1)}, u32[]{:S(2)}, u32[]{:S(2)}) async-start(bf16[32,16,768]{2,1,0:T(8,128)(2,1)} %bitcast.18), calls=%async_computation.3 | async-start | bytes 1572864 | tf_op jit(solution)/shard_map/all_to_all | solution.py:636
  187.4 10.2 %shard_map.211 = (bf16[512,384]{1,0:T(8,128)(2,1)}, bf16[2,512,384]{2,1,0:T(8,128)(2,1)}, bf16[2,512,384]{2,1,0:T(8,128)(2,1)}) custom-call(bf16[512,384]{1,0:T(8,128)(2,1)} %copy-done.13, bf16[512,768]{1,0:T(8,128)(2,1)} %copy-done.12, bf16[512,768]{1,0:T(8,128)(2,1)} %copy-done.12, bf16[512,768]{1,0:T(8,128)(2,1)} %collective-permute-done.14.key_far_ref.value_far_ref, ...), custom_call_target="tpu_custom_call" | custom-call | flops 20000000000 | bytes 4096 | tf_op jit(solution)/shard_map/pallas_call | solution.py:218
  197.7 2.5 collective-permute-done.34.got_ref
  202.3 2.0 shard_map.212
  206.8 1.5 collective-permute-start.35
  209.4 3.1 %convolution_convert_fusion.1 = bf16[512,768]{1,0:T(8,128)(2,1)S(1)} fusion(bf16[512,1152]{1,0:T(8,128)(2,1)} %copy-done.11, bf16[768,1152]{1,0:T(8,128)(2,1)} %copy-done.10), kind=kOutput, calls=%fused_computation.11 | convolution fusion | flops 906362880 | bytes 3735552 | tf_op jit(solution)/shard_map/dot_general | solution.py:28
  214.0 1.5 collective-permute-start.36
  217.1 2.1 collective-permute-start.42
  221.1 3.6 %collective-permute-start.38 = (bf16[128,768]{1,0:T(8,128)(2,1)S(1)}, bf16[128,768]{1,0:T(8,128)(2,1)S(1)}, u32[]{:S(2)}, u32[]{:S(2)}) collective-permute-start(bf16[128,768]{1,0:T(8,128)(2,1)S(1)} %get-tuple-element.193), channel_id=1, source_target_pairs={{0,3},{1,2},{2,1},{3,0},{4,7},{5,6},{6,5},{7,4},{8,11},{9,10},{10,... | collective-permute-start | bytes 589832 | tf_op jit(solution)/shard_map/ppermute | solution.py:45
  224.8 2.3 fusion.2
  227.0 7.5 %collective-permute-done.37 = bf16[128,768]{1,0:T(8,128)(2,1)S(1)} collective-permute-done((bf16[128,768]{1,0:T(8,128)(2,1)S(1)}, bf16[128,768]{1,0:T(8,128)(2,1)S(1)}, u32[]{:S(2)}, u32[]{:S(2)}) %collective-permute-start.37) | collective-permute-done | bytes 196640 | tf_op jit(solution)/shard_map/ppermute | solution.py:45
  234.8 4.7 %collective-permute-start.43 = (bf16[24,2048]{1,0:T(8,128)(2,1)S(1)}, bf16[24,2048]{1,0:T(8,128)(2,1)S(1)}, u32[]{:S(2)}, u32[]{:S(2)}) collective-permute-start(bf16[24,2048]{1,0:T(8,128)(2,1)S(1)} %get-tuple-element.192), channel_id=1, source_target_pairs={{0,1},{1,0},{2,3},{3,2},{4,5},{5,4},{6,7},{7,6},{8,9},{9,8},{10,11... | collective-permute-start | bytes 294920 | tf_op jit(solution)/shard_map/ppermute | solution.py:45
  239.5 2.4 collective-permute-start.45
  242.7 6.8 %collective-permute-done.44 = bf16[24,2048]{1,0:T(8,128)(2,1)S(1)} collective-permute-done((bf16[24,2048]{1,0:T(8,128)(2,1)S(1)}, bf16[24,2048]{1,0:T(8,128)(2,1)S(1)}, u32[]{:S(2)}, u32[]{:S(2)}) %collective-permute-start.44) | collective-permute-done | bytes 98336 | tf_op jit(solution)/shard_map/ppermute | solution.py:45
  (236 shorter events, 55.2 us)
Async XLA Ops:
  4.8 7.9 %collective-permute-start.4 = (bf16[24,2048]{1,0:T(8,128)(2,1)S(1)}, bf16[24,2048]{1,0:T(8,128)(2,1)S(1)}, u32[]{:S(2)}, u32[]{:S(2)}) collective-permute-start(bf16[24,2048]{1,0:T(8,128)(2,1)S(1)} %get-tuple-element.233), channel_id=1, source_target_pairs={{0,1},{1,0},{2,3},{3,2},{4,5},{5,4},{6,7},{7,6},{8,9},{9,8},{10,11... | collective-permute-start | bytes 294920 | tf_op jit(solution)/shard_map/ppermute | solution.py:45
  7.9 8.2 %collective-permute-start.6 = (bf16[24,2048]{1,0:T(8,128)(2,1)S(1)}, bf16[24,2048]{1,0:T(8,128)(2,1)S(1)}, u32[]{:S(2)}, u32[]{:S(2)}) collective-permute-start(bf16[24,2048]{1,0:T(8,128)(2,1)S(1)} %get-tuple-element.233), channel_id=1, source_target_pairs={{0,3},{1,2},{2,1},{3,0},{4,7},{5,6},{6,5},{7,4},{8,11},{9,10},{10,... | collective-permute-start | bytes 294920 | tf_op jit(solution)/shard_map/ppermute | solution.py:45
  10.3 8.9 %collective-permute-start.5 = (bf16[24,2048]{1,0:T(8,128)(2,1)S(1)}, bf16[24,2048]{1,0:T(8,128)(2,1)S(1)}, u32[]{:S(2)}, u32[]{:S(2)}) collective-permute-start(bf16[24,2048]{1,0:T(8,128)(2,1)S(1)} %get-tuple-element.234), channel_id=1, source_target_pairs={{0,2},{1,3},{2,0},{3,1},{4,6},{5,7},{6,4},{7,5},{8,10},{9,11},{10,... | collective-permute-start | bytes 294920 | tf_op jit(solution)/shard_map/ppermute | solution.py:45
  11.5 7.9 %collective-permute-start = (bf16[128,768]{1,0:T(8,128)(2,1)S(1)}, bf16[128,768]{1,0:T(8,128)(2,1)S(1)}, u32[]{:S(2)}, u32[]{:S(2)}) collective-permute-start(bf16[128,768]{1,0:T(8,128)(2,1)S(1)} %broadcast_select_fusion.10), channel_id=1, source_target_pairs={{0,4},{1,5},{2,6},{3,7},{4,0},{5,1},{6,2},{7,3},{8,12},{9,13},{10,... | collective-permute-start | bytes 589832 | tf_op jit(solution)/shard_map/ppermute | solution.py:45
  19.5 11.3 %collective-permute-start.2 = (bf16[128,768]{1,0:T(8,128)(2,1)S(1)}, bf16[128,768]{1,0:T(8,128)(2,1)S(1)}, u32[]{:S(2)}, u32[]{:S(2)}) collective-permute-start(bf16[128,768]{1,0:T(8,128)(2,1)S(1)} %get-tuple-element.204), channel_id=1, source_target_pairs={{0,2},{1,3},{2,0},{3,1},{4,6},{5,7},{6,4},{7,5},{8,10},{9,11},{10,... | collective-permute-start | bytes 589832 | tf_op jit(solution)/shard_map/ppermute | solution.py:45
  20.2 11.9 %collective-permute-start.7 = (bf16[96,1152]{1,0:T(8,128)(2,1)S(1)}, bf16[96,1152]{1,0:T(8,128)(2,1)S(1)}, u32[]{:S(2)}, u32[]{:S(2)}) collective-permute-start(bf16[96,1152]{1,0:T(8,128)(2,1)S(1)} %fusion.16.refs_0_), channel_id=1, source_target_pairs={{0,8},{1,9},{2,10},{3,11},{4,12},{5,13},{6,14},{7,15},{8,0},{9,1},... | collective-permute-start | bytes 663560 | tf_op jit(solution)/shard_map/ppermute | solution.py:45
  21.7 10.8 %collective-permute-start.8 = (bf16[96,1152]{1,0:T(8,128)(2,1)S(1)}, bf16[96,1152]{1,0:T(8,128)(2,1)S(1)}, u32[]{:S(2)}, u32[]{:S(2)}) collective-permute-start(bf16[96,1152]{1,0:T(8,128)(2,1)S(1)} %fusion.16.refs_0_), channel_id=1, source_target_pairs={{0,16},{1,17},{2,18},{3,19},{4,20},{5,21},{6,22},{7,23},{8,24},{9,... | collective-permute-start | bytes 663560 | tf_op jit(solution)/shard_map/ppermute | solution.py:45
  23.3 9.3 %collective-permute-start.9 = (bf16[96,1152]{1,0:T(8,128)(2,1)S(1)}, bf16[96,1152]{1,0:T(8,128)(2,1)S(1)}, u32[]{:S(2)}, u32[]{:S(2)}) collective-permute-start(bf16[96,1152]{1,0:T(8,128)(2,1)S(1)} %fusion.16.refs_0_), channel_id=1, source_target_pairs={{0,24},{1,25},{2,26},{3,27},{4,28},{5,29},{6,30},{7,31},{8,16},{9,... | collective-permute-start | bytes 663560 | tf_op jit(solution)/shard_map/ppermute | solution.py:45
  23.7 10.1 %collective-permute-start.1 = (bf16[128,768]{1,0:T(8,128)(2,1)S(1)}, bf16[128,768]{1,0:T(8,128)(2,1)S(1)}, u32[]{:S(2)}, u32[]{:S(2)}) collective-permute-start(bf16[128,768]{1,0:T(8,128)(2,1)S(1)} %get-tuple-element.203), channel_id=1, source_target_pairs={{0,1},{1,0},{2,3},{3,2},{4,5},{5,4},{6,7},{7,6},{8,9},{9,8},{10,11... | collective-permute-start | bytes 589832 | tf_op jit(solution)/shard_map/ppermute | solution.py:45
  30.8 7.0 %collective-permute-start.3 = (bf16[128,768]{1,0:T(8,128)(2,1)S(1)}, bf16[128,768]{1,0:T(8,128)(2,1)S(1)}, u32[]{:S(2)}, u32[]{:S(2)}) collective-permute-start(bf16[128,768]{1,0:T(8,128)(2,1)S(1)} %collective-permute-done.2), channel_id=1, source_target_pairs={{0,1},{1,0},{2,3},{3,2},{4,5},{5,4},{6,7},{7,6},{8,9},{9,8},{10,11... | collective-permute-start | bytes 589832 | tf_op jit(solution)/shard_map/ppermute | solution.py:45
  33.8 4.5 %collective-permute-start.10 = (bf16[96,1152]{1,0:T(8,128)(2,1)S(1)}, bf16[96,1152]{1,0:T(8,128)(2,1)S(1)}, u32[]{:S(2)}, u32[]{:S(2)}) collective-permute-start(bf16[96,1152]{1,0:T(8,128)(2,1)S(1)} %fusion.16.refs_0_), channel_id=1, source_target_pairs={{0,4},{1,5},{2,6},{3,7},{4,0},{5,1},{6,2},{7,3},{8,12},{9,13},{10,... | collective-permute-start | bytes 663560 | tf_op jit(solution)/shard_map/ppermute | solution.py:45
  33.8 4.5 %collective-permute-start.11 = (bf16[96,1152]{1,0:T(8,128)(2,1)S(1)}, bf16[96,1152]{1,0:T(8,128)(2,1)S(1)}, u32[]{:S(2)}, u32[]{:S(2)}) collective-permute-start(bf16[96,1152]{1,0:T(8,128)(2,1)S(1)} %collective-permute-done.7.refs_1_), channel_id=1, source_target_pairs={{0,4},{1,5},{2,6},{3,7},{4,0},{5,1},{6,2},{7,3},{8,12},{9,13},{10,... | collective-permute-start | bytes 663560 | tf_op jit(solution)/shard_map/ppermute | solution.py:45
  34.3 4.0 %collective-permute-start.12 = (bf16[96,1152]{1,0:T(8,128)(2,1)S(1)}, bf16[96,1152]{1,0:T(8,128)(2,1)S(1)}, u32[]{:S(2)}, u32[]{:S(2)}) collective-permute-start(bf16[96,1152]{1,0:T(8,128)(2,1)S(1)} %collective-permute-done.8.refs_2_), channel_id=1, source_target_pairs={{0,4},{1,5},{2,6},{3,7},{4,0},{5,1},{6,2},{7,3},{8,12},{9,13},{10,... | collective-permute-start | bytes 663560 | tf_op jit(solution)/shard_map/ppermute | solution.py:45
  34.3 4.0 %collective-permute-start.13 = (bf16[96,1152]{1,0:T(8,128)(2,1)S(1)}, bf16[96,1152]{1,0:T(8,128)(2,1)S(1)}, u32[]{:S(2)}, u32[]{:S(2)}) collective-permute-start(bf16[96,1152]{1,0:T(8,128)(2,1)S(1)} %collective-permute-done.9.refs_3_), channel_id=1, source_target_pairs={{0,4},{1,5},{2,6},{3,7},{4,0},{5,1},{6,2},{7,3},{8,12},{9,13},{10,... | collective-permute-start | bytes 663560 | tf_op jit(solution)/shard_map/ppermute | solution.py:45
  41.4 4.0 %collective-permute-start.14 = (bf16[512,768]{1,0:T(8,128)(2,1)S(1)}, bf16[512,768]{1,0:T(8,128)(2,1)}, u32[]{:S(2)}, u32[]{:S(2)}) collective-permute-start(bf16[512,768]{1,0:T(8,128)(2,1)S(1)} %get-tuple-element.105.key_ref.value_ref), channel_id=1, source_target_pairs={{0,4},{1,5},{2,6},{3,7},{4,0},{5,1},{6,2},{7,3},{8,12},{9,13},{10,... | collective-permute-start | bytes 2359304 | tf_op jit(solution)/shard_map/ppermute | solution.py:45
  41.4 23.6 %all-to-all-start = ((bf16[32,16,768]{2,1,0:T(8,128)(2,1)}), bf16[32,16,768]{2,1,0:T(8,128)(2,1)S(1)}, u32[]{:S(2)}, u32[]{:S(2)}) async-start(bf16[32,16,768]{2,1,0:T(8,128)(2,1)} %bitcast.9), calls=%async_computation | async-start | bytes 1572864 | tf_op jit(solution)/shard_map/all_to_all | solution.py:636
  65.0 7.4 %collective-permute-start.15 = (bf16[128,384]{1,0:T(8,128)(2,1)}, bf16[128,384]{1,0:T(8,128)(2,1)S(1)}, u32[]{:S(2)}, u32[]{:S(2)}) collective-permute-start(bf16[128,384]{1,0:T(8,128)(2,1)} %get-tuple-element.112.refs_5_), channel_id=1, source_target_pairs={{0,1},{1,0},{2,3},{3,2},{4,5},{5,4},{6,7},{7,6},{8,9},{9,8},{10,11... | collective-permute-start | bytes 294920 | tf_op jit(solution)/shard_map/ppermute | solution.py:45
  67.9 9.7 %collective-permute-start.16 = (bf16[128,384]{1,0:T(8,128)(2,1)}, bf16[128,384]{1,0:T(8,128)(2,1)S(1)}, u32[]{:S(2)}, u32[]{:S(2)}) collective-permute-start(bf16[128,384]{1,0:T(8,128)(2,1)} %get-tuple-element.113.refs_6_), channel_id=1, source_target_pairs={{0,2},{1,3},{2,0},{3,1},{4,6},{5,7},{6,4},{7,5},{8,10},{9,11},{10,... | collective-permute-start | bytes 294920 | tf_op jit(solution)/shard_map/ppermute | solution.py:45
  68.6 8.9 %collective-permute-start.17 = (bf16[128,384]{1,0:T(8,128)(2,1)}, bf16[128,384]{1,0:T(8,128)(2,1)S(1)}, u32[]{:S(2)}, u32[]{:S(2)}) collective-permute-start(bf16[128,384]{1,0:T(8,128)(2,1)} %get-tuple-element.114.refs_7_), channel_id=1, source_target_pairs={{0,3},{1,2},{2,1},{3,0},{4,7},{5,6},{6,5},{7,4},{8,11},{9,10},{10,... | collective-permute-start | bytes 294920 | tf_op jit(solution)/shard_map/ppermute | solution.py:45
  70.3 8.1 %collective-permute-start.20 = (bf16[96,896]{1,0:T(8,128)(2,1)S(1)}, bf16[96,896]{1,0:T(8,128)(2,1)S(1)}, u32[]{:S(2)}, u32[]{:S(2)}) collective-permute-start(bf16[96,896]{1,0:T(8,128)(2,1)S(1)} %fusion.20), channel_id=1, source_target_pairs={{0,8},{1,9},{2,10},{3,11},{4,12},{5,13},{6,14},{7,15},{8,0},{9,1},... | collective-permute-start | bytes 516104 | tf_op jit(solution)/shard_map/ppermute | solution.py:45
  70.9 10.3 %collective-permute-start.22 = (bf16[96,896]{1,0:T(8,128)(2,1)S(1)}, bf16[96,896]{1,0:T(8,128)(2,1)S(1)}, u32[]{:S(2)}, u32[]{:S(2)}) collective-permute-start(bf16[96,896]{1,0:T(8,128)(2,1)S(1)} %fusion.20), channel_id=1, source_target_pairs={{0,16},{1,17},{2,18},{3,19},{4,20},{5,21},{6,22},{7,23},{8,24},{9,... | collective-permute-start | bytes 516104 | tf_op jit(solution)/shard_map/ppermute | solution.py:45
  72.4 8.8 %collective-permute-start.24 = (bf16[96,896]{1,0:T(8,128)(2,1)S(1)}, bf16[96,896]{1,0:T(8,128)(2,1)S(1)}, u32[]{:S(2)}, u32[]{:S(2)}) collective-permute-start(bf16[96,896]{1,0:T(8,128)(2,1)S(1)} %fusion.20), channel_id=1, source_target_pairs={{0,24},{1,25},{2,26},{3,27},{4,28},{5,29},{6,30},{7,31},{8,16},{9,... | collective-permute-start | bytes 516104 | tf_op jit(solution)/shard_map/ppermute | solution.py:45
  77.5 5.8 %collective-permute-start.19 = (bf16[96,896]{1,0:T(8,128)(2,1)S(1)}, bf16[96,896]{1,0:T(8,128)(2,1)S(1)}, u32[]{:S(2)}, u32[]{:S(2)}) collective-permute-start(bf16[96,896]{1,0:T(8,128)(2,1)S(1)} %fusion.20), channel_id=1, source_target_pairs={{0,4},{1,5},{2,6},{3,7},{4,0},{5,1},{6,2},{7,3},{8,12},{9,13},{10,... | collective-permute-start | bytes 516104 | tf_op jit(solution)/shard_map/ppermute | solution.py:45
  78.3 5.1 %collective-permute-start.21 = (bf16[96,896]{1,0:T(8,128)(2,1)S(1)}, bf16[96,896]{1,0:T(8,128)(2,1)S(1)}, u32[]{:S(2)}, u32[]{:S(2)}) collective-permute-start(bf16[96,896]{1,0:T(8,128)(2,1)S(1)} %collective-permute-done.20), channel_id=1, source_target_pairs={{0,4},{1,5},{2,6},{3,7},{4,0},{5,1},{6,2},{7,3},{8,12},{9,13},{10,... | collective-permute-start | bytes 516104 | tf_op jit(solution)/shard_map/ppermute | solution.py:45
  81.2 2.7 %collective-permute-start.25 = (bf16[96,896]{1,0:T(8,128)(2,1)S(1)}, bf16[96,896]{1,0:T(8,128)(2,1)S(1)}, u32[]{:S(2)}, u32[]{:S(2)}) collective-permute-start(bf16[96,896]{1,0:T(8,128)(2,1)S(1)} %collective-permute-done.24), channel_id=1, source_target_pairs={{0,4},{1,5},{2,6},{3,7},{4,0},{5,1},{6,2},{7,3},{8,12},{9,13},{10,... | collective-permute-start | bytes 516104 | tf_op jit(solution)/shard_map/ppermute | solution.py:45
  83.2 4.1 %collective-permute-start.18 = (bf16[128,768]{1,0:T(8,128)(2,1)S(1)}, bf16[128,768]{1,0:T(8,128)(2,1)S(1)}, u32[]{:S(2)}, u32[]{:S(2)}) collective-permute-start(bf16[128,768]{1,0:T(8,128)(2,1)S(1)} %get-tuple-element.119), channel_id=1, source_target_pairs={{0,4},{1,5},{2,6},{3,7},{4,0},{5,1},{6,2},{7,3},{8,12},{9,13},{10,... | collective-permute-start | bytes 589832 | tf_op jit(solution)/shard_map/ppermute | solution.py:45
  91.7 22.4 %all-to-all-start.1 = ((bf16[32,16,768]{2,1,0:T(8,128)(2,1)}), bf16[32,16,768]{2,1,0:T(8,128)(2,1)S(1)}, u32[]{:S(2)}, u32[]{:S(2)}) async-start(bf16[32,16,768]{2,1,0:T(8,128)(2,1)} %bitcast.53), calls=%async_computation.1 | async-start | bytes 1572864 | tf_op jit(solution)/shard_map/all_to_all | solution.py:636
  129.3 24.0 %all-to-all-start.2 = ((bf16[32,16,768]{2,1,0:T(8,128)(2,1)}), bf16[32,16,768]{2,1,0:T(8,128)(2,1)S(1)}, u32[]{:S(2)}, u32[]{:S(2)}) async-start(bf16[32,16,768]{2,1,0:T(8,128)(2,1)} %bitcast.54), calls=%async_computation.2 | async-start | bytes 1572864 | tf_op jit(solution)/shard_map/all_to_all | solution.py:636
  158.7 2.7 %collective-permute-start.26 = (bf16[128,768]{1,0:T(8,128)(2,1)}, bf16[128,768]{1,0:T(8,128)(2,1)S(1)}, u32[]{:S(2)}, u32[]{:S(2)}) collective-permute-start(bf16[128,768]{1,0:T(8,128)(2,1)} %get-tuple-element.136), channel_id=1, source_target_pairs={{0,4},{1,5},{2,6},{3,7},{4,0},{5,1},{6,2},{7,3},{8,12},{9,13},{10,... | collective-permute-start | bytes 589832 | tf_op jit(solution)/shard_map/ppermute | solution.py:45
  167.0 6.6 %collective-permute-start.27 = (bf16[128,384]{1,0:T(8,128)(2,1)S(1)}, bf16[128,384]{1,0:T(8,128)(2,1)S(1)}, u32[]{:S(2)}, u32[]{:S(2)}) collective-permute-start(bf16[128,384]{1,0:T(8,128)(2,1)S(1)} %get-tuple-element.137), channel_id=1, source_target_pairs={{0,1},{1,0},{2,3},{3,2},{4,5},{5,4},{6,7},{7,6},{8,9},{9,8},{10,11... | collective-permute-start | bytes 294920 | tf_op jit(solution)/shard_map/ppermute | solution.py:45
  169.0 14.0 %collective-permute-start.31 = (bf16[96,896]{1,0:T(8,128)(2,1)S(1)}, bf16[96,896]{1,0:T(8,128)(2,1)S(1)}, u32[]{:S(2)}, u32[]{:S(2)}) collective-permute-start(bf16[96,896]{1,0:T(8,128)(2,1)S(1)} %get-tuple-element.198), channel_id=1, source_target_pairs={{0,8},{1,9},{2,10},{3,11},{4,12},{5,13},{6,14},{7,15},{8,0},{9,1},... | collective-permute-start | bytes 516104 | tf_op jit(solution)/shard_map/ppermute | solution.py:45
  170.6 12.4 %collective-permute-start.32 = (bf16[96,896]{1,0:T(8,128)(2,1)S(1)}, bf16[96,896]{1,0:T(8,128)(2,1)S(1)}, u32[]{:S(2)}, u32[]{:S(2)}) collective-permute-start(bf16[96,896]{1,0:T(8,128)(2,1)S(1)} %get-tuple-element.197), channel_id=1, source_target_pairs={{0,16},{1,17},{2,18},{3,19},{4,20},{5,21},{6,22},{7,23},{8,24},{9,... | collective-permute-start | bytes 516104 | tf_op jit(solution)/shard_map/ppermute | solution.py:45
  171.1 11.9 %collective-permute-start.33 = (bf16[96,896]{1,0:T(8,128)(2,1)S(1)}, bf16[96,896]{1,0:T(8,128)(2,1)S(1)}, u32[]{:S(2)}, u32[]{:S(2)}) collective-permute-start(bf16[96,896]{1,0:T(8,128)(2,1)S(1)} %get-tuple-element.196), channel_id=1, source_target_pairs={{0,24},{1,25},{2,26},{3,27},{4,28},{5,29},{6,30},{7,31},{8,16},{9,... | collective-permute-start | bytes 516104 | tf_op jit(solution)/shard_map/ppermute | solution.py:45
  172.6 10.4 %collective-permute-start.28 = (bf16[128,384]{1,0:T(8,128)(2,1)S(1)}, bf16[128,384]{1,0:T(8,128)(2,1)S(1)}, u32[]{:S(2)}, u32[]{:S(2)}) collective-permute-start(bf16[128,384]{1,0:T(8,128)(2,1)S(1)} %get-tuple-element.138), channel_id=1, source_target_pairs={{0,2},{1,3},{2,0},{3,1},{4,6},{5,7},{6,4},{7,5},{8,10},{9,11},{10,... | collective-permute-start | bytes 294920 | tf_op jit(solution)/shard_map/ppermute | solution.py:45
  173.7 9.3 %collective-permute-start.29 = (bf16[128,384]{1,0:T(8,128)(2,1)S(1)}, bf16[128,384]{1,0:T(8,128)(2,1)S(1)}, u32[]{:S(2)}, u32[]{:S(2)}) collective-permute-start(bf16[128,384]{1,0:T(8,128)(2,1)S(1)} %get-tuple-element.139), channel_id=1, source_target_pairs={{0,3},{1,2},{2,1},{3,0},{4,7},{5,6},{6,5},{7,4},{8,11},{9,10},{10,... | collective-permute-start | bytes 294920 | tf_op jit(solution)/shard_map/ppermute | solution.py:45
  183.8 22.9 %all-to-all-start.3 = ((bf16[32,16,768]{2,1,0:T(8,128)(2,1)}), bf16[32,16,768]{2,1,0:T(8,128)(2,1)}, u32[]{:S(2)}, u32[]{:S(2)}) async-start(bf16[32,16,768]{2,1,0:T(8,128)(2,1)} %bitcast.18), calls=%async_computation.3 | async-start | bytes 1572864 | tf_op jit(solution)/shard_map/all_to_all | solution.py:636
  197.7 2.6 %collective-permute-start.34 = (bf16[2,512,384]{2,1,0:T(8,128)(2,1)}, bf16[2,512,384]{2,1,0:T(8,128)(2,1)S(1)}, u32[]{:S(2)}, u32[]{:S(2)}) collective-permute-start(bf16[2,512,384]{2,1,0:T(8,128)(2,1)} %get-tuple-element.161), channel_id=1, source_target_pairs={{0,4},{1,5},{2,6},{3,7},{4,0},{5,1},{6,2},{7,3},{8,12},{9,13},{10,... | collective-permute-start | bytes 2359304 | tf_op jit(solution)/shard_map/ppermute | solution.py:45
  206.8 5.7 %collective-permute-start.35 = (bf16[384,1152]{1,0:T(8,128)(2,1)S(1)}, bf16[384,1152]{1,0:T(8,128)(2,1)}, u32[]{:S(2)}, u32[]{:S(2)}) collective-permute-start(bf16[384,1152]{1,0:T(8,128)(2,1)S(1)} %get-tuple-element.166), channel_id=1, source_target_pairs={{0,4},{1,5},{2,6},{3,7},{4,0},{5,1},{6,2},{7,3},{8,12},{9,13},{10,... | collective-permute-start | bytes 2654216 | tf_op jit(solution)/shard_map/ppermute | solution.py:45
  214.0 7.1 %collective-permute-start.36 = (bf16[128,768]{1,0:T(8,128)(2,1)S(1)}, bf16[128,768]{1,0:T(8,128)(2,1)S(1)}, u32[]{:S(2)}, u32[]{:S(2)}) collective-permute-start(bf16[128,768]{1,0:T(8,128)(2,1)S(1)} %get-tuple-element.195), channel_id=1, source_target_pairs={{0,1},{1,0},{2,3},{3,2},{4,5},{5,4},{6,7},{7,6},{8,9},{9,8},{10,11... | collective-permute-start | bytes 589832 | tf_op jit(solution)/shard_map/ppermute | solution.py:45
  215.6 18.9 %collective-permute-start.40 = (bf16[96,1152]{1,0:T(8,128)(2,1)S(1)}, bf16[96,1152]{1,0:T(8,128)(2,1)S(1)}, u32[]{:S(2)}, u32[]{:S(2)}) collective-permute-start(bf16[96,1152]{1,0:T(8,128)(2,1)S(1)} %get-tuple-element.189), channel_id=1, source_target_pairs={{0,8},{1,9},{2,10},{3,11},{4,12},{5,13},{6,14},{7,15},{8,0},{9,1},... | collective-permute-start | bytes 663560 | tf_op jit(solution)/shard_map/ppermute | solution.py:45
  215.7 18.8 %collective-permute-start.41 = (bf16[96,1152]{1,0:T(8,128)(2,1)S(1)}, bf16[96,1152]{1,0:T(8,128)(2,1)S(1)}, u32[]{:S(2)}, u32[]{:S(2)}) collective-permute-start(bf16[96,1152]{1,0:T(8,128)(2,1)S(1)} %get-tuple-element.188), channel_id=1, source_target_pairs={{0,16},{1,17},{2,18},{3,19},{4,20},{5,21},{6,22},{7,23},{8,24},{9,... | collective-permute-start | bytes 663560 | tf_op jit(solution)/shard_map/ppermute | solution.py:45
  217.1 17.4 %collective-permute-start.42 = (bf16[96,1152]{1,0:T(8,128)(2,1)S(1)}, bf16[96,1152]{1,0:T(8,128)(2,1)S(1)}, u32[]{:S(2)}, u32[]{:S(2)}) collective-permute-start(bf16[96,1152]{1,0:T(8,128)(2,1)S(1)} %get-tuple-element.187), channel_id=1, source_target_pairs={{0,24},{1,25},{2,26},{3,27},{4,28},{5,29},{6,30},{7,31},{8,16},{9,... | collective-permute-start | bytes 663560 | tf_op jit(solution)/shard_map/ppermute | solution.py:45
  219.1 15.4 %collective-permute-start.37 = (bf16[128,768]{1,0:T(8,128)(2,1)S(1)}, bf16[128,768]{1,0:T(8,128)(2,1)S(1)}, u32[]{:S(2)}, u32[]{:S(2)}) collective-permute-start(bf16[128,768]{1,0:T(8,128)(2,1)S(1)} %get-tuple-element.194), channel_id=1, source_target_pairs={{0,2},{1,3},{2,0},{3,1},{4,6},{5,7},{6,4},{7,5},{8,10},{9,11},{10,... | collective-permute-start | bytes 589832 | tf_op jit(solution)/shard_map/ppermute | solution.py:45
  221.1 13.4 %collective-permute-start.38 = (bf16[128,768]{1,0:T(8,128)(2,1)S(1)}, bf16[128,768]{1,0:T(8,128)(2,1)S(1)}, u32[]{:S(2)}, u32[]{:S(2)}) collective-permute-start(bf16[128,768]{1,0:T(8,128)(2,1)S(1)} %get-tuple-element.193), channel_id=1, source_target_pairs={{0,3},{1,2},{2,1},{3,0},{4,7},{5,6},{6,5},{7,4},{8,11},{9,10},{10,... | collective-permute-start | bytes 589832 | tf_op jit(solution)/shard_map/ppermute | solution.py:45
  234.8 7.9 %collective-permute-start.43 = (bf16[24,2048]{1,0:T(8,128)(2,1)S(1)}, bf16[24,2048]{1,0:T(8,128)(2,1)S(1)}, u32[]{:S(2)}, u32[]{:S(2)}) collective-permute-start(bf16[24,2048]{1,0:T(8,128)(2,1)S(1)} %get-tuple-element.192), channel_id=1, source_target_pairs={{0,1},{1,0},{2,3},{3,2},{4,5},{5,4},{6,7},{7,6},{8,9},{9,8},{10,11... | collective-permute-start | bytes 294920 | tf_op jit(solution)/shard_map/ppermute | solution.py:45
  239.5 10.0 %collective-permute-start.44 = (bf16[24,2048]{1,0:T(8,128)(2,1)S(1)}, bf16[24,2048]{1,0:T(8,128)(2,1)S(1)}, u32[]{:S(2)}, u32[]{:S(2)}) collective-permute-start(bf16[24,2048]{1,0:T(8,128)(2,1)S(1)} %get-tuple-element.191), channel_id=1, source_target_pairs={{0,2},{1,3},{2,0},{3,1},{4,6},{5,7},{6,4},{7,5},{8,10},{9,11},{10,... | collective-permute-start | bytes 294920 | tf_op jit(solution)/shard_map/ppermute | solution.py:45
  239.5 10.0 %collective-permute-start.45 = (bf16[24,2048]{1,0:T(8,128)(2,1)S(1)}, bf16[24,2048]{1,0:T(8,128)(2,1)S(1)}, u32[]{:S(2)}, u32[]{:S(2)}) collective-permute-start(bf16[24,2048]{1,0:T(8,128)(2,1)S(1)} %get-tuple-element.190), channel_id=1, source_target_pairs={{0,3},{1,2},{2,1},{3,0},{4,7},{5,6},{6,5},{7,4},{8,11},{9,10},{10,... | collective-permute-start | bytes 294920 | tf_op jit(solution)/shard_map/ppermute | solution.py:45
  242.1 11.0 %collective-permute-start.39 = (bf16[128,768]{1,0:T(8,128)(2,1)S(1)}, bf16[128,768]{1,0:T(8,128)(2,1)S(1)}, u32[]{:S(2)}, u32[]{:S(2)}) collective-permute-start(bf16[128,768]{1,0:T(8,128)(2,1)S(1)} %broadcast_select_fusion.12), channel_id=1, source_target_pairs={{0,4},{1,5},{2,6},{3,7},{4,0},{5,1},{6,2},{7,3},{8,12},{9,13},{10,... | collective-permute-start | bytes 589832 | tf_op jit(solution)/shard_map/ppermute | solution.py:45
  (41 other events, 289.7 us)
where the time goes:
time: 256 us; the launch traced here: 255 us
  waiting for transfers between devices  80.9 us (32%)
  starting transfers between devices  67.8 us (26%)
  Pallas kernels  49.9 us (19%)
  other arithmetic  19.1 us (7%)
  matrix products  18.9 us (7%)
  local copies, waits for them, and re-layouts  16.6 us (6%)
    ppermute x46, starting transfers between devices, permute(): return lax.ppermute(array, AXES, pairs)  52.9 us
    ppermute x46, waiting for transfers between devices, permute(): return lax.ppermute(array, AXES, pairs)  48 us
    all_to_all x4, waiting for transfers between devices, all_to_all(): return lax.all_to_all(array, AXES, split_axis=0, concat_axis=0, tiled=True)  32.8 us
    all_to_all x4, starting transfers between devices, all_to_all(): return lax.all_to_all(array, AXES, split_axis=0, concat_axis=0, tiled=True)  14.8 us
    pallas_call x7, Pallas kernels, one_step(): pl.pallas_call(kernel, grid=(1,), in_specs=[FLAGS] + [whole(operand.shape...  14.4 us
    pallas_call x1, Pallas kernels, expert_layer(): pl.pallas_call(expert_kernel, grid=(hidden_width // tile,), in_specs=[FLA...  14.3 us
    dot_general x3, matrix products, dot_tn(): lax.dot_general(left, right, (((0,), (0,)), ((), ())), preferred_element_...  12.3 us
    unnamed x78, local copies, waits for them, and re-layouts  12.2 us
  transfers between devices with their start and end apart: 50, of which 20 were waited for; matrix products, arithmetic and copies ran while one was open for 13% of the time, Pallas kernels for 9%

commit v1 on v0

--- a/solution.py
+++ b/solution.py
@@ -114,7 +114,7 @@
     rows = block.shape[0] // links.levels
     parts = [rows_of(block, links.level ^ b, rows) for b in range(links.levels)]
     got = tie(*[links.swap_level(parts[b].astype(BF), b) for b in range(1, links.levels)])
-    return [parts[0]] + [part.astype(F32) for part in got]
+    return [parts[0], *got]
 
 
 def owner_to_workers(links, array):
@@ -140,31 +140,35 @@
     return [(lanes // HEAD_DIM == head).astype(dtype) for head in range(2)]
 
 
-def forward_kernel(
-    query_ref, key_ref, value_ref, key_far_ref, value_far_ref, zero_ref, one_ref, two_ref, three_ref, probs_ref
-):
-    rows = query_ref.shape[0]
+CHUNK = 128
+
+
+def forward_kernel(query_ref, key_ref, value_ref, key_far_ref, value_far_ref, *refs):
+    mixed_refs, weights_ref, inverse_ref = refs[:-2], refs[-2], refs[-1]
     query = query_ref[...] * BF(HEAD_DIM**-0.5)
     key = jnp.concatenate([key_ref[...], key_far_ref[...]], axis=0)
     value = jnp.concatenate([value_ref[...], value_far_ref[...]], axis=0)
-    mixed = jnp.zeros((rows, PAIR), F32)
-    for head, mask in enumerate(head_masks(BF)):
-        scores = dot_nt(query * mask, key)
-        weights = jnp.exp(scores - jnp.max(scores, axis=1, keepdims=True))
-        probs = (weights * (1.0 / jnp.sum(weights, axis=1, keepdims=True))).astype(BF)
-        probs_ref[head] = probs
-        mixed = mixed + dot(probs, value * mask)
-    mixed = mixed.astype(BF)
-    part_rows = rows // 4
-    for part, ref in enumerate((zero_ref, one_ref, two_ref, three_ref)):
-        ref[...] = mixed[part * part_rows : (part + 1) * part_rows]
+    value = jnp.concatenate([value, jnp.ones_like(value)], axis=1)
+    first_head = lax.broadcasted_iota(jnp.int32, (1, PAIR), 1) < HEAD_DIM
+    for part, mixed_ref in enumerate(mixed_refs):
+        rows = slice(part * CHUNK, (part + 1) * CHUNK)
+        sums = []
+        for head, mask in enumerate(head_masks(BF)):
+            scores = dot_nt(query[rows] * mask, key)
+            weights = jnp.exp(scores - jnp.max(scores, axis=1, keepdims=True)).astype(BF)
+            weights_ref[head, rows] = weights
+            sums.append(dot(weights, value))
+        mixed = jnp.where(first_head, sums[0][:, :PAIR], sums[1][:, :PAIR])
+        inverse = 1.0 / jnp.where(first_head, sums[0][:, PAIR:], sums[1][:, PAIR:])
+        inverse_ref[rows] = inverse
+        mixed_ref[...] = (mixed * inverse).astype(BF)
 
 
 def pair_column(rows, block=0):
     return pl.BlockSpec((rows, PAIR), lambda i: (0, block + i))
 
 
-def probs_block(rows):
+def weights_block(rows):
     return pl.BlockSpec((2, rows, 2 * rows), lambda i: (i, 0, 0))
 
 
@@ -175,44 +179,51 @@
         forward_kernel,
         grid=(pairs,),
         in_specs=[pair_column(rows)] + [pair_column(rows), pair_column(rows, pairs)] * 2,
-        out_specs=[pair_column(rows // 4)] * 4 + [probs_block(rows)],
-        out_shape=[jax.ShapeDtypeStruct((rows // 4, half_width), BF)] * 4
-        + [jax.ShapeDtypeStruct((2 * pairs, rows, 2 * rows), BF)],
+        out_specs=[pair_column(CHUNK)] * (rows // CHUNK) + [weights_block(rows), pair_column(rows)],
+        out_shape=[low_shape(CHUNK, half_width)] * (rows // CHUNK)
+        + [low_shape(2 * pairs, rows, 2 * rows), wide_shape(rows, half_width)],
         compiler_params=params(),
-        cost_estimate=cost(2 * 10**10, 4096),
+        cost_estimate=cost(2 * 10**9, 4096),
     )(queries, pair, pair, pair_far, pair_far)
 
 
-def backward_kernel(query_ref, key_ref, value_ref, key_far_ref, value_far_ref, probs_ref, *refs):
+def backward_kernel(
+    query_ref, key_ref, value_ref, key_far_ref, value_far_ref, weights_ref, inverse_ref, *refs
+):
     grad_refs, mixed_refs = refs[:4], refs[4:8]
     grad_query_ref, grad_near_ref, grad_far_ref = refs[8:]
-    rows = query_ref.shape[0]
+    all_rows = query_ref.shape[0]
     factor = BF(HEAD_DIM**-0.5)
     query = query_ref[...] * factor
     key = jnp.concatenate([key_ref[...], key_far_ref[...]], axis=0)
     value = jnp.concatenate([value_ref[...], value_far_ref[...]], axis=0)
-    grad = jnp.concatenate([ref[...] for ref in grad_refs], axis=0)
+    grad = jnp.concatenate([ref[...] for ref in grad_refs], axis=0).astype(F32)
+    grad = grad * inverse_ref[...]
     mixed = jnp.concatenate([ref[...] for ref in mixed_refs], axis=0)
-    together = grad.astype(F32) * mixed.astype(F32)
-    grad_query = jnp.zeros((rows, PAIR), F32)
-    grad_key = jnp.zeros((2 * rows, PAIR), F32)
-    grad_value = jnp.zeros((2 * rows, PAIR), F32)
-    for head, (mask, mask_wide) in enumerate(zip(head_masks(BF), head_masks(F32))):
-        probs = probs_ref[head]
-        grad_one = grad * mask
-        row_dots = jnp.sum(together * mask_wide, axis=1, keepdims=True)
-        grad_probs = dot_nt(grad_one, value)
-        grad_scores = (probs.astype(F32) * (grad_probs - row_dots)).astype(BF)
-        grad_value = grad_value + dot_tn(probs, grad_one)
-        grad_key = grad_key + dot_tn(grad_scores, query * mask)
-        grad_query = grad_query + dot(grad_scores, key * (mask * factor))
-    grad_query_ref[...] = grad_query.astype(BF)
+    together = grad * mixed.astype(F32)
+    grad = grad.astype(BF)
+    grad_key = jnp.zeros((PAIR, 2 * all_rows), F32)
+    grad_value = jnp.zeros((PAIR, 2 * all_rows), F32)
+    for part in range(all_rows // (2 * CHUNK)):
+        rows = slice(part * 2 * CHUNK, (part + 1) * 2 * CHUNK)
+        grad_query = jnp.zeros((2 * CHUNK, PAIR), F32)
+        for head, (mask, mask_wide) in enumerate(zip(head_masks(BF), head_masks(F32))):
+            weights = weights_ref[head, rows]
+            grad_one = grad[rows] * mask
+            row_dots = jnp.sum(together[rows] * mask_wide, axis=1, keepdims=True)
+            grad_weights = dot_nt(grad_one, value)
+            grad_scores = (weights.astype(F32) * (grad_weights - row_dots)).astype(BF)
+            grad_value = grad_value + dot_tn(grad_one, weights)
+            grad_key = grad_key + dot_tn(query[rows] * mask, grad_scores)
+            grad_query = grad_query + dot(grad_scores, key * (mask * factor))
+        grad_query_ref[rows] = grad_query.astype(BF)
     for index, total in enumerate((grad_key, grad_value)):
-        grad_near_ref[index] = total[:rows].astype(BF)
-        grad_far_ref[index] = total[rows:].astype(BF)
-
-
-def attention_backward(queries, pair, pair_far, probs, grads, mixed):
+        total = total.T
+        grad_near_ref[index] = total[:all_rows].astype(BF)
+        grad_far_ref[index] = total[all_rows:].astype(BF)
+
+
+def attention_backward(queries, pair, pair_far, weights, inverse, grads, mixed):
     rows, half_width = queries.shape
     pairs = half_width // PAIR
     return pl.pallas_call(
@@ -220,14 +231,13 @@
         grid=(pairs,),
         in_specs=[pair_column(rows)]
         + [pair_column(rows), pair_column(rows, pairs)] * 2
-        + [probs_block(rows)]
+        + [weights_block(rows), pair_column(rows)]
         + [pair_column(rows // 4)] * 8,
         out_specs=[pair_column(rows)] + [pl.BlockSpec((2, rows, PAIR), lambda i: (0, 0, i))] * 2,
-        out_shape=[jax.ShapeDtypeStruct((rows, half_width), BF)]
-        + [jax.ShapeDtypeStruct((2, rows, half_width), BF)] * 2,
+        out_shape=[low_shape(rows, half_width)] + [low_shape(2, rows, half_width)] * 2,
         compiler_params=params(),
         cost_estimate=cost(2 * 10**10, 4096),
-    )(queries, pair, pair, pair_far, pair_far, probs, *grads, *mixed)
+    )(queries, pair, pair, pair_far, pair_far, weights, inverse, *grads, *mixed)
 
 
 GELU_SCALE = 0.7978845608028654
@@ -288,15 +298,133 @@
                 body(half, same)
 
 
+def turned_column(row):
+    count = row.shape[1]
+    rows = lax.broadcasted_iota(jnp.int32, (count, count), 0)
+    lanes = lax.broadcasted_iota(jnp.int32, (count, count), 1)
+    return jnp.sum(jnp.where(rows == lanes, row, 0.0), axis=1, keepdims=True)
+
+
+def turned_row(column):
+    count = column.shape[0]
+    rows = lax.broadcasted_iota(jnp.int32, (count, count), 0)
+    lanes = lax.broadcasted_iota(jnp.int32, (count, count), 1)
+    return jnp.sum(jnp.where(rows == lanes, column, 0.0), axis=0, keepdims=True)
+
+
+def pack_kernel(
+    flags_ref,
+    query_ref,
+    key_ref,
+    value_ref,
+    output_ref,
+    router_ref,
+    routes_ref,
+    norm_one_ref,
+    norm_two_ref,
+    kept_ref,
+    cross_ref,
+):
+    own_rows, width = query_ref.shape
+    experts = router_ref.shape[1]
+    half_width = width // 2
+    start = 3 * half_width
+    tail = kept_ref.shape[1] - start - width
+    scale = turned_column(norm_one_ref[...].astype(F32))
+    first_half = flags_ref[HALF] == 0
+    for index, ref in enumerate((query_ref, key_ref, value_ref)):
+        scaled = (ref[...].astype(F32) * scale).astype(BF)
+        low, high = scaled[:, :half_width], scaled[:, half_width:]
+        columns = slice(index * half_width, (index + 1) * half_width)
+        kept_ref[:, columns] = jnp.where(first_half, low, high)
+        cross_ref[:, columns] = jnp.where(first_half, high, low)
+    lanes = lax.broadcasted_iota(jnp.int32, (1, tail), 1)
+    index = lax.broadcasted_iota(jnp.int32, (tail, 1), 0) - experts
+    tally = jnp.sum((routes_ref[...] == index).astype(F32), axis=1, keepdims=True)
+    tally = turned_row(tally)
+    router = router_ref[...].astype(F32)
+    router = jnp.concatenate([router, jnp.zeros((own_rows, tail - experts), F32)], axis=1)
+    gain = turned_column(norm_two_ref[...].astype(F32))
+    small = jnp.where(lanes < experts, router, jnp.where(lanes == 2 * experts, gain, tally))
+    for ref in (kept_ref, cross_ref):
+        ref[:, start : start + width] = output_ref[...]
+        ref[:, start + width :] = small.astype(BF)
+
+
+def pack(flags, operands):
+    own_rows, width = operands[0].shape
+    experts = operands[4].shape[1]
+    tail = 2 * experts + 1
+    columns = 3 * width // 2 + width + tail + -tail % 128
+    return one_step(pack_kernel, flags, operands, [low_shape(own_rows, columns)] * 2)
+
+
+def finish_kernel(
+    flags_ref,
+    zero_ref,
+    one_ref,
+    two_ref,
+    three_ref,
+    query_ref,
+    key_ref,
+    value_ref,
+    norm_one_ref,
+    grad_query_ref,
+    grad_key_ref,
+    grad_value_ref,
+    grad_output_ref,
+    grad_router_ref,
+    grad_one_ref,
+    grad_two_ref,
+):
+    width = query_ref.shape[1]
+    experts = grad_router_ref.shape[1]
+    half_width = width // 2
+    start = 3 * half_width
+    near = zero_ref[...] + two_ref[...].astype(F32)
+    far = one_ref[...].astype(F32) + three_ref[...].astype(F32)
+    scale = turned_column(norm_one_ref[...].astype(F32))
+    first_half = flags_ref[HALF] == 0
+    total = jnp.zeros_like(scale)
+    pairs = ((query_ref, grad_query_ref), (key_ref, grad_key_ref), (value_ref, grad_value_ref))
+    for index, (ref, grad_ref) in enumerate(pairs):
+        columns = slice(index * half_width, (index + 1) * half_width)
+        low = jnp.where(first_half, near[:, columns], far[:, columns])
+        high = jnp.where(first_half, far[:, columns], near[:, columns])
+        weight = ref[...].astype(F32)
+        total = total + jnp.sum(weight[:, :half_width] * low, axis=1, keepdims=True)
+        total = total + jnp.sum(weight[:, half_width:] * high, axis=1, keepdims=True)
+        grad_ref[:, :half_width] = low * scale
+        grad_ref[:, half_width:] = high * scale
+    grad_one_ref[...] = turned_row(total)
+    both = near[:, start:] + far[:, start:]
+    grad_output_ref[...] = both[:, :width]
+    small = both[:, width:]
+    grad_router_ref[...] = small[:, :experts]
+    lanes = lax.broadcasted_iota(jnp.int32, (1, small.shape[1]), 1)
+    gain = jnp.sum(jnp.where(lanes == experts, small, 0.0), axis=1, keepdims=True)
+    grad_two_ref[...] = turned_row(gain)
+
+
+def finish(flags, operands, experts):
+    own_rows, width = operands[4].shape
+    shapes = [wide_shape(own_rows, width)] * 4
+    shapes += [wide_shape(own_rows, experts)] + [wide_shape(1, own_rows)] * 2
+    return one_step(finish_kernel, flags, operands, shapes, size=SMALL_BYTES)
+
+
 def project_kernel(count, flags_ref, normed_ref, *refs):
     own_refs, other_refs = refs[:count], refs[count : 2 * count]
-    query_ref, pair_ref, weight_ref = refs[2 * count :]
+    query_ref, pair_ref, weight_ref, extra_ref = refs[2 * count :]
+    columns = weight_ref.shape[1]
     rows = own_refs[0].shape[0]
     core = flags_ref[CORE]
     for m in range(count):
         place = 2 * (flags_ref[PLACE] ^ m)
         for index, ref in ((place + core, own_refs[m]), (place + 1 - core, other_refs[m])):
-            weight_ref[pl.ds(pl.multiple_of(index * rows, 16), rows), :] = ref[...]
+            place_rows = pl.ds(pl.multiple_of(index * rows, 16), rows)
+            weight_ref[place_rows, :] = ref[:, :columns]
+            extra_ref[place_rows, :] = ref[:, columns:]
     projected = dot(normed_ref[...], weight_ref[...]).astype(BF)
     query_ref[...] = projected[:, : query_ref.shape[1]]
     pair_ref[...] = projected[:, query_ref.shape[1] :]
@@ -305,14 +433,15 @@
 def project(flags, normed, own, other):
     count = len(own)
     rows, width = normed.shape
-    columns = own[0].shape[1]
+    columns = 3 * width // 2
     shapes = [
-        low_shape(rows, columns // 3),
-        low_shape(rows, columns * 2 // 3),
+        low_shape(rows, width // 2),
+        low_shape(rows, width),
         low_shape(width, columns),
+        low_shape(width, own[0].shape[1] - columns),
     ]
     kernel = functools.partial(project_kernel, count)
-    return one_step(kernel, flags, [normed, *own, *other], shapes, size=SMALL_BYTES)
+    return one_step(kernel, flags, [normed, *own, *other], shapes)
 
 
 def mixed_route_kernel(flags_ref, zero_ref, one_ref, two_ref, three_ref, mine_ref, sent_ref):
@@ -391,10 +520,41 @@
     return one_step(owner_forward_kernel, flags, operands, shapes)
 
 
+TILE = 1024
+
+
+def cotangent_kernel(cot_ref, compact_ref, weight_out_ref, held_ref, back_ref):
+    @pl.when(pl.program_id(0) == 0)
+    def _():
+        held_ref[...] = dot(compact_ref[...], cot_ref[...]).astype(BF)
+
+    back_ref[...] = dot_nt(held_ref[...], weight_out_ref[0]).astype(BF)
+
+
+def cotangent_layer(cot, compact, expert_out):
+    slots, width = cot.shape
+    capacity = compact.shape[0]
+    hidden_width = expert_out.shape[1]
+    return pl.pallas_call(
+        cotangent_kernel,
+        grid=(hidden_width // TILE,),
+        in_specs=[
+            whole((slots, width)),
+            whole((capacity, slots)),
+            pl.BlockSpec((1, TILE, width), lambda i: (0, i, 0)),
+        ],
+        out_specs=[whole((capacity, width)), pl.BlockSpec((capacity, TILE), lambda i: (0, i))],
+        out_shape=[low_shape(capacity, width), low_shape(capacity, hidden_width)],
+        compiler_params=params(),
+        cost_estimate=cost(2 * capacity * width * hidden_width, 4 * width * hidden_width),
+    )(cot, compact, expert_out)
+
+
 def expert_kernel(
     flags_ref,
     arrived_ref,
     cot_ref,
+    back_ref,
     compact_ref,
     expand_ref,
     router_ref,
@@ -405,11 +565,10 @@
     hidden_ref,
     grad_inner_ref,
     grad_back_ref,
-    taken_back_ref,
+    taken_ref,
     grad_logits_ref,
     result_sum,
     grad_sum,
-    cot_held,
     probs,
     gates,
 ):
@@ -422,74 +581,70 @@
     def _():
         held = dot(compact_ref[...], arrived_ref[...]).astype(BF)
         held_ref[...] = held
-        cot = dot(compact_ref[...], cot_ref[...])
-        cot_held[...] = cot
         logits = dot(held, router_ref[...])
         weights = jnp.exp(logits - jnp.max(logits, axis=1, keepdims=True))
         router_probs = weights / jnp.sum(weights, axis=1, keepdims=True)
         probs[...] = router_probs
         gate = jnp.sum(router_probs * mine, axis=1, keepdims=True)
         gates[...] = gate
-        grad_result_ref[...] = (gate * cot).astype(BF)
+        grad_result_ref[...] = (gate * cot_ref[...].astype(F32)).astype(BF)
         result_sum[...] = jnp.zeros_like(result_sum)
         grad_sum[...] = jnp.zeros_like(grad_sum)
 
     weight_in = weight_in_ref[0]
-    weight_out = weight_out_ref[0]
     hidden, slope = gelu_and_slope(dot(held_ref[...], weight_in))
     hidden = hidden.astype(BF)
     hidden_ref[...] = hidden
-    grad_inner = (dot_nt(grad_result_ref[...], weight_out) * slope).astype(BF)
+    grad_inner = (back_ref[...].astype(F32) * (gates[...] * slope)).astype(BF)
     grad_inner_ref[...] = grad_inner
-    result_sum[...] += dot(hidden, weight_out)
+    result_sum[...] += dot(hidden, weight_out_ref[0])
     grad_sum[...] += dot_nt(grad_inner, weight_in)
 
     @pl.when(step == pl.num_programs(0) - 1)
     def _():
         result = result_sum[...].astype(BF).astype(F32)
         gate = gates[...]
-        grad_gate = jnp.sum(cot_held[...] * result, axis=1, keepdims=True)
+        grad_gate = jnp.sum(cot_ref[...].astype(F32) * result, axis=1, keepdims=True)
         grad_logits = (grad_gate * probs[...] * (mine - gate)).astype(BF)
         grad_logits_ref[...] = grad_logits
         grad_held = grad_sum[...] + dot_nt(grad_logits, router_ref[...])
         grad_back_ref[...] = dot(expand_ref[...], grad_held.astype(BF)).astype(BF)
-        taken_back_ref[...] = dot(expand_ref[...], (gate * result).astype(BF)).astype(BF)
-
-
-def expert_layer(flags, arrived, cot, compact, expand, router, expert_in, expert_out):
+        taken_ref[...] = (gate * result).astype(BF)
+
+
+def expert_layer(flags, arrived, cot, back, compact, expand, router, expert_in, expert_out):
     slots, width = arrived.shape
     capacity = compact.shape[0]
     hidden_width = expert_in.shape[2]
     experts = router.shape[1]
-    tile = 1024
     wide = whole((capacity, width))
-    tall = pl.BlockSpec((capacity, tile), lambda i: (0, i))
+    tall = pl.BlockSpec((capacity, TILE), lambda i: (0, i))
     return pl.pallas_call(
         expert_kernel,
-        grid=(hidden_width // tile,),
+        grid=(hidden_width // TILE,),
         in_specs=[
             FLAGS,
             whole((slots, width)),
-            whole((slots, width)),
+            wide,
+            tall,
             whole((capacity, slots)),
             whole((slots, capacity)),
             whole((width, experts)),
-            pl.BlockSpec((1, width, tile), lambda i: (0, 0, i)),
-            pl.BlockSpec((1, tile, width), lambda i: (0, i, 0)),
+            pl.BlockSpec((1, width, TILE), lambda i: (0, 0, i)),
+            pl.BlockSpec((1, TILE, width), lambda i: (0, i, 0)),
         ],
-        out_specs=[wide, wide, tall, tall, whole((slots, width)), whole((slots, width))]
+        out_specs=[wide, wide, tall, tall, whole((slots, width)), wide]
         + [whole((capacity, experts))],
         out_shape=[
-            jax.ShapeDtypeStruct((capacity, width), BF),
-            jax.ShapeDtypeStruct((capacity, width), BF),
-            jax.ShapeDtypeStruct((capacity, hidden_width), BF),
-            jax.ShapeDtypeStruct((capacity, hidden_width), BF),
-            jax.ShapeDtypeStruct((slots, width), BF),
-            jax.ShapeDtypeStruct((slots, width), BF),
-            jax.ShapeDtypeStruct((capacity, experts), BF),
+            low_shape(capacity, width),
+            low_shape(capacity, width),
+            low_shape(capacity, hidden_width),
+            low_shape(capacity, hidden_width),
+            low_shape(slots, width),
+            low_shape(capacity, width),
+            low_shape(capacity, experts),
         ],
         scratch_shapes=[
-            pltpu.VMEM((capacity, width), F32),
             pltpu.VMEM((capacity, width), F32),
             pltpu.VMEM((capacity, width), F32),
             pltpu.VMEM((capacity, experts), F32),
@@ -497,7 +652,7 @@
         ],
         compiler_params=params(),
         cost_estimate=cost(8 * capacity * width * hidden_width, 8 * width * hidden_width),
-    )(flags, arrived, cot, compact, expand, router, expert_in, expert_out)
+    )(flags, arrived, cot, back, compact, expand, router, expert_in, expert_out)
 
 
 def owner_backward_kernel(
@@ -570,34 +725,6 @@
     return [wide_shape(width // 2, columns), low_shape(width // 2, columns)]
 
 
-def output_grads_kernel(
-    rows, flags_ref, mixed_ref, branch_ref, router_ref, gain_ref, keep_ref, send_ref, total
-):
-    width, experts = router_ref.shape
-    extra = total.shape[1] - width
-    total[:, :width] = dot_tn(mixed_ref[...], branch_ref[...])
-    gain = dot_tn(gain_ref[...], jnp.ones((GAIN_ROWS, extra), BF))
-    router = router_ref[...]
-    router = jnp.concatenate([router, jnp.zeros((width, extra - experts), F32)], axis=1)
-    lanes = lax.broadcasted_iota(jnp.int32, (1, extra), 1)
-    total[:, width:] = jnp.where(lanes == experts, gain, router)
-    deal_rows(flags_ref, total, keep_ref, send_ref, rows)
-
-
-def output_grads(flags, mixed, branch, router, gain_rows, rows):
-    width, experts = router.shape
-    columns = width + experts + 1
-    columns += -columns % 128
-    return one_step(
-        functools.partial(output_grads_kernel, rows),
-        flags,
-        [mixed, branch, router, gain_rows],
-        dealt(width, columns),
-        [pltpu.VMEM((width, columns), F32)],
-        SMALL_BYTES,
-    )
-
-
 def weight_grads_kernel(
     rows,
     flags_ref,
@@ -605,30 +732,45 @@
     query_ref,
     near_ref,
     got_ref,
+    mixed_ref,
+    branch_ref,
+    router_ref,
+    gain_ref,
     projected_ref,
     keep_ref,
     send_ref,
     total,
 ):
     part = query_ref.shape[1]
+    width, experts = router_ref.shape
+    extra = total.shape[1] - 3 * part - width
     projected_ref[:, :part] = query_ref[...]
     for index in range(2):
         both = near_ref[index].astype(F32) + got_ref[index].astype(F32)
         projected_ref[:, (index + 1) * part : (index + 2) * part] = both.astype(BF)
-    total[...] = dot_tn(normed_ref[...], projected_ref[...])
+    total[:, : 3 * part] = dot_tn(normed_ref[...], projected_ref[...])
+    total[:, 3 * part : 3 * part + width] = dot_tn(mixed_ref[...], branch_ref[...])
+    gain = dot_tn(gain_ref[...], jnp.ones((GAIN_ROWS, extra), BF))
+    router = router_ref[...]
+    router = jnp.concatenate([router, jnp.zeros((width, extra - experts), F32)], axis=1)
+    lanes = lax.broadcasted_iota(jnp.int32, (1, extra), 1)
+    total[:, 3 * part + width :] = jnp.where(lanes == experts, gain, router)
     deal_rows(flags_ref, total, keep_ref, send_ref, rows)
 
 
-def weight_grads(flags, normed, query, near, got, rows):
-    work_rows, width = normed.shape
-    columns = 3 * query.shape[1]
+def weight_grads(flags, operands, rows):
+    work_rows, width = operands[0].shape
+    part = operands[1].shape[1]
+    experts = operands[6].shape[1]
+    columns = 3 * part + width + experts + 1
+    columns += -columns % 128
     return one_step(
         functools.partial(weight_grads_kernel, rows),
         flags,
-        [normed, query, near, got],
-        [low_shape(work_rows, columns)] + dealt(width, columns),
+        operands,
+        [low_shape(work_rows, 3 * part)] + dealt(width, columns),
         [pltpu.VMEM((width, columns), F32)],
-        SMALL_BYTES,
+        2 * SMALL_BYTES,
     )
 
 
@@ -668,31 +810,21 @@
 
     mine = pick(core, inputs[:half_rows], inputs[half_rows:])
     got = links.swap_core(pick(core, inputs[half_rows:], inputs[:half_rows]))
-    scale = norm_one.astype(F32)[:, None]
-    scaled = [(w.astype(F32) * scale).astype(BF) for w in (w_query, w_key, w_value)]
-    low = jnp.concatenate([w[:, :half_width] for w in scaled], axis=1)
-    high = jnp.concatenate([w[:, half_width:] for w in scaled], axis=1)
-    kept, cross = pick(level & 1, low, high), pick(level & 1, high, low)
-    chosen = routes[:, 0]
-    picked = (chosen[:, None] == jnp.arange(experts, dtype=jnp.int32)[None, :]).astype(jnp.int32)
-    tally = jnp.sum(picked, axis=0).astype(BF)
-    extra = jnp.concatenate(
-        [w_output, w_router, jnp.broadcast_to(tally[None], (own_rows, experts)), norm_two[:, None]],
-        axis=1,
-    )
-    extra = jnp.pad(extra, ((0, 0), (0, -extra.shape[1] % 128)))
-    kept = jnp.concatenate([kept, extra], axis=1)
-    cross = jnp.concatenate([cross, extra], axis=1)
+    kept, cross = pack(
+        flags,
+        [w_query, w_key, w_value, w_output, w_router, routes.reshape(1, rows)]
+        + [norm_one.reshape(1, own_rows), norm_two.reshape(1, own_rows)],
+    )
     level_block = gather_levels(links, [kept, cross, kept, cross])
     level_rows = level_block.shape[0]
-    level_weights = level_block[:, : 3 * half_width]
     got = gate(got, kept, cross)
     near, far = pick(same, mine, got), pick(same, got, mine)
     near_first = links.swap_level(near, 1)
     far_first = links.swap_level(far, 2)
     far_second = links.swap_level(far_first, 1)
-    own_weights = gather_groups(links, level_weights)
-    picked = gate(picked, level_block)
+    own_blocks = gather_groups(links, level_block)
+    chosen = gate(routes, level_block)[:, 0]
+    picked = (chosen[:, None] == jnp.arange(experts, dtype=jnp.int32)[None, :]).astype(jnp.int32)
     rank = jnp.sum((jnp.cumsum(picked, axis=0) - picked) * picked, axis=1)
     place = chosen * most + rank
     slot_index = jnp.arange(experts * most, dtype=jnp.int32)
@@ -700,29 +832,26 @@
     to_tokens = (place[:, None] == slot_index[None, :]).astype(BF)
     cot_slots = dot(to_slots, cotangent).astype(BF).reshape(experts, most, width)
 
-    own_weights = tie(*own_weights, near_first, far_first, cot_slots)[:-3]
-    other_weights = [links.swap_core(part) for part in own_weights]
+    own_blocks = tie(*own_blocks, near_first, far_first, cot_slots)[:-3]
+    other_blocks = [links.swap_core(part) for part in own_blocks]
 
     source = jnp.concatenate([near, near_first, far_first, far_second], axis=0).astype(F32)
     normed_work = (
         source * lax.rsqrt(jnp.mean(source * source, axis=-1, keepdims=True) + EPSILON)
     ).astype(BF)
     if level_rows % 16 == 0:
-        queries, pair, weights = project(flags, normed_work, own_weights, other_weights)
+        queries, pair, weights, full_extra = project(flags, normed_work, own_blocks, other_blocks)
     else:
-        weights = in_order(links, own_weights, other_weights)
+        full = in_order(links, own_blocks, other_blocks)
+        weights, full_extra = full[:, : 3 * half_width], full[:, 3 * half_width :]
         projected = dot(normed_work, weights).astype(BF)
         queries, pair = projected[:, :half_width], projected[:, half_width:]
     pair_far = links.swap_core(pair)
-    cot_arrived = all_to_all(gate(cot_slots, far_second, *other_weights)).reshape(-1, width)
-    *mixed_parts, probs = attention_forward(queries, pair, pair_far)
+    cot_arrived = all_to_all(gate(cot_slots, far_second)).reshape(-1, width)
+    *mixed_parts, attention_weights, inverse = attention_forward(queries, pair, pair_far)
     mixed_parts = tie(*mixed_parts, cot_arrived)[:-1]
 
     back = tie(*[links.swap_level(mixed_parts[b], b) for b in (1, 2, 3)])
-    level_extra = gate(level_block[:, 3 * half_width :], queries)
-    own_extra = gather_groups(links, level_extra)
-    other_extra = [links.swap_core(gate(part, *back)) for part in own_extra]
-    full_extra = in_order(links, own_extra, other_extra)
     full_router = full_extra[:, width : width + experts]
     gain_two = full_extra[:, width + 2 * experts].astype(F32)[None]
     tallies = full_extra[::own_rows, width + experts : width + 2 * experts].astype(F32)
@@ -743,35 +872,51 @@
     )
     arrived = all_to_all(second_slots.reshape(experts, most, width)).reshape(-1, width)
 
-    held, grad_result, hidden, grad_inner, grad_back, taken_back, grad_logits = expert_layer(
-        flags, arrived, cot_arrived, compact, expand, full_router, expert_in, expert_out
+    cot_held, cot_back = cotangent_layer(gate(cot_arrived, second_slots), compact, expert_out)
+    held, grad_result, hidden, grad_inner, grad_back, taken_held, grad_logits = expert_layer(
+        flags,
+        gate(arrived, cot_back),
+        cot_held,
+        cot_back,
+        compact,
+        expand,
+        full_router,
+        expert_in,
+        expert_out,
     )
     grad_returned = all_to_all(grad_back.reshape(experts, most, width)).reshape(-1, width)
     grad_router = dot_tn(held, grad_logits)
     grad_weight_out = dot_tn(hidden, grad_result)
     grad_weight_in = dot_tn(held, grad_inner)
-    grad_returned = gate(grad_returned, grad_weight_in, grad_weight_out, grad_router)
+    taken_back = dot(expand, taken_held).astype(BF)
+    grad_returned = gate(
+        grad_returned, grad_weight_in, grad_weight_out, grad_router, taken_back, to_tokens
+    )
 
     grad_middle, grad_branch, grad_mine, grad_sent, gain_rows = owner_backward(
         flags, grad_returned, to_tokens, cotangent, middle, gain_two, full_extra
     )
     routed = grad_route(flags, grad_mine, links.swap_core(grad_sent))
-    got = tie(*[links.swap_level(routed[b], b) for b in (1, 2, 3)])
-
-    keep, send = output_grads(flags, gate(mixed_low, routed[0]), grad_branch, grad_router, gain_rows, level_rows)
-    summed = reduce_cores(links, keep, send)
-    summed = reduce_groups(
-        links, [summed[m * level_rows : (m + 1) * level_rows] for m in range(links.groups // 2)]
-    )
-    got = tie(*got, summed)[:-1]
+    got = [links.swap_level(routed[b], b) for b in (1, 2, 3)]
+
+    got = tie(*got)
     taken_back = gate(taken_back, *got).reshape(experts, most, width)
     taken_arrived = all_to_all(taken_back).reshape(-1, width)
     grad_queries, grad_near, grad_far = attention_backward(
-        queries, pair, pair_far, probs, [routed[0], *got], mixed_parts
+        queries,
+        pair,
+        pair_far,
+        attention_weights,
+        inverse,
+        [routed[0], *got],
+        mixed_parts,
     )
     got_pair = links.swap_core(grad_far)
     grad_projected, keep, send = weight_grads(
-        flags, normed_work, grad_queries, grad_near, got_pair, level_rows
+        flags,
+        [normed_work, grad_queries, grad_near, got_pair]
+        + [mixed_low, grad_branch, grad_router, gain_rows],
+        level_rows,
     )
     grad_first_work = dot_nt(grad_projected, weights).astype(BF)
     core_sum = reduce_cores(links, keep, gate(send, taken_arrived))
@@ -792,37 +937,21 @@
     )
     output = (middle + dot(to_tokens, taken_arrived)).astype(BF)
 
-    columns = group_sum.shape[1]
-    sums = jnp.concatenate([group_sum, summed], axis=1)
-    sums = reduce_levels(links, gate(sums, *back))
-    zero, one, two, three = [part[:, :columns] for part in sums]
-    summed = sum(part[:, columns:] for part in sums)
-    kept, cross = zero + two, one + three
-    low, high = pick(level & 1, kept, cross), pick(level & 1, cross, kept)
-    grad_weights = [
-        jnp.concatenate(
-            [part[:, i * half_width : (i + 1) * half_width] for part in (low, high)], axis=1
-        )
-        for i in range(3)
-    ]
-    grad_norm_one = sum(
-        jnp.sum(w.astype(F32) * g, axis=1)
-        for w, g in zip((w_query, w_key, w_value), grad_weights)
-    )
-    grad_weights = [g * scale for g in grad_weights]
-
-    grad_w_output = summed[:, :width]
-    grad_w_router = summed[:, width : width + experts]
-    grad_norm_two = summed[:, width + experts]
+    sums = reduce_levels(links, gate(group_sum, *back))
+    *grad_weights, grad_w_output, grad_w_router, grad_norm_one, grad_norm_two = finish(
+        flags,
+        [*sums, w_query, w_key, w_value, norm_one.reshape(1, own_rows)],
+        experts,
+    )
     return (
         output,
         grad_input,
-        grad_norm_one,
+        grad_norm_one.reshape(own_rows),
         grad_weights[0],
         grad_weights[1],
         grad_weights[2],
         grad_w_output,
-        grad_norm_two,
+        grad_norm_two.reshape(own_rows),
         grad_w_router,
         grad_weight_in[None],
         grad_weight_out[None],

time: 256 us -> 236 us (0.922)
  waiting for transfers between devices: 80.9 us -> 69.6 us
  starting transfers between devices: 67.8 us -> 58.5 us
  Pallas kernels: 49.9 us -> 58.4 us
  other arithmetic: 19.1 us -> 12 us
    all_to_all x4, waiting for transfers between devices: 32.8 us -> 17 us  [all_to_all(): return lax.all_to_all(array, AXES, split_axis=0, concat_axis=0, tiled=True)]
    ppermute x46 -> x35, starting transfers between devices: 52.9 us -> 42.7 us  [permute(): return lax.ppermute(array, AXES, pairs)]
    pallas_call x7 -> x8, Pallas kernels: 14.4 us -> 22.2 us  [one_step(): pl.pallas_call(kernel, grid=(1,), in_specs=[FLAGS] + [whole(operand.shape...]
    pallas_call x1 -> x2, Pallas kernels: 14.3 us -> 19.5 us  [the longest x1 13.5 us: expert_layer(): pl.pallas_call(expert_kernel, grid=(hidden_width // TILE,), in_specs=[FLA...]
    ppermute x46 -> x35, waiting for transfers between devices: 48 us -> 52.6 us  [permute(): return lax.ppermute(array, AXES, pairs)]
    pallas_call x1, Pallas kernels: 11 us -> 7.81 us  [attention_forward(): pl.pallas_call(forward_kernel, grid=(pairs,), in_specs=[pair_column(rows)...]
    dot_general x2 -> x3, matrix products: 3.56 us -> 6.11 us  [dot(): return jnp.dot(left, right, preferred_element_type=F32)]
    unnamed x78 -> x84, local copies, waits for them, and re-layouts: 12.2 us -> 10.5 us
  transfers between devices with their start and end apart: 50 -> 39, of which waited for: 20 -> 17; matrix products, arithmetic and copies ran while one was open for 13% -> 15% of each run, Pallas kernels for 9% -> 14%
where the time goes in v1:
time: 236 us; the launch traced here: 235 us
  waiting for transfers between devices  69.6 us (29%)
  starting transfers between devices  58.5 us (25%)
  Pallas kernels  58.4 us (25%)
  matrix products  19.9 us (8%)
  local copies, waits for them, and re-layouts  15.1 us (6%)
  other arithmetic  12 us (5%)
    ppermute x35, waiting for transfers between devices, permute(): return lax.ppermute(array, AXES, pairs)  52.6 us
    ppermute x35, starting transfers between devices, permute(): return lax.ppermute(array, AXES, pairs)  42.7 us
    pallas_call x8, Pallas kernels, one_step(): pl.pallas_call(kernel, grid=(1,), in_specs=[FLAGS] + [whole(operand.shape...  22.2 us
    all_to_all x4, waiting for transfers between devices, all_to_all(): return lax.all_to_all(array, AXES, split_axis=0, concat_axis=0, tiled=True)  17 us
    all_to_all x4, starting transfers between devices, all_to_all(): return lax.all_to_all(array, AXES, split_axis=0, concat_axis=0, tiled=True)  15.7 us
    pallas_call x1, Pallas kernels, expert_layer(): pl.pallas_call(expert_kernel, grid=(hidden_width // TILE,), in_specs=[FLA...  13.5 us
    dot_general x3, matrix products, dot_tn(): lax.dot_general(left, right, (((0,), (0,)), ((), ())), preferred_element_...  10.6 us
    unnamed x84, local copies, waits for them, and re-layouts  10.5 us
  transfers between devices with their start and end apart: 39, of which 17 were waited for; matrix products, arithmetic and copies ran while one was open for 15% of the time, Pallas kernels for 14%

profile of v1, /device:TPU:0, one launch (start us, length us, event | category | flops | bytes accessed | tf_op | source)
XLA Modules:
  0.0 234.9 jit_solution(10289117653512519888)
XLA Ops:
  1.3 1.7 shard_map.203
  2.9 3.0 %collective-permute-start.4 = (bf16[24,2048]{1,0:T(8,128)(2,1)}, bf16[24,2048]{1,0:T(8,128)(2,1)S(1)}, u32[]{:S(2)}, u32[]{:S(2)}) collective-permute-start(bf16[24,2048]{1,0:T(8,128)(2,1)} %get-tuple-element.97), channel_id=1, source_target_pairs={{0,1},{1,0},{2,3},{3,2},{4,5},{5,4},{6,7},{7,6},{8,9},{9,8},{10,11... | collective-permute-start | bytes 294920 | tf_op jit(solution)/shard_map/ppermute | solution.py:45
  5.9 2.5 %collective-permute-start.6 = (bf16[24,2048]{1,0:T(8,128)(2,1)}, bf16[24,2048]{1,0:T(8,128)(2,1)S(1)}, u32[]{:S(2)}, u32[]{:S(2)}) collective-permute-start(bf16[24,2048]{1,0:T(8,128)(2,1)} %get-tuple-element.97), channel_id=1, source_target_pairs={{0,3},{1,2},{2,1},{3,0},{4,7},{5,6},{6,5},{7,4},{8,11},{9,10},{10,... | collective-permute-start | bytes 294920 | tf_op jit(solution)/shard_map/ppermute | solution.py:45
  9.7 7.9 %collective-permute-done.5 = bf16[24,2048]{1,0:T(8,128)(2,1)S(1)} collective-permute-done((bf16[24,2048]{1,0:T(8,128)(2,1)}, bf16[24,2048]{1,0:T(8,128)(2,1)S(1)}, u32[]{:S(2)}, u32[]{:S(2)}) %collective-permute-start.5) | collective-permute-done | bytes 98336 | tf_op jit(solution)/shard_map/ppermute | solution.py:45
  18.7 1.6 collective-permute-start.7
  20.2 1.5 collective-permute-start.8
  23.8 2.6 %collective-permute-start.1 = (bf16[128,768]{1,0:T(8,128)(2,1)S(1)}, bf16[128,768]{1,0:T(8,128)(2,1)S(1)}, u32[]{:S(2)}, u32[]{:S(2)}) collective-permute-start(bf16[128,768]{1,0:T(8,128)(2,1)S(1)} %get-tuple-element.192), channel_id=1, source_target_pairs={{0,1},{1,0},{2,3},{3,2},{4,5},{5,4},{6,7},{7,6},{8,9},{9,8},{10,11... | collective-permute-start | bytes 589832 | tf_op jit(solution)/shard_map/ppermute | solution.py:45
  26.5 7.1 %collective-permute-done.2 = bf16[128,768]{1,0:T(8,128)(2,1)S(1)} collective-permute-done((bf16[128,768]{1,0:T(8,128)(2,1)S(1)}, bf16[128,768]{1,0:T(8,128)(2,1)S(1)}, u32[]{:S(2)}, u32[]{:S(2)}) %collective-permute-start.2) | collective-permute-done | bytes 196640 | tf_op jit(solution)/shard_map/ppermute | solution.py:45
  34.9 4.1 %collective-permute-done.8.refs_2_ = bf16[96,2048]{1,0:T(8,128)(2,1)S(1)} collective-permute-done((bf16[96,2048]{1,0:T(8,128)(2,1)S(1)}, bf16[96,2048]{1,0:T(8,128)(2,1)S(1)}, u32[]{:S(2)}, u32[]{:S(2)}) %collective-permute-start.8) | collective-permute-done | bytes 393248 | tf_op jit(solution)/shard_map/ppermute | solution.py:45
  40.1 3.6 %all-to-all-start = ((bf16[32,16,768]{2,1,0:T(8,128)(2,1)}), bf16[32,16,768]{2,1,0:T(8,128)(2,1)S(1)}, u32[]{:S(2)}, u32[]{:S(2)}) async-start(bf16[32,16,768]{2,1,0:T(8,128)(2,1)} %bitcast.11), calls=%async_computation | async-start | bytes 1572864 | tf_op jit(solution)/shard_map/all_to_all | solution.py:778
  45.7 5.3 %shard_map.204 = (bf16[512,384]{1,0:T(8,128)(2,1)}, bf16[512,768]{1,0:T(8,128)(2,1)}, bf16[768,1152]{1,0:T(8,128)(2,1)}, bf16[768,896]{1,0:T(8,128)(2,1)}) custom-call(s32[5]{0:T(128)} %stack.23.flags_ref, bf16[512,768]{1,0:T(8,128)(2,1)} %fusion.1.normed_ref, bf16[96,2048]{1,0:T(8,128)(2,1)} %copy-done.26, bf16[96,2048]{1,0:T(8,128)(2,1)} %copy-done.31, ...), custom_call_target="tpu_custom_call" | custom-call | bytes 1048576 | tf_op jit(solution)/shard_map/pallas_call | solution.py:272
  52.1 1.4 collective-permute-done.14.key_far_ref.value_far_ref
  54.4 7.8 %shard_map.205 = (bf16[128,384]{1,0:T(8,128)(2,1)}, bf16[128,384]{1,0:T(8,128)(2,1)}, bf16[128,384]{1,0:T(8,128)(2,1)}, bf16[128,384]{1,0:T(8,128)(2,1)}, bf16[6...) custom-call(bf16[512,384]{1,0:T(8,128)(2,1)} %get-tuple-element.107.query_ref, ...), custom_call_target="tpu_custom_call" | custom-call | flops 2000000000 | bytes 4096 | tf_op jit(solution)/shard_map/pallas_call | solution.py:178
  63.2 2.9 %collective-permute-start.15 = (bf16[128,384]{1,0:T(8,128)(2,1)}, bf16[128,384]{1,0:T(8,128)(2,1)S(1)}, u32[]{:S(2)}, u32[]{:S(2)}) collective-permute-start(bf16[128,384]{1,0:T(8,128)(2,1)} %get-tuple-element.115.refs_5_), channel_id=1, source_target_pairs={{0,1},{1,0},{2,3},{3,2},{4,5},{5,4},{6,7},{7,6},{8,9},{9,8},{10,11... | collective-permute-start | bytes 294920 | tf_op jit(solution)/shard_map/ppermute | solution.py:45
  66.9 1.6 collective-permute-start.17
  70.7 5.2 %collective-permute-done.16.two_ref = bf16[128,384]{1,0:T(8,128)(2,1)S(1)} collective-permute-done((bf16[128,384]{1,0:T(8,128)(2,1)}, bf16[128,384]{1,0:T(8,128)(2,1)S(1)}, u32[]{:S(2)}, u32[]{:S(2)}) %collective-permute-start.16) | collective-permute-done | bytes 98336 | tf_op jit(solution)/shard_map/ppermute | solution.py:45
  80.6 3.6 %shard_map.207 = (bf16[256,768]{1,0:T(8,128)(2,1)}, f32[256,768]{1,0:T(8,128)}, bf16[512,768]{1,0:T(8,128)(2,1)}) custom-call(s32[5]{0:T(128)} %stack.23.flags_ref, bf16[128,768]{1,0:T(8,128)(2,1)} %copy-done.5, bf16[128,768]{1,0:T(8,128)(2,1)} %copy-done.35, bf16[256,768]{1,0:T(8,128)(2,1)} %inputs_ref.1, bf16[768,896]{1,0:T(8,128)(2,1)} %get-tuple-element.123.weight_ref, ...), custom_call_target="tpu_custom_call" | custom-call | bytes 1048576 | tf_op jit(solution)/shard_map/pallas_call | solution.py:272
  84.2 4.2 %all-to-all-start.1 = ((bf16[32,16,768]{2,1,0:T(8,128)(2,1)}), bf16[32,16,768]{2,1,0:T(8,128)(2,1)S(1)}, u32[]{:S(2)}, u32[]{:S(2)}) async-start(bf16[32,16,768]{2,1,0:T(8,128)(2,1)} %bitcast.63), calls=%async_computation.1 | async-start | bytes 1572864 | tf_op jit(solution)/shard_map/all_to_all | solution.py:778
  88.4 1.6 slice.60.router_ref
  92.4 6.0 %shard_map.208 = (bf16[320,768]{1,0:T(8,128)(2,1)}, bf16[320,3072]{1,0:T(8,128)(2,1)}) custom-call(bf16[512,768]{1,0:T(8,128)(2,1)} %bitcast.60, bf16[320,512]{1,0:T(8,128)(2,1)} %fusion.9.compact_ref, bf16[1,3072,768]{2,1,0:T(8,128)(2,1)} %weight_out_ref.3), custom_call_target="tpu_custom_call" | custom-call | flops 1509949440 | bytes 9437184 | tf_op jit(solution)/shard_map/pallas_call | solution.py:538
  98.4 9.5 %all-to-all-done.1 = bf16[32,16,768]{2,1,0:T(8,128)(2,1)S(1)} async-done(((bf16[32,16,768]{2,1,0:T(8,128)(2,1)}), bf16[32,16,768]{2,1,0:T(8,128)(2,1)S(1)}, u32[]{:S(2)}, u32[]{:S(2)}) %all-to-all-start.1) | async-done | bytes 786464 | tf_op jit(solution)/shard_map/all_to_all | solution.py:778
  108.8 13.5 %shard_map.209 = (bf16[320,768]{1,0:T(8,128)(2,1)}, bf16[320,768]{1,0:T(8,128)(2,1)}, bf16[320,3072]{1,0:T(8,128)(2,1)}, bf16[320,3072]{1,0:T(8,128)(2,1)}, bf16...) custom-call(s32[5]{0:T(128)} %stack.23.flags_ref, bf16[512,768]{1,0:T(8,128)(2,1)} %bitcast.62, ...), custom_call_target="tpu_custom_call" | custom-call | flops 6039797760 | bytes 18874368 | tf_op jit(solution)/shard_map/pallas_call | solution.py:622
  122.3 4.4 %all-to-all-start.2 = ((bf16[32,16,768]{2,1,0:T(8,128)(2,1)}), bf16[32,16,768]{2,1,0:T(8,128)(2,1)S(1)}, u32[]{:S(2)}, u32[]{:S(2)}) async-start(bf16[32,16,768]{2,1,0:T(8,128)(2,1)} %bitcast.64), calls=%async_computation.2 | async-start | bytes 1572864 | tf_op jit(solution)/shard_map/all_to_all | solution.py:778
  126.9 2.5 %convolution_convert_fusion = bf16[512,768]{1,0:T(8,128)(2,1)} fusion(bf16[320,768]{1,0:T(8,128)(2,1)} %get-tuple-element.130, s32[512]{0:T(512)S(1)} %and_select_fusion), kind=kOutput, calls=%fused_computation.5 | convolution fusion | flops 252215296 | bytes 1280000 | tf_op jit(solution)/shard_map/dot_general | solution.py:20
  129.5 5.2 %fusion.22 = f32[768,3072]{1,0:T(8,128)} fusion(bf16[320,768]{1,0:T(8,128)(2,1)S(1)} %copy-done.25, bf16[320,3072]{1,0:T(8,128)(2,1)S(1)} %copy-done.24), kind=kOutput, calls=%fused_computation.81 | convolution fusion | flops 1509949440 | bytes 11894784 | tf_op jit(solution)/shard_map/dot_general | solution.py:24
  134.7 5.2 %fusion.23 = f32[3072,768]{1,0:T(8,128)} fusion(bf16[320,3072]{1,0:T(8,128)(2,1)S(1)} %copy-done.23, bf16[320,768]{1,0:T(8,128)(2,1)S(1)} %copy-done.30), kind=kOutput, calls=%fused_computation.82 | convolution fusion | flops 1509949440 | bytes 11894784 | tf_op jit(solution)/shard_map/dot_general | solution.py:24
  139.8 6.4 %all-to-all-done.2 = bf16[32,16,768]{2,1,0:T(8,128)(2,1)S(1)} async-done(((bf16[32,16,768]{2,1,0:T(8,128)(2,1)}), bf16[32,16,768]{2,1,0:T(8,128)(2,1)S(1)}, u32[]{:S(2)}, u32[]{:S(2)}) %all-to-all-start.2) | async-done | bytes 786464 | tf_op jit(solution)/shard_map/all_to_all | solution.py:778
  147.2 4.4 %shard_map.210 = (f32[256,768]{1,0:T(8,128)}, bf16[256,768]{1,0:T(8,128)(2,1)}, bf16[128,768]{1,0:T(8,128)(2,1)}, bf16[128,768]{1,0:T(8,128)(2,1)}, bf16[16,768]{1,0:T(8,128)(2,1)}) custom-call(s32[5]{0:T(128)} %stack.23.flags_ref, bf16[512,768]{1,0:T(8,128)(2,1)} %bitcast.61, bf16[256,512]{1,0:T(8,128)(2,1)} %fusion.10.to_tokens_ref, ...), custom_call_target="tpu_custom_call" | custom-call | bytes 1048576 | tf_op jit(solution)/shard_map/pallas_call | solution.py:272
  151.6 1.5 collective-permute-start.19
  156.6 1.8 collective-permute-start.20
  159.1 1.8 collective-permute-start.22
  161.6 6.9 %collective-permute-done.21.refs_2_ = bf16[128,384]{1,0:T(8,128)(2,1)S(1)} collective-permute-done((bf16[128,384]{1,0:T(8,128)(2,1)S(1)}, bf16[128,384]{1,0:T(8,128)(2,1)S(1)}, u32[]{:S(2)}, u32[]{:S(2)}) %collective-permute-start.21) | collective-permute-done | bytes 98336 | tf_op jit(solution)/shard_map/ppermute | solution.py:45
  168.5 3.6 %all-to-all-start.3 = ((bf16[32,16,768]{2,1,0:T(8,128)(2,1)}), bf16[32,16,768]{2,1,0:T(8,128)(2,1)}, u32[]{:S(2)}, u32[]{:S(2)}) async-start(bf16[32,16,768]{2,1,0:T(8,128)(2,1)} %bitcast.20), calls=%async_computation.3 | async-start | bytes 1572864 | tf_op jit(solution)/shard_map/all_to_all | solution.py:778
  172.2 8.9 %shard_map.212 = (bf16[512,384]{1,0:T(8,128)(2,1)}, bf16[2,512,384]{2,1,0:T(8,128)(2,1)}, bf16[2,512,384]{2,1,0:T(8,128)(2,1)}) custom-call(bf16[512,384]{1,0:T(8,128)(2,1)} %get-tuple-element.107.query_ref, bf16[512,768]{1,0:T(8,128)(2,1)} %get-tuple-element.108.key_ref.value_ref, bf16[512,768]{1,0:T(8,128)(2,1)} %get-tuple-element.108.key_ref.value_ref, ...), custom_call_target="tpu_custom_call" | custom-call | flops 20000000000 | bytes 4096 | tf_op jit(solution)/shard_map/pallas_call | solution.py:229
  181.4 2.3 collective-permute-done.23.got_ref
  185.9 4.6 %shard_map.213 = (bf16[512,1152]{1,0:T(8,128)(2,1)S(1)}, f32[384,2048]{1,0:T(8,128)}, bf16[384,2048]{1,0:T(8,128)(2,1)}) custom-call(s32[5]{0:T(128)S(1)} %copy-done.12, bf16[512,768]{1,0:T(8,128)(2,1)S(1)} %copy-done, bf16[512,384]{1,0:T(8,128)(2,1)S(1)} %copy-done.4, bf16[2,512,384]{2,1,0:T(8,128)(2,1)S(1)} %copy-done.1, ...), custom_call_target="tpu_custom_call" | custom-call | bytes 1048576 | tf_op jit(solution)/shard_map/pallas_call | solution.py:272
  191.5 1.5 collective-permute-start.24
  193.2 3.2 %convolution_convert_fusion.2 = bf16[512,768]{1,0:T(8,128)(2,1)S(1)} fusion(bf16[512,1152]{1,0:T(8,128)(2,1)} %copy-done.15, bf16[768,1152]{1,0:T(8,128)(2,1)} %get-tuple-element.158), kind=kOutput, calls=%fused_computation.7 | convolution fusion | flops 906362880 | bytes 3735552 | tf_op jit(solution)/shard_map/dot_general | solution.py:28
  197.3 1.7 collective-permute-start.25
  199.2 1.4 collective-permute-start.30
  200.6 2.0 collective-permute-start.31
  204.4 3.4 %collective-permute-start.27 = (bf16[128,768]{1,0:T(8,128)(2,1)S(1)}, bf16[128,768]{1,0:T(8,128)(2,1)S(1)}, u32[]{:S(2)}, u32[]{:S(2)}) collective-permute-start(bf16[128,768]{1,0:T(8,128)(2,1)S(1)} %get-tuple-element.189), channel_id=1, source_target_pairs={{0,3},{1,2},{2,1},{3,0},{4,7},{5,6},{6,5},{7,4},{8,11},{9,10},{10,... | collective-permute-start | bytes 589832 | tf_op jit(solution)/shard_map/ppermute | solution.py:45
  207.8 2.3 fusion.2
  210.1 7.7 %collective-permute-done.26 = bf16[128,768]{1,0:T(8,128)(2,1)S(1)} collective-permute-done((bf16[128,768]{1,0:T(8,128)(2,1)S(1)}, bf16[128,768]{1,0:T(8,128)(2,1)S(1)}, u32[]{:S(2)}, u32[]{:S(2)}) %collective-permute-start.26) | collective-permute-done | bytes 196640 | tf_op jit(solution)/shard_map/ppermute | solution.py:45
  219.0 4.1 %collective-permute-start.32 = (bf16[24,2048]{1,0:T(8,128)(2,1)S(1)}, bf16[24,2048]{1,0:T(8,128)(2,1)S(1)}, u32[]{:S(2)}, u32[]{:S(2)}) collective-permute-start(bf16[24,2048]{1,0:T(8,128)(2,1)S(1)} %get-tuple-element.188), channel_id=1, source_target_pairs={{0,1},{1,0},{2,3},{3,2},{4,5},{5,4},{6,7},{7,6},{8,9},{9,8},{10,11... | collective-permute-start | bytes 294920 | tf_op jit(solution)/shard_map/ppermute | solution.py:45
  223.0 2.4 %collective-permute-start.34 = (bf16[24,2048]{1,0:T(8,128)(2,1)S(1)}, bf16[24,2048]{1,0:T(8,128)(2,1)S(1)}, u32[]{:S(2)}, u32[]{:S(2)}) collective-permute-start(bf16[24,2048]{1,0:T(8,128)(2,1)S(1)} %get-tuple-element.186), channel_id=1, source_target_pairs={{0,3},{1,2},{2,1},{3,0},{4,7},{5,6},{6,5},{7,4},{8,11},{9,10},{10,... | collective-permute-start | bytes 294920 | tf_op jit(solution)/shard_map/ppermute | solution.py:45
  227.2 6.3 %collective-permute-done.33.two_ref = bf16[24,2048]{1,0:T(8,128)(2,1)S(1)} collective-permute-done((bf16[24,2048]{1,0:T(8,128)(2,1)S(1)}, bf16[24,2048]{1,0:T(8,128)(2,1)S(1)}, u32[]{:S(2)}, u32[]{:S(2)}) %collective-permute-start.33) | collective-permute-done | bytes 98336 | tf_op jit(solution)/shard_map/ppermute | solution.py:45
  233.6 1.4 shard_map.214
  (186 shorter events, 38.3 us)
Async XLA Ops:
  0.7 21.6 %copy-start.37 = (s32[256,1]{0,1:T(1,128)S(1)}, s32[256,1]{0,1:T(1,128)}, u32[]{:S(2)}) copy-start(s32[256,1]{0,1:T(1,128)} %param.22) | copy-start | bytes 3076
  2.9 6.8 %collective-permute-start.4 = (bf16[24,2048]{1,0:T(8,128)(2,1)}, bf16[24,2048]{1,0:T(8,128)(2,1)S(1)}, u32[]{:S(2)}, u32[]{:S(2)}) collective-permute-start(bf16[24,2048]{1,0:T(8,128)(2,1)} %get-tuple-element.97), channel_id=1, source_target_pairs={{0,1},{1,0},{2,3},{3,2},{4,5},{5,4},{6,7},{7,6},{8,9},{9,8},{10,11... | collective-permute-start | bytes 294920 | tf_op jit(solution)/shard_map/ppermute | solution.py:45
  5.9 11.7 %collective-permute-start.6 = (bf16[24,2048]{1,0:T(8,128)(2,1)}, bf16[24,2048]{1,0:T(8,128)(2,1)S(1)}, u32[]{:S(2)}, u32[]{:S(2)}) collective-permute-start(bf16[24,2048]{1,0:T(8,128)(2,1)} %get-tuple-element.97), channel_id=1, source_target_pairs={{0,3},{1,2},{2,1},{3,0},{4,7},{5,6},{6,5},{7,4},{8,11},{9,10},{10,... | collective-permute-start | bytes 294920 | tf_op jit(solution)/shard_map/ppermute | solution.py:45
  8.4 9.2 %collective-permute-start.5 = (bf16[24,2048]{1,0:T(8,128)(2,1)}, bf16[24,2048]{1,0:T(8,128)(2,1)S(1)}, u32[]{:S(2)}, u32[]{:S(2)}) collective-permute-start(bf16[24,2048]{1,0:T(8,128)(2,1)} %get-tuple-element.96), channel_id=1, source_target_pairs={{0,2},{1,3},{2,0},{3,1},{4,6},{5,7},{6,4},{7,5},{8,10},{9,11},{10,... | collective-permute-start | bytes 294920 | tf_op jit(solution)/shard_map/ppermute | solution.py:45
  8.5 14.6 %copy-start.17 = (bf16[256,768]{1,0:T(8,128)(2,1)S(1)}, bf16[256,768]{1,0:T(8,128)(2,1)}, u32[]{:S(2)}) copy-start(bf16[256,768]{1,0:T(8,128)(2,1)} %inputs_ref.1) | copy-start | bytes 1179652
  9.6 13.5 %collective-permute-start = (bf16[128,768]{1,0:T(8,128)(2,1)S(1)}, bf16[128,768]{1,0:T(8,128)(2,1)S(1)}, u32[]{:S(2)}, u32[]{:S(2)}) collective-permute-start(bf16[128,768]{1,0:T(8,128)(2,1)S(1)} %broadcast_select_fusion.4), channel_id=1, source_target_pairs={{0,4},{1,5},{2,6},{3,7},{4,0},{5,1},{6,2},{7,3},{8,12},{9,13},{10,... | collective-permute-start | bytes 589832 | tf_op jit(solution)/shard_map/ppermute | solution.py:45
  18.5 15.0 %copy-start.27 = (bf16[256,768]{1,0:T(8,128)(2,1)S(1)}, bf16[256,768]{1,0:T(8,128)(2,1)}, u32[]{:S(2)}) copy-start(bf16[256,768]{1,0:T(8,128)(2,1)} %cotangent_ref.1) | copy-start | bytes 1179652
  18.7 21.4 %copy-start.26 = (bf16[96,2048]{1,0:T(8,128)(2,1)}, bf16[96,2048]{1,0:T(8,128)(2,1)S(1)}, u32[]{:S(2)}) copy-start(bf16[96,2048]{1,0:T(8,128)(2,1)S(1)} %pad_maximum_fusion.1.refs_0_) | copy-start | bytes 1179652
  18.7 16.2 %collective-permute-start.7 = (bf16[96,2048]{1,0:T(8,128)(2,1)S(1)}, bf16[96,2048]{1,0:T(8,128)(2,1)S(1)}, u32[]{:S(2)}, u32[]{:S(2)}) collective-permute-start(bf16[96,2048]{1,0:T(8,128)(2,1)S(1)} %pad_maximum_fusion.1.refs_0_), channel_id=1, source_target_pairs={{0,8},{1,9},{2,10},{3,11},{4,12},{5,13},{6,14},{7,15},{8,0},{9,1},... | collective-permute-start | bytes 1179656 | tf_op jit(solution)/shard_map/ppermute | solution.py:45
  20.2 18.7 %collective-permute-start.8 = (bf16[96,2048]{1,0:T(8,128)(2,1)S(1)}, bf16[96,2048]{1,0:T(8,128)(2,1)S(1)}, u32[]{:S(2)}, u32[]{:S(2)}) collective-permute-start(bf16[96,2048]{1,0:T(8,128)(2,1)S(1)} %pad_maximum_fusion.1.refs_0_), channel_id=1, source_target_pairs={{0,16},{1,17},{2,18},{3,19},{4,20},{5,21},{6,22},{7,23},{8,24},{9,... | collective-permute-start | bytes 1179656 | tf_op jit(solution)/shard_map/ppermute | solution.py:45
  21.8 17.2 %collective-permute-start.9 = (bf16[96,2048]{1,0:T(8,128)(2,1)S(1)}, bf16[96,2048]{1,0:T(8,128)(2,1)S(1)}, u32[]{:S(2)}, u32[]{:S(2)}) collective-permute-start(bf16[96,2048]{1,0:T(8,128)(2,1)S(1)} %pad_maximum_fusion.1.refs_0_), channel_id=1, source_target_pairs={{0,24},{1,25},{2,26},{3,27},{4,28},{5,29},{6,30},{7,31},{8,16},{9,... | collective-permute-start | bytes 1179656 | tf_op jit(solution)/shard_map/ppermute | solution.py:45
  23.2 10.3 %collective-permute-start.2 = (bf16[128,768]{1,0:T(8,128)(2,1)S(1)}, bf16[128,768]{1,0:T(8,128)(2,1)S(1)}, u32[]{:S(2)}, u32[]{:S(2)}) collective-permute-start(bf16[128,768]{1,0:T(8,128)(2,1)S(1)} %get-tuple-element.193), channel_id=1, source_target_pairs={{0,2},{1,3},{2,0},{3,1},{4,6},{5,7},{6,4},{7,5},{8,10},{9,11},{10,... | collective-permute-start | bytes 589832 | tf_op jit(solution)/shard_map/ppermute | solution.py:45
  23.8 11.0 %collective-permute-start.1 = (bf16[128,768]{1,0:T(8,128)(2,1)S(1)}, bf16[128,768]{1,0:T(8,128)(2,1)S(1)}, u32[]{:S(2)}, u32[]{:S(2)}) collective-permute-start(bf16[128,768]{1,0:T(8,128)(2,1)S(1)} %get-tuple-element.192), channel_id=1, source_target_pairs={{0,1},{1,0},{2,3},{3,2},{4,5},{5,4},{6,7},{7,6},{8,9},{9,8},{10,11... | collective-permute-start | bytes 589832 | tf_op jit(solution)/shard_map/ppermute | solution.py:45
  33.6 6.5 %collective-permute-start.3 = (bf16[128,768]{1,0:T(8,128)(2,1)S(1)}, bf16[128,768]{1,0:T(8,128)(2,1)S(1)}, u32[]{:S(2)}, u32[]{:S(2)}) collective-permute-start(bf16[128,768]{1,0:T(8,128)(2,1)S(1)} %collective-permute-done.2), channel_id=1, source_target_pairs={{0,1},{1,0},{2,3},{3,2},{4,5},{5,4},{6,7},{7,6},{8,9},{9,8},{10,11... | collective-permute-start | bytes 589832 | tf_op jit(solution)/shard_map/ppermute | solution.py:45
  39.0 6.0 %collective-permute-start.10 = (bf16[96,2048]{1,0:T(8,128)(2,1)S(1)}, bf16[96,2048]{1,0:T(8,128)(2,1)S(1)}, u32[]{:S(2)}, u32[]{:S(2)}) collective-permute-start(bf16[96,2048]{1,0:T(8,128)(2,1)S(1)} %pad_maximum_fusion.1.refs_0_), channel_id=1, source_target_pairs={{0,4},{1,5},{2,6},{3,7},{4,0},{5,1},{6,2},{7,3},{8,12},{9,13},{10,... | collective-permute-start | bytes 1179656 | tf_op jit(solution)/shard_map/ppermute | solution.py:45
  39.0 5.9 %collective-permute-start.11 = (bf16[96,2048]{1,0:T(8,128)(2,1)S(1)}, bf16[96,2048]{1,0:T(8,128)(2,1)}, u32[]{:S(2)}, u32[]{:S(2)}) collective-permute-start(bf16[96,2048]{1,0:T(8,128)(2,1)S(1)} %collective-permute-done.7.refs_1_), channel_id=1, source_target_pairs={{0,4},{1,5},{2,6},{3,7},{4,0},{5,1},{6,2},{7,3},{8,12},{9,13},{10,... | collective-permute-start | bytes 1179656 | tf_op jit(solution)/shard_map/ppermute | solution.py:45
  39.5 5.4 %collective-permute-start.12 = (bf16[96,2048]{1,0:T(8,128)(2,1)S(1)}, bf16[96,2048]{1,0:T(8,128)(2,1)}, u32[]{:S(2)}, u32[]{:S(2)}) collective-permute-start(bf16[96,2048]{1,0:T(8,128)(2,1)S(1)} %collective-permute-done.8.refs_2_), channel_id=1, source_target_pairs={{0,4},{1,5},{2,6},{3,7},{4,0},{5,1},{6,2},{7,3},{8,12},{9,13},{10,... | collective-permute-start | bytes 1179656 | tf_op jit(solution)/shard_map/ppermute | solution.py:45
  39.6 5.4 %collective-permute-start.13 = (bf16[96,2048]{1,0:T(8,128)(2,1)S(1)}, bf16[96,2048]{1,0:T(8,128)(2,1)}, u32[]{:S(2)}, u32[]{:S(2)}) collective-permute-start(bf16[96,2048]{1,0:T(8,128)(2,1)S(1)} %collective-permute-done.9.refs_3_), channel_id=1, source_target_pairs={{0,4},{1,5},{2,6},{3,7},{4,0},{5,1},{6,2},{7,3},{8,12},{9,13},{10,... | collective-permute-start | bytes 1179656 | tf_op jit(solution)/shard_map/ppermute | solution.py:45
  40.1 23.2 %all-to-all-start = ((bf16[32,16,768]{2,1,0:T(8,128)(2,1)}), bf16[32,16,768]{2,1,0:T(8,128)(2,1)S(1)}, u32[]{:S(2)}, u32[]{:S(2)}) async-start(bf16[32,16,768]{2,1,0:T(8,128)(2,1)} %bitcast.11), calls=%async_computation | async-start | bytes 1572864 | tf_op jit(solution)/shard_map/all_to_all | solution.py:778
  51.0 2.5 %collective-permute-start.14 = (bf16[512,768]{1,0:T(8,128)(2,1)}, bf16[512,768]{1,0:T(8,128)(2,1)S(1)}, u32[]{:S(2)}, u32[]{:S(2)}) collective-permute-start(bf16[512,768]{1,0:T(8,128)(2,1)} %get-tuple-element.108.key_ref.value_ref), channel_id=1, source_target_pairs={{0,4},{1,5},{2,6},{3,7},{4,0},{5,1},{6,2},{7,3},{8,12},{9,13},{10,... | collective-permute-start | bytes 2359304 | tf_op jit(solution)/shard_map/ppermute | solution.py:45
  54.4 21.4 %copy-start.11 = (s32[5]{0:T(128)S(1)}, s32[5]{0:T(128)}, u32[]{:S(2)}) copy-start(s32[5]{0:T(128)} %stack.23.flags_ref) | copy-start | bytes 64
  63.2 29.1 %copy-start.21 = (bf16[32,16,768]{2,1,0:T(8,128)(2,1)}, bf16[32,16,768]{2,1,0:T(8,128)(2,1)S(1)}, u32[]{:S(2)}) copy-start(bf16[32,16,768]{2,1,0:T(8,128)(2,1)S(1)} %all-to-all-done) | copy-start | bytes 2359300
  63.2 7.4 %collective-permute-start.15 = (bf16[128,384]{1,0:T(8,128)(2,1)}, bf16[128,384]{1,0:T(8,128)(2,1)S(1)}, u32[]{:S(2)}, u32[]{:S(2)}) collective-permute-start(bf16[128,384]{1,0:T(8,128)(2,1)} %get-tuple-element.115.refs_5_), channel_id=1, source_target_pairs={{0,1},{1,0},{2,3},{3,2},{4,5},{5,4},{6,7},{7,6},{8,9},{9,8},{10,11... | collective-permute-start | bytes 294920 | tf_op jit(solution)/shard_map/ppermute | solution.py:45
  66.2 9.7 %collective-permute-start.16 = (bf16[128,384]{1,0:T(8,128)(2,1)}, bf16[128,384]{1,0:T(8,128)(2,1)S(1)}, u32[]{:S(2)}, u32[]{:S(2)}) collective-permute-start(bf16[128,384]{1,0:T(8,128)(2,1)} %get-tuple-element.116.refs_6_), channel_id=1, source_target_pairs={{0,2},{1,3},{2,0},{3,1},{4,6},{5,7},{6,4},{7,5},{8,10},{9,11},{10,... | collective-permute-start | bytes 294920 | tf_op jit(solution)/shard_map/ppermute | solution.py:45
  66.9 8.9 %collective-permute-start.17 = (bf16[128,384]{1,0:T(8,128)(2,1)}, bf16[128,384]{1,0:T(8,128)(2,1)S(1)}, u32[]{:S(2)}, u32[]{:S(2)}) collective-permute-start(bf16[128,384]{1,0:T(8,128)(2,1)} %get-tuple-element.117.refs_7_), channel_id=1, source_target_pairs={{0,3},{1,2},{2,1},{3,0},{4,7},{5,6},{6,5},{7,4},{8,11},{9,10},{10,... | collective-permute-start | bytes 294920 | tf_op jit(solution)/shard_map/ppermute | solution.py:45
  78.0 1.9 collective-permute-start.18
  84.2 23.7 %all-to-all-start.1 = ((bf16[32,16,768]{2,1,0:T(8,128)(2,1)}), bf16[32,16,768]{2,1,0:T(8,128)(2,1)S(1)}, u32[]{:S(2)}, u32[]{:S(2)}) async-start(bf16[32,16,768]{2,1,0:T(8,128)(2,1)} %bitcast.63), calls=%async_computation.1 | async-start | bytes 1572864 | tf_op jit(solution)/shard_map/all_to_all | solution.py:778
  122.3 24.0 %all-to-all-start.2 = ((bf16[32,16,768]{2,1,0:T(8,128)(2,1)}), bf16[32,16,768]{2,1,0:T(8,128)(2,1)S(1)}, u32[]{:S(2)}, u32[]{:S(2)}) async-start(bf16[32,16,768]{2,1,0:T(8,128)(2,1)} %bitcast.64), calls=%async_computation.2 | async-start | bytes 1572864 | tf_op jit(solution)/shard_map/all_to_all | solution.py:778
  151.6 2.7 %collective-permute-start.19 = (bf16[128,768]{1,0:T(8,128)(2,1)}, bf16[128,768]{1,0:T(8,128)(2,1)S(1)}, u32[]{:S(2)}, u32[]{:S(2)}) collective-permute-start(bf16[128,768]{1,0:T(8,128)(2,1)} %get-tuple-element.139), channel_id=1, source_target_pairs={{0,4},{1,5},{2,6},{3,7},{4,0},{5,1},{6,2},{7,3},{8,12},{9,13},{10,... | collective-permute-start | bytes 589832 | tf_op jit(solution)/shard_map/ppermute | solution.py:45
  156.6 5.1 %collective-permute-start.20 = (bf16[128,384]{1,0:T(8,128)(2,1)S(1)}, bf16[128,384]{1,0:T(8,128)(2,1)S(1)}, u32[]{:S(2)}, u32[]{:S(2)}) collective-permute-start(bf16[128,384]{1,0:T(8,128)(2,1)S(1)} %get-tuple-element.140), channel_id=1, source_target_pairs={{0,1},{1,0},{2,3},{3,2},{4,5},{5,4},{6,7},{7,6},{8,9},{9,8},{10,11... | collective-permute-start | bytes 294920 | tf_op jit(solution)/shard_map/ppermute | solution.py:45
  158.4 10.1 %collective-permute-start.21 = (bf16[128,384]{1,0:T(8,128)(2,1)S(1)}, bf16[128,384]{1,0:T(8,128)(2,1)S(1)}, u32[]{:S(2)}, u32[]{:S(2)}) collective-permute-start(bf16[128,384]{1,0:T(8,128)(2,1)S(1)} %get-tuple-element.141), channel_id=1, source_target_pairs={{0,2},{1,3},{2,0},{3,1},{4,6},{5,7},{6,4},{7,5},{8,10},{9,11},{10,... | collective-permute-start | bytes 294920 | tf_op jit(solution)/shard_map/ppermute | solution.py:45
  159.1 9.4 %collective-permute-start.22 = (bf16[128,384]{1,0:T(8,128)(2,1)S(1)}, bf16[128,384]{1,0:T(8,128)(2,1)S(1)}, u32[]{:S(2)}, u32[]{:S(2)}) collective-permute-start(bf16[128,384]{1,0:T(8,128)(2,1)S(1)} %get-tuple-element.142), channel_id=1, source_target_pairs={{0,3},{1,2},{2,1},{3,0},{4,7},{5,6},{6,5},{7,4},{8,11},{9,10},{10,... | collective-permute-start | bytes 294920 | tf_op jit(solution)/shard_map/ppermute | solution.py:45
  168.5 23.0 %all-to-all-start.3 = ((bf16[32,16,768]{2,1,0:T(8,128)(2,1)}), bf16[32,16,768]{2,1,0:T(8,128)(2,1)}, u32[]{:S(2)}, u32[]{:S(2)}) async-start(bf16[32,16,768]{2,1,0:T(8,128)(2,1)} %bitcast.20), calls=%async_computation.3 | async-start | bytes 1572864 | tf_op jit(solution)/shard_map/all_to_all | solution.py:778
  172.2 11.6 %copy-start = (bf16[512,768]{1,0:T(8,128)(2,1)S(1)}, bf16[512,768]{1,0:T(8,128)(2,1)}, u32[]{:S(2)}) copy-start(bf16[512,768]{1,0:T(8,128)(2,1)} %fusion.1.normed_ref) | copy-start | bytes 2359300
  172.2 11.5 %copy-start.2 = (bf16[256,768]{1,0:T(8,128)(2,1)S(1)}, bf16[256,768]{1,0:T(8,128)(2,1)}, u32[]{:S(2)}) copy-start(bf16[256,768]{1,0:T(8,128)(2,1)} %get-tuple-element.154.mixed_ref) | copy-start | bytes 1179652
  172.2 11.5 %copy-start.3 = (bf16[256,768]{1,0:T(8,128)(2,1)S(1)}, bf16[256,768]{1,0:T(8,128)(2,1)}, u32[]{:S(2)}) copy-start(bf16[256,768]{1,0:T(8,128)(2,1)} %get-tuple-element.155.branch_ref) | copy-start | bytes 1179652
  181.1 2.6 %collective-permute-start.23 = (bf16[2,512,384]{2,1,0:T(8,128)(2,1)}, bf16[2,512,384]{2,1,0:T(8,128)(2,1)S(1)}, u32[]{:S(2)}, u32[]{:S(2)}) collective-permute-start(bf16[2,512,384]{2,1,0:T(8,128)(2,1)} %get-tuple-element.153), channel_id=1, source_target_pairs={{0,4},{1,5},{2,6},{3,7},{4,0},{5,1},{6,2},{7,3},{8,12},{9,13},{10,... | collective-permute-start | bytes 2359304 | tf_op jit(solution)/shard_map/ppermute | solution.py:45
  191.5 4.9 %collective-permute-start.24 = (bf16[384,2048]{1,0:T(8,128)(2,1)}, bf16[384,2048]{1,0:T(8,128)(2,1)S(1)}, u32[]{:S(2)}, u32[]{:S(2)}) collective-permute-start(bf16[384,2048]{1,0:T(8,128)(2,1)} %get-tuple-element.161), channel_id=1, source_target_pairs={{0,4},{1,5},{2,6},{3,7},{4,0},{5,1},{6,2},{7,3},{8,12},{9,13},{10,... | collective-permute-start | bytes 4718600 | tf_op jit(solution)/shard_map/ppermute | solution.py:45
  197.3 7.1 %collective-permute-start.25 = (bf16[128,768]{1,0:T(8,128)(2,1)S(1)}, bf16[128,768]{1,0:T(8,128)(2,1)S(1)}, u32[]{:S(2)}, u32[]{:S(2)}) collective-permute-start(bf16[128,768]{1,0:T(8,128)(2,1)S(1)} %get-tuple-element.191), channel_id=1, source_target_pairs={{0,1},{1,0},{2,3},{3,2},{4,5},{5,4},{6,7},{7,6},{8,9},{9,8},{10,11... | collective-permute-start | bytes 589832 | tf_op jit(solution)/shard_map/ppermute | solution.py:45
  199.1 18.9 %collective-permute-start.29 = (bf16[96,2048]{1,0:T(8,128)(2,1)S(1)}, bf16[96,2048]{1,0:T(8,128)(2,1)S(1)}, u32[]{:S(2)}, u32[]{:S(2)}) collective-permute-start(bf16[96,2048]{1,0:T(8,128)(2,1)S(1)} %get-tuple-element.185), channel_id=1, source_target_pairs={{0,8},{1,9},{2,10},{3,11},{4,12},{5,13},{6,14},{7,15},{8,0},{9,1},... | collective-permute-start | bytes 1179656 | tf_op jit(solution)/shard_map/ppermute | solution.py:45
  199.2 19.5 %collective-permute-start.30 = (bf16[96,2048]{1,0:T(8,128)(2,1)S(1)}, bf16[96,2048]{1,0:T(8,128)(2,1)S(1)}, u32[]{:S(2)}, u32[]{:S(2)}) collective-permute-start(bf16[96,2048]{1,0:T(8,128)(2,1)S(1)} %get-tuple-element.184), channel_id=1, source_target_pairs={{0,16},{1,17},{2,18},{3,19},{4,20},{5,21},{6,22},{7,23},{8,24},{9,... | collective-permute-start | bytes 1179656 | tf_op jit(solution)/shard_map/ppermute | solution.py:45
  200.6 18.1 %collective-permute-start.31 = (bf16[96,2048]{1,0:T(8,128)(2,1)S(1)}, bf16[96,2048]{1,0:T(8,128)(2,1)S(1)}, u32[]{:S(2)}, u32[]{:S(2)}) collective-permute-start(bf16[96,2048]{1,0:T(8,128)(2,1)S(1)} %get-tuple-element.183), channel_id=1, source_target_pairs={{0,24},{1,25},{2,26},{3,27},{4,28},{5,29},{6,30},{7,31},{8,16},{9,... | collective-permute-start | bytes 1179656 | tf_op jit(solution)/shard_map/ppermute | solution.py:45
  202.7 15.1 %collective-permute-start.26 = (bf16[128,768]{1,0:T(8,128)(2,1)S(1)}, bf16[128,768]{1,0:T(8,128)(2,1)S(1)}, u32[]{:S(2)}, u32[]{:S(2)}) collective-permute-start(bf16[128,768]{1,0:T(8,128)(2,1)S(1)} %get-tuple-element.190), channel_id=1, source_target_pairs={{0,2},{1,3},{2,0},{3,1},{4,6},{5,7},{6,4},{7,5},{8,10},{9,11},{10,... | collective-permute-start | bytes 589832 | tf_op jit(solution)/shard_map/ppermute | solution.py:45
  204.4 13.4 %collective-permute-start.27 = (bf16[128,768]{1,0:T(8,128)(2,1)S(1)}, bf16[128,768]{1,0:T(8,128)(2,1)S(1)}, u32[]{:S(2)}, u32[]{:S(2)}) collective-permute-start(bf16[128,768]{1,0:T(8,128)(2,1)S(1)} %get-tuple-element.189), channel_id=1, source_target_pairs={{0,3},{1,2},{2,1},{3,0},{4,7},{5,6},{6,5},{7,4},{8,11},{9,10},{10,... | collective-permute-start | bytes 589832 | tf_op jit(solution)/shard_map/ppermute | solution.py:45
  217.9 7.6 %collective-permute-start.28 = (bf16[128,768]{1,0:T(8,128)(2,1)S(1)}, bf16[128,768]{1,0:T(8,128)(2,1)S(1)}, u32[]{:S(2)}, u32[]{:S(2)}) collective-permute-start(bf16[128,768]{1,0:T(8,128)(2,1)S(1)} %broadcast_select_fusion.6), channel_id=1, source_target_pairs={{0,4},{1,5},{2,6},{3,7},{4,0},{5,1},{6,2},{7,3},{8,12},{9,13},{10,... | collective-permute-start | bytes 589832 | tf_op jit(solution)/shard_map/ppermute | solution.py:45
  219.0 8.2 %collective-permute-start.32 = (bf16[24,2048]{1,0:T(8,128)(2,1)S(1)}, bf16[24,2048]{1,0:T(8,128)(2,1)S(1)}, u32[]{:S(2)}, u32[]{:S(2)}) collective-permute-start(bf16[24,2048]{1,0:T(8,128)(2,1)S(1)} %get-tuple-element.188), channel_id=1, source_target_pairs={{0,1},{1,0},{2,3},{3,2},{4,5},{5,4},{6,7},{7,6},{8,9},{9,8},{10,11... | collective-permute-start | bytes 294920 | tf_op jit(solution)/shard_map/ppermute | solution.py:45
  223.0 10.5 %collective-permute-start.33 = (bf16[24,2048]{1,0:T(8,128)(2,1)S(1)}, bf16[24,2048]{1,0:T(8,128)(2,1)S(1)}, u32[]{:S(2)}, u32[]{:S(2)}) collective-permute-start(bf16[24,2048]{1,0:T(8,128)(2,1)S(1)} %get-tuple-element.187), channel_id=1, source_target_pairs={{0,2},{1,3},{2,0},{3,1},{4,6},{5,7},{6,4},{7,5},{8,10},{9,11},{10,... | collective-permute-start | bytes 294920 | tf_op jit(solution)/shard_map/ppermute | solution.py:45
  223.0 10.5 %collective-permute-start.34 = (bf16[24,2048]{1,0:T(8,128)(2,1)S(1)}, bf16[24,2048]{1,0:T(8,128)(2,1)S(1)}, u32[]{:S(2)}, u32[]{:S(2)}) collective-permute-start(bf16[24,2048]{1,0:T(8,128)(2,1)S(1)} %get-tuple-element.186), channel_id=1, source_target_pairs={{0,3},{1,2},{2,1},{3,0},{4,7},{5,6},{6,5},{7,4},{8,11},{9,10},{10,... | collective-permute-start | bytes 294920 | tf_op jit(solution)/shard_map/ppermute | solution.py:45
  (33 other events, 153.6 us)

commit v2 on v1

--- a/solution.py
+++ b/solution.py
@@ -415,16 +415,14 @@
 
 def project_kernel(count, flags_ref, normed_ref, *refs):
     own_refs, other_refs = refs[:count], refs[count : 2 * count]
-    query_ref, pair_ref, weight_ref, extra_ref = refs[2 * count :]
-    columns = weight_ref.shape[1]
+    query_ref, pair_ref, weight_ref = refs[2 * count :]
     rows = own_refs[0].shape[0]
     core = flags_ref[CORE]
     for m in range(count):
         place = 2 * (flags_ref[PLACE] ^ m)
         for index, ref in ((place + core, own_refs[m]), (place + 1 - core, other_refs[m])):
             place_rows = pl.ds(pl.multiple_of(index * rows, 16), rows)
-            weight_ref[place_rows, :] = ref[:, :columns]
-            extra_ref[place_rows, :] = ref[:, columns:]
+            weight_ref[place_rows, :] = ref[...]
     projected = dot(normed_ref[...], weight_ref[...]).astype(BF)
     query_ref[...] = projected[:, : query_ref.shape[1]]
     pair_ref[...] = projected[:, query_ref.shape[1] :]
@@ -438,10 +436,32 @@
         low_shape(rows, width // 2),
         low_shape(rows, width),
         low_shape(width, columns),
-        low_shape(width, own[0].shape[1] - columns),
     ]
     kernel = functools.partial(project_kernel, count)
     return one_step(kernel, flags, [normed, *own, *other], shapes)
+
+
+def assemble_kernel(lane, flags_ref, *refs):
+    *own_refs, other_ref, full_ref, row_ref = refs
+    rows = own_refs[0].shape[0]
+    width = full_ref.shape[0]
+    core = flags_ref[CORE]
+    for m, own_ref in enumerate(own_refs):
+        place = 2 * (flags_ref[PLACE] ^ m)
+        full_ref[pl.ds(pl.multiple_of((place + core) * rows, 16), rows), :] = own_ref[...]
+        full_ref[pl.ds(pl.multiple_of((place + 1 - core) * rows, 16), rows), :] = other_ref[
+            m * rows : (m + 1) * rows, :
+        ]
+    start = width + lane // 128 * 128
+    block = full_ref[:, start : start + 128].astype(F32).T
+    row_ref[...] = block[lane % 128 : lane % 128 + 1]
+
+
+def assemble(flags, operands, lane):
+    columns = operands[0].shape[1]
+    width = 2 * operands[-1].shape[0]
+    shapes = [low_shape(width, columns), wide_shape(1, width)]
+    return one_step(functools.partial(assemble_kernel, lane), flags, operands, shapes)
 
 
 def mixed_route_kernel(flags_ref, zero_ref, one_ref, two_ref, three_ref, mine_ref, sent_ref):
@@ -822,7 +842,8 @@
     near_first = links.swap_level(near, 1)
     far_first = links.swap_level(far, 2)
     far_second = links.swap_level(far_first, 1)
-    own_blocks = gather_groups(links, level_block)
+    level_weights = level_block[:, : 3 * half_width]
+    own_blocks = gather_groups(links, level_weights)
     chosen = gate(routes, level_block)[:, 0]
     picked = (chosen[:, None] == jnp.arange(experts, dtype=jnp.int32)[None, :]).astype(jnp.int32)
     rank = jnp.sum((jnp.cumsum(picked, axis=0) - picked) * picked, axis=1)
@@ -839,21 +860,32 @@
     normed_work = (
         source * lax.rsqrt(jnp.mean(source * source, axis=-1, keepdims=True) + EPSILON)
     ).astype(BF)
+    own_extra = gather_groups(links, gate(level_block[:, 3 * half_width :], *own_blocks))
     if level_rows % 16 == 0:
-        queries, pair, weights, full_extra = project(flags, normed_work, own_blocks, other_blocks)
+        queries, pair, weights = project(flags, normed_work, own_blocks, other_blocks)
     else:
-        full = in_order(links, own_blocks, other_blocks)
-        weights, full_extra = full[:, : 3 * half_width], full[:, 3 * half_width :]
+        weights = in_order(links, own_blocks, other_blocks)
         projected = dot(normed_work, weights).astype(BF)
         queries, pair = projected[:, :half_width], projected[:, half_width:]
     pair_far = links.swap_core(pair)
-    cot_arrived = all_to_all(gate(cot_slots, far_second)).reshape(-1, width)
+    cot_arrived = all_to_all(gate(cot_slots, *own_blocks)).reshape(-1, width)
     *mixed_parts, attention_weights, inverse = attention_forward(queries, pair, pair_far)
-    mixed_parts = tie(*mixed_parts, cot_arrived)[:-1]
-
-    back = tie(*[links.swap_level(mixed_parts[b], b) for b in (1, 2, 3)])
+    mixed_parts = tie(*mixed_parts, cot_arrived, *own_extra)[:4]
+
+    own_extra = tie(*own_extra, *mixed_parts)[: len(own_extra)]
+    other_extra = links.swap_core(jnp.concatenate(own_extra, axis=0))
+    if level_rows % 16 == 0:
+        full_extra, gain_two = assemble(flags, [*own_extra, other_extra], 2 * experts)
+    else:
+        other_parts = [
+            other_extra[m * level_rows : (m + 1) * level_rows] for m in range(len(own_extra))
+        ]
+        full_extra = in_order(links, own_extra, other_parts)
+        gain_two = full_extra[:, width + 2 * experts].astype(F32)[None]
     full_router = full_extra[:, width : width + experts]
-    gain_two = full_extra[:, width + 2 * experts].astype(F32)[None]
+    last_part = gate(mixed_parts[3], gain_two)
+    back = [links.swap_level(mixed_parts[1], 1), links.swap_level(mixed_parts[2], 2)]
+    back = tie(*back, links.swap_level(last_part, 3))
     tallies = full_extra[::own_rows, width + experts : width + 2 * experts].astype(F32)
     mine_only = (jnp.arange(experts, dtype=jnp.int32) == device).astype(F32)[None, :]
     counts = jnp.sum(tallies * mine_only, axis=1).astype(jnp.int32)

time: 236 us -> 232 us (0.983)
  waiting for transfers between devices: 69.6 us -> 60.5 us
  starting transfers between devices: 58.5 us -> 61.6 us
    ppermute x35 -> x39, waiting for transfers between devices: 52.6 us -> 44.5 us  [permute(): return lax.ppermute(array, AXES, pairs)]
    ppermute x35 -> x39, starting transfers between devices: 42.7 us -> 46 us  [permute(): return lax.ppermute(array, AXES, pairs)]
    pallas_call x8 -> x9, Pallas kernels: 22.2 us -> 24.2 us  [one_step(): pl.pallas_call(kernel, grid=(1,), in_specs=[FLAGS] + [whole(operand.shape...]
    unnamed x84 -> x104, local copies, waits for them, and re-layouts: 10.5 us -> 10.6 us
  transfers between devices with their start and end apart: 39 -> 43, of which waited for: 17 -> 19; matrix products, arithmetic and copies ran while one was open for 15% -> 15% of each run, Pallas kernels for 14% -> 15%
where the time goes in v2:
time: 232 us; the launch traced here: 231 us
  starting transfers between devices  61.6 us (27%)
  waiting for transfers between devices  60.5 us (26%)
  Pallas kernels  60.4 us (26%)
  matrix products  19.9 us (9%)
  local copies, waits for them, and re-layouts  14.6 us (6%)
  other arithmetic  13 us (6%)
    ppermute x39, starting transfers between devices, permute(): return lax.ppermute(array, AXES, pairs)  46 us
    ppermute x39, waiting for transfers between devices, permute(): return lax.ppermute(array, AXES, pairs)  44.5 us
    pallas_call x9, Pallas kernels, one_step(): pl.pallas_call(kernel, grid=(1,), in_specs=[FLAGS] + [whole(operand.shape...  24.2 us
    all_to_all x4, waiting for transfers between devices, all_to_all(): return lax.all_to_all(array, AXES, split_axis=0, concat_axis=0, tiled=True)  16 us
    all_to_all x4, starting transfers between devices, all_to_all(): return lax.all_to_all(array, AXES, split_axis=0, concat_axis=0, tiled=True)  15.6 us
    pallas_call x1, Pallas kernels, expert_layer(): pl.pallas_call(expert_kernel, grid=(hidden_width // TILE,), in_specs=[FLA...  13.5 us
    unnamed x104, local copies, waits for them, and re-layouts  10.6 us
    dot_general x3, matrix products, dot_tn(): lax.dot_general(left, right, (((0,), (0,)), ((), ())), preferred_element_...  10.6 us
  transfers between devices with their start and end apart: 43, of which 19 were waited for; matrix products, arithmetic and copies ran while one was open for 15% of the time, Pallas kernels for 15%

profile of v2, /device:TPU:0, one launch (start us, length us, event | category | flops | bytes accessed | tf_op | source)
XLA Modules:
  0.0 231.3 jit_solution(6877564308228827538)
XLA Ops:
  1.3 1.7 shard_map.203
  2.9 3.0 %collective-permute-start.4 = (bf16[24,2048]{1,0:T(8,128)(2,1)}, bf16[24,2048]{1,0:T(8,128)(2,1)S(1)}, u32[]{:S(2)}, u32[]{:S(2)}) collective-permute-start(bf16[24,2048]{1,0:T(8,128)(2,1)} %get-tuple-element.104), channel_id=1, source_target_pairs={{0,1},{1,0},{2,3},{3,2},{4,5},{5,4},{6,7},{7,6},{8,9},{9,8},{10,11... | collective-permute-start | bytes 294920 | tf_op jit(solution)/shard_map/ppermute | solution.py:45
  5.9 2.5 %collective-permute-start.6 = (bf16[24,2048]{1,0:T(8,128)(2,1)}, bf16[24,2048]{1,0:T(8,128)(2,1)S(1)}, u32[]{:S(2)}, u32[]{:S(2)}) collective-permute-start(bf16[24,2048]{1,0:T(8,128)(2,1)} %get-tuple-element.104), channel_id=1, source_target_pairs={{0,3},{1,2},{2,1},{3,0},{4,7},{5,6},{6,5},{7,4},{8,11},{9,10},{10,... | collective-permute-start | bytes 294920 | tf_op jit(solution)/shard_map/ppermute | solution.py:45
  12.6 5.0 %collective-permute-done.5 = bf16[24,2048]{1,0:T(8,128)(2,1)S(1)} collective-permute-done((bf16[24,2048]{1,0:T(8,128)(2,1)}, bf16[24,2048]{1,0:T(8,128)(2,1)S(1)}, u32[]{:S(2)}, u32[]{:S(2)}) %collective-permute-start.5) | collective-permute-done | bytes 98336 | tf_op jit(solution)/shard_map/ppermute | solution.py:45
  19.3 1.6 collective-permute-start.7
  20.9 1.5 collective-permute-start.8
  22.9 2.6 %collective-permute-start.1 = (bf16[128,768]{1,0:T(8,128)(2,1)S(1)}, bf16[128,768]{1,0:T(8,128)(2,1)S(1)}, u32[]{:S(2)}, u32[]{:S(2)}) collective-permute-start(bf16[128,768]{1,0:T(8,128)(2,1)S(1)} %get-tuple-element.206), channel_id=1, source_target_pairs={{0,1},{1,0},{2,3},{3,2},{4,5},{5,4},{6,7},{7,6},{8,9},{9,8},{10,11... | collective-permute-start | bytes 589832 | tf_op jit(solution)/shard_map/ppermute | solution.py:45
  25.5 4.4 %collective-permute-done.2 = bf16[128,768]{1,0:T(8,128)(2,1)S(1)} collective-permute-done((bf16[128,768]{1,0:T(8,128)(2,1)S(1)}, bf16[128,768]{1,0:T(8,128)(2,1)S(1)}, u32[]{:S(2)}, u32[]{:S(2)}) %collective-permute-start.2) | collective-permute-done | bytes 196640 | tf_op jit(solution)/shard_map/ppermute | solution.py:45
  34.0 3.8 %all-to-all-start = ((bf16[32,16,768]{2,1,0:T(8,128)(2,1)}), bf16[32,16,768]{2,1,0:T(8,128)(2,1)S(1)}, u32[]{:S(2)}, u32[]{:S(2)}) async-start(bf16[32,16,768]{2,1,0:T(8,128)(2,1)} %bitcast.11), calls=%async_computation | async-start | bytes 1572864 | tf_op jit(solution)/shard_map/all_to_all | solution.py:798
  40.0 4.6 %shard_map.204 = (bf16[512,384]{1,0:T(8,128)(2,1)}, bf16[512,768]{1,0:T(8,128)(2,1)}, bf16[768,1152]{1,0:T(8,128)(2,1)}) custom-call(s32[5]{0:T(128)} %stack.23.flags_ref, bf16[512,768]{1,0:T(8,128)(2,1)} %fusion.1.normed_ref, bf16[96,1152]{1,0:T(8,128)(2,1)} %copy-done.28, bf16[96,1152]{1,0:T(8,128)(2,1)} %copy-done.36, bf16[96,1152]{1,0:T(8,128)(2,1)} %copy-done.37, ...), custom_call_target="tpu_custom_call" | custom-call | bytes 1048576 | tf_op jit(solution)/shard_map/pallas_call | solution.py:272
  44.9 1.7 collective-permute-start.15
  46.6 1.5 collective-permute-start.16
  49.4 7.8 %shard_map.205 = (bf16[128,384]{1,0:T(8,128)(2,1)}, bf16[128,384]{1,0:T(8,128)(2,1)}, bf16[128,384]{1,0:T(8,128)(2,1)}, bf16[128,384]{1,0:T(8,128)(2,1)}, bf16[6...) custom-call(bf16[512,384]{1,0:T(8,128)(2,1)} %get-tuple-element.114.query_ref, ...), custom_call_target="tpu_custom_call" | custom-call | flops 2000000000 | bytes 4096 | tf_op jit(solution)/shard_map/pallas_call | solution.py:178
  60.2 2.5 %collective-permute-start.18 = (bf16[128,384]{1,0:T(8,128)(2,1)S(1)}, bf16[128,384]{1,0:T(8,128)(2,1)S(1)}, u32[]{:S(2)}, u32[]{:S(2)}) collective-permute-start(bf16[128,384]{1,0:T(8,128)(2,1)S(1)} %copy-done.46), channel_id=1, source_target_pairs={{0,1},{1,0},{2,3},{3,2},{4,5},{5,4},{6,7},{7,6},{8,9},{9,8},{10,11... | collective-permute-start | bytes 294920 | tf_op jit(solution)/shard_map/ppermute | solution.py:45
  64.8 2.7 %shard_map.206 = (bf16[768,896]{1,0:T(8,128)(2,1)}, f32[1,768]{1,0:T(1,128)}) custom-call(s32[5]{0:T(128)} %stack.23.flags_ref, bf16[96,896]{1,0:T(8,128)(2,1)} %copy-done.27, bf16[96,896]{1,0:T(8,128)(2,1)} %copy-done.32, bf16[96,896]{1,0:T(8,128)(2,1)} %copy-done.33, bf16[96,896]{1,0:T(8,128)(2,1)} %copy-done.34, bf16[384,896]{1,0:T(8,128)(2,1)} %copy-done.31), custom_call_target="tpu_custom_call" | custom-call | bytes 1048576 | tf_op jit(solution)/shard_map/pallas_call | solution.py:272
  70.5 3.5 %collective-permute-done.21.three_ref = bf16[128,384]{1,0:T(8,128)(2,1)S(1)} collective-permute-done((bf16[128,384]{1,0:T(8,128)(2,1)S(1)}, bf16[128,384]{1,0:T(8,128)(2,1)S(1)}, u32[]{:S(2)}, u32[]{:S(2)}) %collective-permute-start.21) | collective-permute-done | bytes 98336 | tf_op jit(solution)/shard_map/ppermute | solution.py:45
  77.4 3.6 %shard_map.208 = (bf16[256,768]{1,0:T(8,128)(2,1)}, f32[256,768]{1,0:T(8,128)}, bf16[512,768]{1,0:T(8,128)(2,1)}) custom-call(s32[5]{0:T(128)} %stack.23.flags_ref, bf16[128,768]{1,0:T(8,128)(2,1)} %copy-done.5, bf16[128,768]{1,0:T(8,128)(2,1)} %copy-done.42, bf16[256,768]{1,0:T(8,128)(2,1)} %inputs_ref.1, bf16[768,896]{1,0:T(8,128)(2,1)} %get-tuple-element.137.weight_ref, ...), custom_call_target="tpu_custom_call" | custom-call | bytes 1048576 | tf_op jit(solution)/shard_map/pallas_call | solution.py:272
  81.0 3.8 %all-to-all-start.1 = ((bf16[32,16,768]{2,1,0:T(8,128)(2,1)}), bf16[32,16,768]{2,1,0:T(8,128)(2,1)S(1)}, u32[]{:S(2)}, u32[]{:S(2)}) async-start(bf16[32,16,768]{2,1,0:T(8,128)(2,1)} %bitcast.63), calls=%async_computation.1 | async-start | bytes 1572864 | tf_op jit(solution)/shard_map/all_to_all | solution.py:798
  84.8 1.6 slice.64.router_ref
  88.7 6.0 %shard_map.209 = (bf16[320,768]{1,0:T(8,128)(2,1)}, bf16[320,3072]{1,0:T(8,128)(2,1)}) custom-call(bf16[512,768]{1,0:T(8,128)(2,1)} %bitcast.60, bf16[320,512]{1,0:T(8,128)(2,1)} %fusion.9.compact_ref, bf16[1,3072,768]{2,1,0:T(8,128)(2,1)} %weight_out_ref.3), custom_call_target="tpu_custom_call" | custom-call | flops 1509949440 | bytes 9437184 | tf_op jit(solution)/shard_map/pallas_call | solution.py:558
  94.8 9.5 %all-to-all-done.1 = bf16[32,16,768]{2,1,0:T(8,128)(2,1)S(1)} async-done(((bf16[32,16,768]{2,1,0:T(8,128)(2,1)}), bf16[32,16,768]{2,1,0:T(8,128)(2,1)S(1)}, u32[]{:S(2)}, u32[]{:S(2)}) %all-to-all-start.1) | async-done | bytes 786464 | tf_op jit(solution)/shard_map/all_to_all | solution.py:798
  105.2 13.5 %shard_map.210 = (bf16[320,768]{1,0:T(8,128)(2,1)}, bf16[320,768]{1,0:T(8,128)(2,1)}, bf16[320,3072]{1,0:T(8,128)(2,1)}, bf16[320,3072]{1,0:T(8,128)(2,1)}, bf16...) custom-call(s32[5]{0:T(128)} %stack.23.flags_ref, bf16[512,768]{1,0:T(8,128)(2,1)} %bitcast.62, ...), custom_call_target="tpu_custom_call" | custom-call | flops 6039797760 | bytes 18874368 | tf_op jit(solution)/shard_map/pallas_call | solution.py:642
  118.7 4.4 %all-to-all-start.2 = ((bf16[32,16,768]{2,1,0:T(8,128)(2,1)}), bf16[32,16,768]{2,1,0:T(8,128)(2,1)S(1)}, u32[]{:S(2)}, u32[]{:S(2)}) async-start(bf16[32,16,768]{2,1,0:T(8,128)(2,1)} %bitcast.64), calls=%async_computation.2 | async-start | bytes 1572864 | tf_op jit(solution)/shard_map/all_to_all | solution.py:798
  123.3 2.5 %convolution_convert_fusion = bf16[512,768]{1,0:T(8,128)(2,1)} fusion(bf16[320,768]{1,0:T(8,128)(2,1)} %get-tuple-element.144, s32[512]{0:T(512)S(1)} %and_select_fusion), kind=kOutput, calls=%fused_computation.5 | convolution fusion | flops 252215296 | bytes 1280000 | tf_op jit(solution)/shard_map/dot_general | solution.py:20
  125.9 5.2 %fusion.24 = f32[768,3072]{1,0:T(8,128)} fusion(bf16[320,768]{1,0:T(8,128)(2,1)S(1)} %copy-done.25, bf16[320,3072]{1,0:T(8,128)(2,1)S(1)} %copy-done.24), kind=kOutput, calls=%fused_computation.87 | convolution fusion | flops 1509949440 | bytes 11894784 | tf_op jit(solution)/shard_map/dot_general | solution.py:24
  131.0 5.2 %fusion.25 = f32[3072,768]{1,0:T(8,128)} fusion(bf16[320,3072]{1,0:T(8,128)(2,1)S(1)} %copy-done.23, bf16[320,768]{1,0:T(8,128)(2,1)S(1)} %copy-done.35), kind=kOutput, calls=%fused_computation.88 | convolution fusion | flops 1509949440 | bytes 11894784 | tf_op jit(solution)/shard_map/dot_general | solution.py:24
  136.2 6.4 %all-to-all-done.2 = bf16[32,16,768]{2,1,0:T(8,128)(2,1)S(1)} async-done(((bf16[32,16,768]{2,1,0:T(8,128)(2,1)}), bf16[32,16,768]{2,1,0:T(8,128)(2,1)S(1)}, u32[]{:S(2)}, u32[]{:S(2)}) %all-to-all-start.2) | async-done | bytes 786464 | tf_op jit(solution)/shard_map/all_to_all | solution.py:798
  143.6 4.5 %shard_map.211 = (f32[256,768]{1,0:T(8,128)}, bf16[256,768]{1,0:T(8,128)(2,1)}, bf16[128,768]{1,0:T(8,128)(2,1)}, bf16[128,768]{1,0:T(8,128)(2,1)}, bf16[16,768]{1,0:T(8,128)(2,1)}) custom-call(s32[5]{0:T(128)} %stack.23.flags_ref, bf16[512,768]{1,0:T(8,128)(2,1)} %bitcast.61, bf16[256,512]{1,0:T(8,128)(2,1)} %fusion.10.to_tokens_ref, ...), custom_call_target="tpu_custom_call" | custom-call | bytes 1048576 | tf_op jit(solution)/shard_map/pallas_call | solution.py:272
  148.1 1.5 collective-permute-start.23
  153.0 1.8 collective-permute-start.24
  155.6 1.8 collective-permute-start.26
  158.1 6.9 %collective-permute-done.25.refs_2_ = bf16[128,384]{1,0:T(8,128)(2,1)S(1)} collective-permute-done((bf16[128,384]{1,0:T(8,128)(2,1)S(1)}, bf16[128,384]{1,0:T(8,128)(2,1)S(1)}, u32[]{:S(2)}, u32[]{:S(2)}) %collective-permute-start.25) | collective-permute-done | bytes 98336 | tf_op jit(solution)/shard_map/ppermute | solution.py:45
  164.9 3.6 %all-to-all-start.3 = ((bf16[32,16,768]{2,1,0:T(8,128)(2,1)}), bf16[32,16,768]{2,1,0:T(8,128)(2,1)}, u32[]{:S(2)}, u32[]{:S(2)}) async-start(bf16[32,16,768]{2,1,0:T(8,128)(2,1)} %bitcast.20), calls=%async_computation.3 | async-start | bytes 1572864 | tf_op jit(solution)/shard_map/all_to_all | solution.py:798
  168.6 8.9 %shard_map.213 = (bf16[512,384]{1,0:T(8,128)(2,1)}, bf16[2,512,384]{2,1,0:T(8,128)(2,1)}, bf16[2,512,384]{2,1,0:T(8,128)(2,1)}) custom-call(bf16[512,384]{1,0:T(8,128)(2,1)} %get-tuple-element.114.query_ref, bf16[512,768]{1,0:T(8,128)(2,1)} %get-tuple-element.115.key_ref.value_ref, bf16[512,768]{1,0:T(8,128)(2,1)} %get-tuple-element.115.key_ref.value_ref, ...), custom_call_target="tpu_custom_call" | custom-call | flops 20000000000 | bytes 4096 | tf_op jit(solution)/shard_map/pallas_call | solution.py:229
  177.8 2.3 %collective-permute-done.27.got_ref = bf16[2,512,384]{2,1,0:T(8,128)(2,1)S(1)} collective-permute-done((bf16[2,512,384]{2,1,0:T(8,128)(2,1)}, bf16[2,512,384]{2,1,0:T(8,128)(2,1)S(1)}, u32[]{:S(2)}, u32[]{:S(2)}) %collective-permute-start.27) | collective-permute-done | bytes 786464 | tf_op jit(solution)/shard_map/ppermute | solution.py:45
  182.2 4.6 %shard_map.214 = (bf16[512,1152]{1,0:T(8,128)(2,1)S(1)}, f32[384,2048]{1,0:T(8,128)}, bf16[384,2048]{1,0:T(8,128)(2,1)}) custom-call(s32[5]{0:T(128)S(1)} %copy-done.12, bf16[512,768]{1,0:T(8,128)(2,1)S(1)} %copy-done, bf16[512,384]{1,0:T(8,128)(2,1)S(1)} %copy-done.4, bf16[2,512,384]{2,1,0:T(8,128)(2,1)S(1)} %copy-done.1, ...), custom_call_target="tpu_custom_call" | custom-call | bytes 1048576 | tf_op jit(solution)/shard_map/pallas_call | solution.py:272
  187.9 1.5 collective-permute-start.28
  189.6 3.2 %convolution_convert_fusion.2 = bf16[512,768]{1,0:T(8,128)(2,1)S(1)} fusion(bf16[512,1152]{1,0:T(8,128)(2,1)} %copy-done.15, bf16[768,1152]{1,0:T(8,128)(2,1)} %get-tuple-element.172), kind=kOutput, calls=%fused_computation.7 | convolution fusion | flops 906362880 | bytes 3735552 | tf_op jit(solution)/shard_map/dot_general | solution.py:28
  193.7 1.8 collective-permute-start.29
  195.6 1.5 collective-permute-start.34
  197.0 2.0 collective-permute-start.35
  200.8 3.4 %collective-permute-start.31 = (bf16[128,768]{1,0:T(8,128)(2,1)S(1)}, bf16[128,768]{1,0:T(8,128)(2,1)S(1)}, u32[]{:S(2)}, u32[]{:S(2)}) collective-permute-start(bf16[128,768]{1,0:T(8,128)(2,1)S(1)} %get-tuple-element.203), channel_id=1, source_target_pairs={{0,3},{1,2},{2,1},{3,0},{4,7},{5,6},{6,5},{7,4},{8,11},{9,10},{10,... | collective-permute-start | bytes 589832 | tf_op jit(solution)/shard_map/ppermute | solution.py:45
  204.2 2.3 fusion.2
  206.5 7.7 %collective-permute-done.30 = bf16[128,768]{1,0:T(8,128)(2,1)S(1)} collective-permute-done((bf16[128,768]{1,0:T(8,128)(2,1)S(1)}, bf16[128,768]{1,0:T(8,128)(2,1)S(1)}, u32[]{:S(2)}, u32[]{:S(2)}) %collective-permute-start.30) | collective-permute-done | bytes 196640 | tf_op jit(solution)/shard_map/ppermute | solution.py:45
  215.4 4.0 %collective-permute-start.36 = (bf16[24,2048]{1,0:T(8,128)(2,1)S(1)}, bf16[24,2048]{1,0:T(8,128)(2,1)S(1)}, u32[]{:S(2)}, u32[]{:S(2)}) collective-permute-start(bf16[24,2048]{1,0:T(8,128)(2,1)S(1)} %get-tuple-element.202), channel_id=1, source_target_pairs={{0,1},{1,0},{2,3},{3,2},{4,5},{5,4},{6,7},{7,6},{8,9},{9,8},{10,11... | collective-permute-start | bytes 294920 | tf_op jit(solution)/shard_map/ppermute | solution.py:45
  219.4 2.4 %collective-permute-start.38 = (bf16[24,2048]{1,0:T(8,128)(2,1)S(1)}, bf16[24,2048]{1,0:T(8,128)(2,1)S(1)}, u32[]{:S(2)}, u32[]{:S(2)}) collective-permute-start(bf16[24,2048]{1,0:T(8,128)(2,1)S(1)} %get-tuple-element.200), channel_id=1, source_target_pairs={{0,3},{1,2},{2,1},{3,0},{4,7},{5,6},{6,5},{7,4},{8,11},{9,10},{10,... | collective-permute-start | bytes 294920 | tf_op jit(solution)/shard_map/ppermute | solution.py:45
  223.6 6.4 %collective-permute-done.37.two_ref = bf16[24,2048]{1,0:T(8,128)(2,1)S(1)} collective-permute-done((bf16[24,2048]{1,0:T(8,128)(2,1)S(1)}, bf16[24,2048]{1,0:T(8,128)(2,1)S(1)}, u32[]{:S(2)}, u32[]{:S(2)}) %collective-permute-start.37) | collective-permute-done | bytes 98336 | tf_op jit(solution)/shard_map/ppermute | solution.py:45
  230.0 1.4 shard_map.215
  (215 shorter events, 44.4 us)
Async XLA Ops:
  0.6 18.0 %copy-start.17 = (bf16[256,768]{1,0:T(8,128)(2,1)S(1)}, bf16[256,768]{1,0:T(8,128)(2,1)}, u32[]{:S(2)}) copy-start(bf16[256,768]{1,0:T(8,128)(2,1)} %inputs_ref.1) | copy-start | bytes 1179652
  2.9 9.7 %collective-permute-start.4 = (bf16[24,2048]{1,0:T(8,128)(2,1)}, bf16[24,2048]{1,0:T(8,128)(2,1)S(1)}, u32[]{:S(2)}, u32[]{:S(2)}) collective-permute-start(bf16[24,2048]{1,0:T(8,128)(2,1)} %get-tuple-element.104), channel_id=1, source_target_pairs={{0,1},{1,0},{2,3},{3,2},{4,5},{5,4},{6,7},{7,6},{8,9},{9,8},{10,11... | collective-permute-start | bytes 294920 | tf_op jit(solution)/shard_map/ppermute | solution.py:45
  5.9 11.7 %collective-permute-start.6 = (bf16[24,2048]{1,0:T(8,128)(2,1)}, bf16[24,2048]{1,0:T(8,128)(2,1)S(1)}, u32[]{:S(2)}, u32[]{:S(2)}) collective-permute-start(bf16[24,2048]{1,0:T(8,128)(2,1)} %get-tuple-element.104), channel_id=1, source_target_pairs={{0,3},{1,2},{2,1},{3,0},{4,7},{5,6},{6,5},{7,4},{8,11},{9,10},{10,... | collective-permute-start | bytes 294920 | tf_op jit(solution)/shard_map/ppermute | solution.py:45
  8.4 9.2 %collective-permute-start.5 = (bf16[24,2048]{1,0:T(8,128)(2,1)}, bf16[24,2048]{1,0:T(8,128)(2,1)S(1)}, u32[]{:S(2)}, u32[]{:S(2)}) collective-permute-start(bf16[24,2048]{1,0:T(8,128)(2,1)} %get-tuple-element.103), channel_id=1, source_target_pairs={{0,2},{1,3},{2,0},{3,1},{4,6},{5,7},{6,4},{7,5},{8,10},{9,11},{10,... | collective-permute-start | bytes 294920 | tf_op jit(solution)/shard_map/ppermute | solution.py:45
  9.6 9.1 %collective-permute-start = (bf16[128,768]{1,0:T(8,128)(2,1)S(1)}, bf16[128,768]{1,0:T(8,128)(2,1)S(1)}, u32[]{:S(2)}, u32[]{:S(2)}) collective-permute-start(bf16[128,768]{1,0:T(8,128)(2,1)S(1)} %broadcast_select_fusion.4), channel_id=1, source_target_pairs={{0,4},{1,5},{2,6},{3,7},{4,0},{5,1},{6,2},{7,3},{8,12},{9,13},{10,... | collective-permute-start | bytes 589832 | tf_op jit(solution)/shard_map/ppermute | solution.py:45
  12.6 17.3 %copy-start.26 = (bf16[256,768]{1,0:T(8,128)(2,1)S(1)}, bf16[256,768]{1,0:T(8,128)(2,1)}, u32[]{:S(2)}) copy-start(bf16[256,768]{1,0:T(8,128)(2,1)} %cotangent_ref.1) | copy-start | bytes 1179652
  18.7 11.2 %collective-permute-start.2 = (bf16[128,768]{1,0:T(8,128)(2,1)S(1)}, bf16[128,768]{1,0:T(8,128)(2,1)S(1)}, u32[]{:S(2)}, u32[]{:S(2)}) collective-permute-start(bf16[128,768]{1,0:T(8,128)(2,1)S(1)} %get-tuple-element.207), channel_id=1, source_target_pairs={{0,2},{1,3},{2,0},{3,1},{4,6},{5,7},{6,4},{7,5},{8,10},{9,11},{10,... | collective-permute-start | bytes 589832 | tf_op jit(solution)/shard_map/ppermute | solution.py:45
  19.3 18.8 %copy-start.28 = (bf16[96,1152]{1,0:T(8,128)(2,1)}, bf16[96,1152]{1,0:T(8,128)(2,1)S(1)}, u32[]{:S(2)}) copy-start(bf16[96,1152]{1,0:T(8,128)(2,1)S(1)} %fusion.15.refs_0_) | copy-start | bytes 663556
  19.3 11.9 %collective-permute-start.7 = (bf16[96,1152]{1,0:T(8,128)(2,1)S(1)}, bf16[96,1152]{1,0:T(8,128)(2,1)S(1)}, u32[]{:S(2)}, u32[]{:S(2)}) collective-permute-start(bf16[96,1152]{1,0:T(8,128)(2,1)S(1)} %fusion.15.refs_0_), channel_id=1, source_target_pairs={{0,8},{1,9},{2,10},{3,11},{4,12},{5,13},{6,14},{7,15},{8,0},{9,1},... | collective-permute-start | bytes 663560 | tf_op jit(solution)/shard_map/ppermute | solution.py:45
  20.9 10.8 %collective-permute-start.8 = (bf16[96,1152]{1,0:T(8,128)(2,1)S(1)}, bf16[96,1152]{1,0:T(8,128)(2,1)S(1)}, u32[]{:S(2)}, u32[]{:S(2)}) collective-permute-start(bf16[96,1152]{1,0:T(8,128)(2,1)S(1)} %fusion.15.refs_0_), channel_id=1, source_target_pairs={{0,16},{1,17},{2,18},{3,19},{4,20},{5,21},{6,22},{7,23},{8,24},{9,... | collective-permute-start | bytes 663560 | tf_op jit(solution)/shard_map/ppermute | solution.py:45
  22.4 9.3 %collective-permute-start.9 = (bf16[96,1152]{1,0:T(8,128)(2,1)S(1)}, bf16[96,1152]{1,0:T(8,128)(2,1)S(1)}, u32[]{:S(2)}, u32[]{:S(2)}) collective-permute-start(bf16[96,1152]{1,0:T(8,128)(2,1)S(1)} %fusion.15.refs_0_), channel_id=1, source_target_pairs={{0,24},{1,25},{2,26},{3,27},{4,28},{5,29},{6,30},{7,31},{8,16},{9,... | collective-permute-start | bytes 663560 | tf_op jit(solution)/shard_map/ppermute | solution.py:45
  22.9 10.1 %collective-permute-start.1 = (bf16[128,768]{1,0:T(8,128)(2,1)S(1)}, bf16[128,768]{1,0:T(8,128)(2,1)S(1)}, u32[]{:S(2)}, u32[]{:S(2)}) collective-permute-start(bf16[128,768]{1,0:T(8,128)(2,1)S(1)} %get-tuple-element.206), channel_id=1, source_target_pairs={{0,1},{1,0},{2,3},{3,2},{4,5},{5,4},{6,7},{7,6},{8,9},{9,8},{10,11... | collective-permute-start | bytes 589832 | tf_op jit(solution)/shard_map/ppermute | solution.py:45
  29.9 7.9 %collective-permute-start.3 = (bf16[128,768]{1,0:T(8,128)(2,1)S(1)}, bf16[128,768]{1,0:T(8,128)(2,1)S(1)}, u32[]{:S(2)}, u32[]{:S(2)}) collective-permute-start(bf16[128,768]{1,0:T(8,128)(2,1)S(1)} %collective-permute-done.2), channel_id=1, source_target_pairs={{0,1},{1,0},{2,3},{3,2},{4,5},{5,4},{6,7},{7,6},{8,9},{9,8},{10,11... | collective-permute-start | bytes 589832 | tf_op jit(solution)/shard_map/ppermute | solution.py:45
  33.0 6.2 %collective-permute-start.10 = (bf16[96,1152]{1,0:T(8,128)(2,1)S(1)}, bf16[96,1152]{1,0:T(8,128)(2,1)S(1)}, u32[]{:S(2)}, u32[]{:S(2)}) collective-permute-start(bf16[96,1152]{1,0:T(8,128)(2,1)S(1)} %fusion.15.refs_0_), channel_id=1, source_target_pairs={{0,4},{1,5},{2,6},{3,7},{4,0},{5,1},{6,2},{7,3},{8,12},{9,13},{10,... | collective-permute-start | bytes 663560 | tf_op jit(solution)/shard_map/ppermute | solution.py:45
  33.0 6.2 %collective-permute-start.11 = (bf16[96,1152]{1,0:T(8,128)(2,1)S(1)}, bf16[96,1152]{1,0:T(8,128)(2,1)S(1)}, u32[]{:S(2)}, u32[]{:S(2)}) collective-permute-start(bf16[96,1152]{1,0:T(8,128)(2,1)S(1)} %collective-permute-done.7.refs_1_), channel_id=1, source_target_pairs={{0,4},{1,5},{2,6},{3,7},{4,0},{5,1},{6,2},{7,3},{8,12},{9,13},{10,... | collective-permute-start | bytes 663560 | tf_op jit(solution)/shard_map/ppermute | solution.py:45
  33.5 5.7 %collective-permute-start.12 = (bf16[96,1152]{1,0:T(8,128)(2,1)S(1)}, bf16[96,1152]{1,0:T(8,128)(2,1)S(1)}, u32[]{:S(2)}, u32[]{:S(2)}) collective-permute-start(bf16[96,1152]{1,0:T(8,128)(2,1)S(1)} %collective-permute-done.8.refs_2_), channel_id=1, source_target_pairs={{0,4},{1,5},{2,6},{3,7},{4,0},{5,1},{6,2},{7,3},{8,12},{9,13},{10,... | collective-permute-start | bytes 663560 | tf_op jit(solution)/shard_map/ppermute | solution.py:45
  33.5 5.8 %collective-permute-start.13 = (bf16[96,1152]{1,0:T(8,128)(2,1)S(1)}, bf16[96,1152]{1,0:T(8,128)(2,1)}, u32[]{:S(2)}, u32[]{:S(2)}) collective-permute-start(bf16[96,1152]{1,0:T(8,128)(2,1)S(1)} %collective-permute-done.9.refs_3_), channel_id=1, source_target_pairs={{0,4},{1,5},{2,6},{3,7},{4,0},{5,1},{6,2},{7,3},{8,12},{9,13},{10,... | collective-permute-start | bytes 663560 | tf_op jit(solution)/shard_map/ppermute | solution.py:45
  34.0 25.1 %all-to-all-start = ((bf16[32,16,768]{2,1,0:T(8,128)(2,1)}), bf16[32,16,768]{2,1,0:T(8,128)(2,1)S(1)}, u32[]{:S(2)}, u32[]{:S(2)}) async-start(bf16[32,16,768]{2,1,0:T(8,128)(2,1)} %bitcast.11), calls=%async_computation | async-start | bytes 1572864 | tf_op jit(solution)/shard_map/all_to_all | solution.py:798
  44.6 3.8 %collective-permute-start.14 = (bf16[512,768]{1,0:T(8,128)(2,1)}, bf16[512,768]{1,0:T(8,128)(2,1)S(1)}, u32[]{:S(2)}, u32[]{:S(2)}) collective-permute-start(bf16[512,768]{1,0:T(8,128)(2,1)} %get-tuple-element.115.key_ref.value_ref), channel_id=1, source_target_pairs={{0,4},{1,5},{2,6},{3,7},{4,0},{5,1},{6,2},{7,3},{8,12},{9,13},{10,... | collective-permute-start | bytes 2359304 | tf_op jit(solution)/shard_map/ppermute | solution.py:45
  44.9 12.3 %collective-permute-start.15 = (bf16[96,896]{1,0:T(8,128)(2,1)S(1)}, bf16[96,896]{1,0:T(8,128)(2,1)S(1)}, u32[]{:S(2)}, u32[]{:S(2)}) collective-permute-start(bf16[96,896]{1,0:T(8,128)(2,1)S(1)} %fusion.16.refs_0_), channel_id=1, source_target_pairs={{0,8},{1,9},{2,10},{3,11},{4,12},{5,13},{6,14},{7,15},{8,0},{9,1},... | collective-permute-start | bytes 516104 | tf_op jit(solution)/shard_map/ppermute | solution.py:45
  46.6 11.2 %collective-permute-start.16 = (bf16[96,896]{1,0:T(8,128)(2,1)S(1)}, bf16[96,896]{1,0:T(8,128)(2,1)S(1)}, u32[]{:S(2)}, u32[]{:S(2)}) collective-permute-start(bf16[96,896]{1,0:T(8,128)(2,1)S(1)} %fusion.16.refs_0_), channel_id=1, source_target_pairs={{0,16},{1,17},{2,18},{3,19},{4,20},{5,21},{6,22},{7,23},{8,24},{9,... | collective-permute-start | bytes 516104 | tf_op jit(solution)/shard_map/ppermute | solution.py:45
  48.1 11.0 %collective-permute-start.17 = (bf16[96,896]{1,0:T(8,128)(2,1)S(1)}, bf16[96,896]{1,0:T(8,128)(2,1)S(1)}, u32[]{:S(2)}, u32[]{:S(2)}) collective-permute-start(bf16[96,896]{1,0:T(8,128)(2,1)S(1)} %fusion.16.refs_0_), channel_id=1, source_target_pairs={{0,24},{1,25},{2,26},{3,27},{4,28},{5,29},{6,30},{7,31},{8,16},{9,... | collective-permute-start | bytes 516104 | tf_op jit(solution)/shard_map/ppermute | solution.py:45
  59.1 14.9 %copy-start.10 = (bf16[128,384]{1,0:T(8,128)(2,1)S(1)}, bf16[128,384]{1,0:T(8,128)(2,1)}, u32[]{:S(2)}) copy-start(bf16[128,384]{1,0:T(8,128)(2,1)} %get-tuple-element.122.zero_ref.refs_4_) | copy-start | bytes 294916
  59.1 14.9 %copy-start.11 = (s32[5]{0:T(128)S(1)}, s32[5]{0:T(128)}, u32[]{:S(2)}) copy-start(s32[5]{0:T(128)} %stack.23.flags_ref) | copy-start | bytes 64
  59.2 4.8 %collective-permute-start.20 = (bf16[384,896]{1,0:T(8,128)(2,1)S(1)}, bf16[384,896]{1,0:T(8,128)(2,1)S(1)}, u32[]{:S(2)}, u32[]{:S(2)}) collective-permute-start(bf16[384,896]{1,0:T(8,128)(2,1)S(1)} %pad_maximum_fusion.1), channel_id=1, source_target_pairs={{0,4},{1,5},{2,6},{3,7},{4,0},{5,1},{6,2},{7,3},{8,12},{9,13},{10,... | collective-permute-start | bytes 2064392 | tf_op jit(solution)/shard_map/ppermute | solution.py:45
  60.2 9.3 %collective-permute-start.18 = (bf16[128,384]{1,0:T(8,128)(2,1)S(1)}, bf16[128,384]{1,0:T(8,128)(2,1)S(1)}, u32[]{:S(2)}, u32[]{:S(2)}) collective-permute-start(bf16[128,384]{1,0:T(8,128)(2,1)S(1)} %copy-done.46), channel_id=1, source_target_pairs={{0,1},{1,0},{2,3},{3,2},{4,5},{5,4},{6,7},{7,6},{8,9},{9,8},{10,11... | collective-permute-start | bytes 294920 | tf_op jit(solution)/shard_map/ppermute | solution.py:45
  62.7 7.8 %collective-permute-start.19 = (bf16[128,384]{1,0:T(8,128)(2,1)S(1)}, bf16[128,384]{1,0:T(8,128)(2,1)S(1)}, u32[]{:S(2)}, u32[]{:S(2)}) collective-permute-start(bf16[128,384]{1,0:T(8,128)(2,1)S(1)} %copy-done.47), channel_id=1, source_target_pairs={{0,2},{1,3},{2,0},{3,1},{4,6},{5,7},{6,4},{7,5},{8,10},{9,11},{10,... | collective-permute-start | bytes 294920 | tf_op jit(solution)/shard_map/ppermute | solution.py:45
  67.5 6.5 %collective-permute-start.21 = (bf16[128,384]{1,0:T(8,128)(2,1)S(1)}, bf16[128,384]{1,0:T(8,128)(2,1)S(1)}, u32[]{:S(2)}, u32[]{:S(2)}) collective-permute-start(bf16[128,384]{1,0:T(8,128)(2,1)S(1)} %copy-done.48), channel_id=1, source_target_pairs={{0,3},{1,2},{2,1},{3,0},{4,7},{5,6},{6,5},{7,4},{8,11},{9,10},{10,... | collective-permute-start | bytes 294920 | tf_op jit(solution)/shard_map/ppermute | solution.py:45
  75.3 1.4 collective-permute-start.22
  81.0 23.2 %all-to-all-start.1 = ((bf16[32,16,768]{2,1,0:T(8,128)(2,1)}), bf16[32,16,768]{2,1,0:T(8,128)(2,1)S(1)}, u32[]{:S(2)}, u32[]{:S(2)}) async-start(bf16[32,16,768]{2,1,0:T(8,128)(2,1)} %bitcast.63), calls=%async_computation.1 | async-start | bytes 1572864 | tf_op jit(solution)/shard_map/all_to_all | solution.py:798
  118.7 24.0 %all-to-all-start.2 = ((bf16[32,16,768]{2,1,0:T(8,128)(2,1)}), bf16[32,16,768]{2,1,0:T(8,128)(2,1)S(1)}, u32[]{:S(2)}, u32[]{:S(2)}) async-start(bf16[32,16,768]{2,1,0:T(8,128)(2,1)} %bitcast.64), calls=%async_computation.2 | async-start | bytes 1572864 | tf_op jit(solution)/shard_map/all_to_all | solution.py:798
  148.1 2.7 %collective-permute-start.23 = (bf16[128,768]{1,0:T(8,128)(2,1)}, bf16[128,768]{1,0:T(8,128)(2,1)S(1)}, u32[]{:S(2)}, u32[]{:S(2)}) collective-permute-start(bf16[128,768]{1,0:T(8,128)(2,1)} %get-tuple-element.153), channel_id=1, source_target_pairs={{0,4},{1,5},{2,6},{3,7},{4,0},{5,1},{6,2},{7,3},{8,12},{9,13},{10,... | collective-permute-start | bytes 589832 | tf_op jit(solution)/shard_map/ppermute | solution.py:45
  153.0 5.1 %collective-permute-start.24 = (bf16[128,384]{1,0:T(8,128)(2,1)S(1)}, bf16[128,384]{1,0:T(8,128)(2,1)S(1)}, u32[]{:S(2)}, u32[]{:S(2)}) collective-permute-start(bf16[128,384]{1,0:T(8,128)(2,1)S(1)} %get-tuple-element.154), channel_id=1, source_target_pairs={{0,1},{1,0},{2,3},{3,2},{4,5},{5,4},{6,7},{7,6},{8,9},{9,8},{10,11... | collective-permute-start | bytes 294920 | tf_op jit(solution)/shard_map/ppermute | solution.py:45
  154.8 10.1 %collective-permute-start.25 = (bf16[128,384]{1,0:T(8,128)(2,1)S(1)}, bf16[128,384]{1,0:T(8,128)(2,1)S(1)}, u32[]{:S(2)}, u32[]{:S(2)}) collective-permute-start(bf16[128,384]{1,0:T(8,128)(2,1)S(1)} %get-tuple-element.155), channel_id=1, source_target_pairs={{0,2},{1,3},{2,0},{3,1},{4,6},{5,7},{6,4},{7,5},{8,10},{9,11},{10,... | collective-permute-start | bytes 294920 | tf_op jit(solution)/shard_map/ppermute | solution.py:45
  155.6 9.4 %collective-permute-start.26 = (bf16[128,384]{1,0:T(8,128)(2,1)S(1)}, bf16[128,384]{1,0:T(8,128)(2,1)S(1)}, u32[]{:S(2)}, u32[]{:S(2)}) collective-permute-start(bf16[128,384]{1,0:T(8,128)(2,1)S(1)} %get-tuple-element.156), channel_id=1, source_target_pairs={{0,3},{1,2},{2,1},{3,0},{4,7},{5,6},{6,5},{7,4},{8,11},{9,10},{10,... | collective-permute-start | bytes 294920 | tf_op jit(solution)/shard_map/ppermute | solution.py:45
  164.9 23.0 %all-to-all-start.3 = ((bf16[32,16,768]{2,1,0:T(8,128)(2,1)}), bf16[32,16,768]{2,1,0:T(8,128)(2,1)}, u32[]{:S(2)}, u32[]{:S(2)}) async-start(bf16[32,16,768]{2,1,0:T(8,128)(2,1)} %bitcast.20), calls=%async_computation.3 | async-start | bytes 1572864 | tf_op jit(solution)/shard_map/all_to_all | solution.py:798
  177.5 2.6 %collective-permute-start.27 = (bf16[2,512,384]{2,1,0:T(8,128)(2,1)}, bf16[2,512,384]{2,1,0:T(8,128)(2,1)S(1)}, u32[]{:S(2)}, u32[]{:S(2)}) collective-permute-start(bf16[2,512,384]{2,1,0:T(8,128)(2,1)} %get-tuple-element.167), channel_id=1, source_target_pairs={{0,4},{1,5},{2,6},{3,7},{4,0},{5,1},{6,2},{7,3},{8,12},{9,13},{10,... | collective-permute-start | bytes 2359304 | tf_op jit(solution)/shard_map/ppermute | solution.py:45
  187.9 4.8 %collective-permute-start.28 = (bf16[384,2048]{1,0:T(8,128)(2,1)}, bf16[384,2048]{1,0:T(8,128)(2,1)S(1)}, u32[]{:S(2)}, u32[]{:S(2)}) collective-permute-start(bf16[384,2048]{1,0:T(8,128)(2,1)} %get-tuple-element.175), channel_id=1, source_target_pairs={{0,4},{1,5},{2,6},{3,7},{4,0},{5,1},{6,2},{7,3},{8,12},{9,13},{10,... | collective-permute-start | bytes 4718600 | tf_op jit(solution)/shard_map/ppermute | solution.py:45
  193.7 7.1 %collective-permute-start.29 = (bf16[128,768]{1,0:T(8,128)(2,1)S(1)}, bf16[128,768]{1,0:T(8,128)(2,1)S(1)}, u32[]{:S(2)}, u32[]{:S(2)}) collective-permute-start(bf16[128,768]{1,0:T(8,128)(2,1)S(1)} %get-tuple-element.205), channel_id=1, source_target_pairs={{0,1},{1,0},{2,3},{3,2},{4,5},{5,4},{6,7},{7,6},{8,9},{9,8},{10,11... | collective-permute-start | bytes 589832 | tf_op jit(solution)/shard_map/ppermute | solution.py:45
  195.5 18.9 %collective-permute-start.33 = (bf16[96,2048]{1,0:T(8,128)(2,1)S(1)}, bf16[96,2048]{1,0:T(8,128)(2,1)S(1)}, u32[]{:S(2)}, u32[]{:S(2)}) collective-permute-start(bf16[96,2048]{1,0:T(8,128)(2,1)S(1)} %get-tuple-element.199), channel_id=1, source_target_pairs={{0,8},{1,9},{2,10},{3,11},{4,12},{5,13},{6,14},{7,15},{8,0},{9,1},... | collective-permute-start | bytes 1179656 | tf_op jit(solution)/shard_map/ppermute | solution.py:45
  195.6 19.5 %collective-permute-start.34 = (bf16[96,2048]{1,0:T(8,128)(2,1)S(1)}, bf16[96,2048]{1,0:T(8,128)(2,1)S(1)}, u32[]{:S(2)}, u32[]{:S(2)}) collective-permute-start(bf16[96,2048]{1,0:T(8,128)(2,1)S(1)} %get-tuple-element.198), channel_id=1, source_target_pairs={{0,16},{1,17},{2,18},{3,19},{4,20},{5,21},{6,22},{7,23},{8,24},{9,... | collective-permute-start | bytes 1179656 | tf_op jit(solution)/shard_map/ppermute | solution.py:45
  197.0 18.1 %collective-permute-start.35 = (bf16[96,2048]{1,0:T(8,128)(2,1)S(1)}, bf16[96,2048]{1,0:T(8,128)(2,1)S(1)}, u32[]{:S(2)}, u32[]{:S(2)}) collective-permute-start(bf16[96,2048]{1,0:T(8,128)(2,1)S(1)} %get-tuple-element.197), channel_id=1, source_target_pairs={{0,24},{1,25},{2,26},{3,27},{4,28},{5,29},{6,30},{7,31},{8,16},{9,... | collective-permute-start | bytes 1179656 | tf_op jit(solution)/shard_map/ppermute | solution.py:45
  199.1 15.1 %collective-permute-start.30 = (bf16[128,768]{1,0:T(8,128)(2,1)S(1)}, bf16[128,768]{1,0:T(8,128)(2,1)S(1)}, u32[]{:S(2)}, u32[]{:S(2)}) collective-permute-start(bf16[128,768]{1,0:T(8,128)(2,1)S(1)} %get-tuple-element.204), channel_id=1, source_target_pairs={{0,2},{1,3},{2,0},{3,1},{4,6},{5,7},{6,4},{7,5},{8,10},{9,11},{10,... | collective-permute-start | bytes 589832 | tf_op jit(solution)/shard_map/ppermute | solution.py:45
  200.8 13.4 %collective-permute-start.31 = (bf16[128,768]{1,0:T(8,128)(2,1)S(1)}, bf16[128,768]{1,0:T(8,128)(2,1)S(1)}, u32[]{:S(2)}, u32[]{:S(2)}) collective-permute-start(bf16[128,768]{1,0:T(8,128)(2,1)S(1)} %get-tuple-element.203), channel_id=1, source_target_pairs={{0,3},{1,2},{2,1},{3,0},{4,7},{5,6},{6,5},{7,4},{8,11},{9,10},{10,... | collective-permute-start | bytes 589832 | tf_op jit(solution)/shard_map/ppermute | solution.py:45
  214.3 7.6 %collective-permute-start.32 = (bf16[128,768]{1,0:T(8,128)(2,1)S(1)}, bf16[128,768]{1,0:T(8,128)(2,1)S(1)}, u32[]{:S(2)}, u32[]{:S(2)}) collective-permute-start(bf16[128,768]{1,0:T(8,128)(2,1)S(1)} %broadcast_select_fusion.6), channel_id=1, source_target_pairs={{0,4},{1,5},{2,6},{3,7},{4,0},{5,1},{6,2},{7,3},{8,12},{9,13},{10,... | collective-permute-start | bytes 589832 | tf_op jit(solution)/shard_map/ppermute | solution.py:45
  215.4 8.2 %collective-permute-start.36 = (bf16[24,2048]{1,0:T(8,128)(2,1)S(1)}, bf16[24,2048]{1,0:T(8,128)(2,1)S(1)}, u32[]{:S(2)}, u32[]{:S(2)}) collective-permute-start(bf16[24,2048]{1,0:T(8,128)(2,1)S(1)} %get-tuple-element.202), channel_id=1, source_target_pairs={{0,1},{1,0},{2,3},{3,2},{4,5},{5,4},{6,7},{7,6},{8,9},{9,8},{10,11... | collective-permute-start | bytes 294920 | tf_op jit(solution)/shard_map/ppermute | solution.py:45
  219.4 10.5 %collective-permute-start.37 = (bf16[24,2048]{1,0:T(8,128)(2,1)S(1)}, bf16[24,2048]{1,0:T(8,128)(2,1)S(1)}, u32[]{:S(2)}, u32[]{:S(2)}) collective-permute-start(bf16[24,2048]{1,0:T(8,128)(2,1)S(1)} %get-tuple-element.201), channel_id=1, source_target_pairs={{0,2},{1,3},{2,0},{3,1},{4,6},{5,7},{6,4},{7,5},{8,10},{9,11},{10,... | collective-permute-start | bytes 294920 | tf_op jit(solution)/shard_map/ppermute | solution.py:45
  219.4 10.5 %collective-permute-start.38 = (bf16[24,2048]{1,0:T(8,128)(2,1)S(1)}, bf16[24,2048]{1,0:T(8,128)(2,1)S(1)}, u32[]{:S(2)}, u32[]{:S(2)}) collective-permute-start(bf16[24,2048]{1,0:T(8,128)(2,1)S(1)} %get-tuple-element.200), channel_id=1, source_target_pairs={{0,3},{1,2},{2,1},{3,0},{4,7},{5,6},{6,5},{7,4},{8,11},{9,10},{10,... | collective-permute-start | bytes 294920 | tf_op jit(solution)/shard_map/ppermute | solution.py:45
  (47 other events, 261.8 us)

commit v3 on v2

--- a/solution.py
+++ b/solution.py
@@ -110,10 +110,12 @@
     return total
 
 
-def reduce_levels(links, block):
+def reduce_levels(links, block, before_last):
     rows = block.shape[0] // links.levels
     parts = [rows_of(block, links.level ^ b, rows) for b in range(links.levels)]
-    got = tie(*[links.swap_level(parts[b].astype(BF), b) for b in range(1, links.levels)])
+    sent = [part.astype(BF) for part in parts[1:]]
+    sent[-1] = gate(sent[-1], before_last)
+    got = tie(*[links.swap_level(part, b + 1) for b, part in enumerate(sent)])
     return [parts[0], *got]
 
 
@@ -579,18 +581,16 @@
     expand_ref,
     router_ref,
     weight_in_ref,
-    weight_out_ref,
     held_ref,
     grad_result_ref,
     hidden_ref,
     grad_inner_ref,
     grad_back_ref,
-    taken_ref,
     grad_logits_ref,
-    result_sum,
+    gate_ref,
     grad_sum,
     probs,
-    gates,
+    grad_gate,
 ):
     step = pl.program_id(0)
     experts = router_ref.shape[1]
@@ -605,34 +605,31 @@
         weights = jnp.exp(logits - jnp.max(logits, axis=1, keepdims=True))
         router_probs = weights / jnp.sum(weights, axis=1, keepdims=True)
         probs[...] = router_probs
-        gate = jnp.sum(router_probs * mine, axis=1, keepdims=True)
-        gates[...] = gate
-        grad_result_ref[...] = (gate * cot_ref[...].astype(F32)).astype(BF)
-        result_sum[...] = jnp.zeros_like(result_sum)
+        gate_rows = jnp.sum(router_probs * mine, axis=1, keepdims=True)
+        gate_ref[...] = gate_rows
+        grad_result_ref[...] = (gate_rows * cot_ref[...].astype(F32)).astype(BF)
         grad_sum[...] = jnp.zeros_like(grad_sum)
+        grad_gate[...] = jnp.zeros_like(grad_gate)
 
     weight_in = weight_in_ref[0]
     hidden, slope = gelu_and_slope(dot(held_ref[...], weight_in))
     hidden = hidden.astype(BF)
     hidden_ref[...] = hidden
-    grad_inner = (back_ref[...].astype(F32) * (gates[...] * slope)).astype(BF)
+    back = back_ref[...].astype(F32)
+    grad_inner = (back * (gate_ref[...] * slope)).astype(BF)
     grad_inner_ref[...] = grad_inner
-    result_sum[...] += dot(hidden, weight_out_ref[0])
+    grad_gate[...] += jnp.sum(hidden.astype(F32) * back, axis=1, keepdims=True)
     grad_sum[...] += dot_nt(grad_inner, weight_in)
 
     @pl.when(step == pl.num_programs(0) - 1)
     def _():
-        result = result_sum[...].astype(BF).astype(F32)
-        gate = gates[...]
-        grad_gate = jnp.sum(cot_ref[...].astype(F32) * result, axis=1, keepdims=True)
-        grad_logits = (grad_gate * probs[...] * (mine - gate)).astype(BF)
+        grad_logits = (grad_gate[...] * probs[...] * (mine - gate_ref[...])).astype(BF)
         grad_logits_ref[...] = grad_logits
         grad_held = grad_sum[...] + dot_nt(grad_logits, router_ref[...])
         grad_back_ref[...] = dot(expand_ref[...], grad_held.astype(BF)).astype(BF)
-        taken_ref[...] = (gate * result).astype(BF)
-
-
-def expert_layer(flags, arrived, cot, back, compact, expand, router, expert_in, expert_out):
+
+
+def expert_layer(flags, arrived, cot, back, compact, expand, router, expert_in):
     slots, width = arrived.shape
     capacity = compact.shape[0]
     hidden_width = expert_in.shape[2]
@@ -651,28 +648,26 @@
             whole((slots, capacity)),
             whole((width, experts)),
             pl.BlockSpec((1, width, TILE), lambda i: (0, 0, i)),
-            pl.BlockSpec((1, TILE, width), lambda i: (0, i, 0)),
         ],
-        out_specs=[wide, wide, tall, tall, whole((slots, width)), wide]
-        + [whole((capacity, experts))],
+        out_specs=[wide, wide, tall, tall, whole((slots, width))]
+        + [whole((capacity, experts)), whole((capacity, 1))],
         out_shape=[
             low_shape(capacity, width),
             low_shape(capacity, width),
             low_shape(capacity, hidden_width),
             low_shape(capacity, hidden_width),
             low_shape(slots, width),
-            low_shape(capacity, width),
             low_shape(capacity, experts),
+            wide_shape(capacity, 1),
         ],
         scratch_shapes=[
-            pltpu.VMEM((capacity, width), F32),
             pltpu.VMEM((capacity, width), F32),
             pltpu.VMEM((capacity, experts), F32),
             pltpu.VMEM((capacity, 1), F32),
         ],
         compiler_params=params(),
         cost_estimate=cost(8 * capacity * width * hidden_width, 8 * width * hidden_width),
-    )(flags, arrived, cot, back, compact, expand, router, expert_in, expert_out)
+    )(flags, arrived, cot, back, compact, expand, router, expert_in)
 
 
 def owner_backward_kernel(
@@ -905,7 +900,7 @@
     arrived = all_to_all(second_slots.reshape(experts, most, width)).reshape(-1, width)
 
     cot_held, cot_back = cotangent_layer(gate(cot_arrived, second_slots), compact, expert_out)
-    held, grad_result, hidden, grad_inner, grad_back, taken_held, grad_logits = expert_layer(
+    held, grad_result, hidden, grad_inner, grad_back, grad_logits, gate_rows = expert_layer(
         flags,
         gate(arrived, cot_back),
         cot_held,
@@ -914,13 +909,13 @@
         expand,
         full_router,
         expert_in,
-        expert_out,
     )
     grad_returned = all_to_all(grad_back.reshape(experts, most, width)).reshape(-1, width)
     grad_router = dot_tn(held, grad_logits)
     grad_weight_out = dot_tn(hidden, grad_result)
     grad_weight_in = dot_tn(held, grad_inner)
-    taken_back = dot(expand, taken_held).astype(BF)
+    result = dot(hidden, expert_out[0]).astype(BF).astype(F32)
+    taken_back = dot(expand, (gate_rows * result).astype(BF)).astype(BF)
     grad_returned = gate(
         grad_returned, grad_weight_in, grad_weight_out, grad_router, taken_back, to_tokens
     )
@@ -958,6 +953,7 @@
     )
     parts = gate(grad_first_work, core_sum).reshape(blocks, half_rows, width)
     back = tie(*[links.swap_level(parts[b], b) for b in (1, 2, 3)])
+    back = tie(*back, group_sum)[:-1]
     near = (parts[0].astype(F32) + back[0].astype(F32)).astype(BF)
     far = (back[1].astype(F32) + back[2].astype(F32)).astype(BF)
     grad_first = workers_to_owner(links, near, far).astype(F32)
@@ -969,7 +965,7 @@
     )
     output = (middle + dot(to_tokens, taken_arrived)).astype(BF)
 
-    sums = reduce_levels(links, gate(group_sum, *back))
+    sums = reduce_levels(links, gate(group_sum, *back), grad_input)
     *grad_weights, grad_w_output, grad_w_router, grad_norm_one, grad_norm_two = finish(
         flags,
         [*sums, w_query, w_key, w_value, norm_one.reshape(1, own_rows)],

time: 232 us -> 232 us (level)
  matrix products: 19.9 us -> 24.8 us
  waiting for transfers between devices: 60.5 us -> 55.8 us
    all_to_all x4, waiting for transfers between devices: 16 us -> 10.8 us  [all_to_all(): return lax.all_to_all(array, AXES, split_axis=0, concat_axis=0, tiled=True)]
    dot_general x3, matrix products: 6.11 us -> 9.33 us  [dot(): return jnp.dot(left, right, preferred_element_type=F32)]
  transfers between devices with their start and end apart: 43 -> 43, of which waited for: 19 -> 19; matrix products, arithmetic and copies ran while one was open for 15% -> 17% of each run, Pallas kernels for 15% -> 15%
where the time goes in v3:
time: 232 us; the launch traced here: 230 us
  starting transfers between devices  62 us (27%)
  Pallas kernels  58.8 us (25%)
  waiting for transfers between devices  55.8 us (24%)
  matrix products  24.8 us (11%)
  local copies, waits for them, and re-layouts  14.6 us (6%)
  other arithmetic  13.1 us (6%)
    ppermute x39, starting transfers between devices, permute(): return lax.ppermute(array, AXES, pairs)  45.6 us
    ppermute x39, waiting for transfers between devices, permute(): return lax.ppermute(array, AXES, pairs)  44.9 us
    pallas_call x9, Pallas kernels, one_step(): pl.pallas_call(kernel, grid=(1,), in_specs=[FLAGS] + [whole(operand.shape...  24.2 us
    all_to_all x4, starting transfers between devices, all_to_all(): return lax.all_to_all(array, AXES, split_axis=0, concat_axis=0, tiled=True)  16.4 us
    dot_general x3, matrix products, dot_tn(): lax.dot_general(left, right, (((0,), (0,)), ((), ())), preferred_element_...  12.3 us
    pallas_call x1, Pallas kernels, expert_layer(): pl.pallas_call(expert_kernel, grid=(hidden_width // TILE,), in_specs=[FLA...  11.9 us
    all_to_all x4, waiting for transfers between devices, all_to_all(): return lax.all_to_all(array, AXES, split_axis=0, concat_axis=0, tiled=True)  10.8 us
    unnamed x104, local copies, waits for them, and re-layouts  10.5 us
  transfers between devices with their start and end apart: 43, of which 19 were waited for; matrix products, arithmetic and copies ran while one was open for 17% of the time, Pallas kernels for 15%

profile of v3, /device:TPU:0, one launch (start us, length us, event | category | flops | bytes accessed | tf_op | source)
XLA Modules:
  0.0 230.5 jit_solution(16319358875090341004)
XLA Ops:
  1.3 1.7 shard_map.203
  2.9 3.0 %collective-permute-start.4 = (bf16[24,2048]{1,0:T(8,128)(2,1)}, bf16[24,2048]{1,0:T(8,128)(2,1)S(1)}, u32[]{:S(2)}, u32[]{:S(2)}) collective-permute-start(bf16[24,2048]{1,0:T(8,128)(2,1)} %get-tuple-element.108), channel_id=1, source_target_pairs={{0,1},{1,0},{2,3},{3,2},{4,5},{5,4},{6,7},{7,6},{8,9},{9,8},{10,11... | collective-permute-start | bytes 294920 | tf_op jit(solution)/shard_map/ppermute | solution.py:45
  5.9 2.5 %collective-permute-start.6 = (bf16[24,2048]{1,0:T(8,128)(2,1)}, bf16[24,2048]{1,0:T(8,128)(2,1)S(1)}, u32[]{:S(2)}, u32[]{:S(2)}) collective-permute-start(bf16[24,2048]{1,0:T(8,128)(2,1)} %get-tuple-element.108), channel_id=1, source_target_pairs={{0,3},{1,2},{2,1},{3,0},{4,7},{5,6},{6,5},{7,4},{8,11},{9,10},{10,... | collective-permute-start | bytes 294920 | tf_op jit(solution)/shard_map/ppermute | solution.py:45
  12.7 5.3 %collective-permute-done.5 = bf16[24,2048]{1,0:T(8,128)(2,1)S(1)} collective-permute-done((bf16[24,2048]{1,0:T(8,128)(2,1)}, bf16[24,2048]{1,0:T(8,128)(2,1)S(1)}, u32[]{:S(2)}, u32[]{:S(2)}) %collective-permute-start.5) | collective-permute-done | bytes 98336 | tf_op jit(solution)/shard_map/ppermute | solution.py:45
  19.3 1.6 collective-permute-start.7
  20.8 1.5 collective-permute-start.8
  22.8 2.7 %collective-permute-start.1 = (bf16[128,768]{1,0:T(8,128)(2,1)S(1)}, bf16[128,768]{1,0:T(8,128)(2,1)S(1)}, u32[]{:S(2)}, u32[]{:S(2)}) collective-permute-start(bf16[128,768]{1,0:T(8,128)(2,1)S(1)} %get-tuple-element.214), channel_id=1, source_target_pairs={{0,1},{1,0},{2,3},{3,2},{4,5},{5,4},{6,7},{7,6},{8,9},{9,8},{10,11... | collective-permute-start | bytes 589832 | tf_op jit(solution)/shard_map/ppermute | solution.py:45
  25.5 4.4 %collective-permute-done.2 = bf16[128,768]{1,0:T(8,128)(2,1)S(1)} collective-permute-done((bf16[128,768]{1,0:T(8,128)(2,1)S(1)}, bf16[128,768]{1,0:T(8,128)(2,1)S(1)}, u32[]{:S(2)}, u32[]{:S(2)}) %collective-permute-start.2) | collective-permute-done | bytes 196640 | tf_op jit(solution)/shard_map/ppermute | solution.py:45
  34.0 4.5 %all-to-all-start = ((bf16[32,16,768]{2,1,0:T(8,128)(2,1)}), bf16[32,16,768]{2,1,0:T(8,128)(2,1)S(1)}, u32[]{:S(2)}, u32[]{:S(2)}) async-start(bf16[32,16,768]{2,1,0:T(8,128)(2,1)} %bitcast.11), calls=%async_computation | async-start | bytes 1572864 | tf_op jit(solution)/shard_map/all_to_all | solution.py:793
  40.7 4.7 %shard_map.204 = (bf16[512,384]{1,0:T(8,128)(2,1)}, bf16[512,768]{1,0:T(8,128)(2,1)}, bf16[768,1152]{1,0:T(8,128)(2,1)}) custom-call(s32[5]{0:T(128)} %stack.23.flags_ref, bf16[512,768]{1,0:T(8,128)(2,1)} %fusion.3.normed_ref, bf16[96,1152]{1,0:T(8,128)(2,1)} %copy-done.27, bf16[96,1152]{1,0:T(8,128)(2,1)} %copy-done.35, bf16[96,1152]{1,0:T(8,128)(2,1)} %copy-done.36, ...), custom_call_target="tpu_custom_call" | custom-call | bytes 1048576 | tf_op jit(solution)/shard_map/pallas_call | solution.py:274
  45.7 1.7 collective-permute-start.15
  47.4 1.5 collective-permute-start.16
  50.1 7.8 %shard_map.205 = (bf16[128,384]{1,0:T(8,128)(2,1)}, bf16[128,384]{1,0:T(8,128)(2,1)}, bf16[128,384]{1,0:T(8,128)(2,1)}, bf16[128,384]{1,0:T(8,128)(2,1)}, bf16[6...) custom-call(bf16[512,384]{1,0:T(8,128)(2,1)} %get-tuple-element.118.query_ref, ...), custom_call_target="tpu_custom_call" | custom-call | flops 2000000000 | bytes 4096 | tf_op jit(solution)/shard_map/pallas_call | solution.py:180
  60.8 2.6 %collective-permute-start.18 = (bf16[128,384]{1,0:T(8,128)(2,1)S(1)}, bf16[128,384]{1,0:T(8,128)(2,1)S(1)}, u32[]{:S(2)}, u32[]{:S(2)}) collective-permute-start(bf16[128,384]{1,0:T(8,128)(2,1)S(1)} %copy-done.46), channel_id=1, source_target_pairs={{0,1},{1,0},{2,3},{3,2},{4,5},{5,4},{6,7},{7,6},{8,9},{9,8},{10,11... | collective-permute-start | bytes 294920 | tf_op jit(solution)/shard_map/ppermute | solution.py:45
  65.5 2.7 %shard_map.206 = (bf16[768,896]{1,0:T(8,128)(2,1)}, f32[1,768]{1,0:T(1,128)}) custom-call(s32[5]{0:T(128)} %stack.23.flags_ref, bf16[96,896]{1,0:T(8,128)(2,1)} %copy-done.26, bf16[96,896]{1,0:T(8,128)(2,1)} %copy-done.31, bf16[96,896]{1,0:T(8,128)(2,1)} %copy-done.32, bf16[96,896]{1,0:T(8,128)(2,1)} %copy-done.33, bf16[384,896]{1,0:T(8,128)(2,1)} %copy-done.30), custom_call_target="tpu_custom_call" | custom-call | bytes 1048576 | tf_op jit(solution)/shard_map/pallas_call | solution.py:274
  71.2 3.4 %collective-permute-done.21.three_ref = bf16[128,384]{1,0:T(8,128)(2,1)S(1)} collective-permute-done((bf16[128,384]{1,0:T(8,128)(2,1)S(1)}, bf16[128,384]{1,0:T(8,128)(2,1)S(1)}, u32[]{:S(2)}, u32[]{:S(2)}) %collective-permute-start.21) | collective-permute-done | bytes 98336 | tf_op jit(solution)/shard_map/ppermute | solution.py:45
  78.0 3.6 %shard_map.208 = (bf16[256,768]{1,0:T(8,128)(2,1)}, f32[256,768]{1,0:T(8,128)}, bf16[512,768]{1,0:T(8,128)(2,1)}) custom-call(s32[5]{0:T(128)} %stack.23.flags_ref, bf16[128,768]{1,0:T(8,128)(2,1)} %copy-done.5, bf16[128,768]{1,0:T(8,128)(2,1)} %copy-done.41, bf16[256,768]{1,0:T(8,128)(2,1)} %inputs_ref.1, bf16[768,896]{1,0:T(8,128)(2,1)} %get-tuple-element.141.weight_ref, ...), custom_call_target="tpu_custom_call" | custom-call | bytes 1048576 | tf_op jit(solution)/shard_map/pallas_call | solution.py:274
  81.7 4.0 %all-to-all-start.1 = ((bf16[32,16,768]{2,1,0:T(8,128)(2,1)}), bf16[32,16,768]{2,1,0:T(8,128)(2,1)S(1)}, u32[]{:S(2)}, u32[]{:S(2)}) async-start(bf16[32,16,768]{2,1,0:T(8,128)(2,1)} %bitcast.76), calls=%async_computation.1 | async-start | bytes 1572864 | tf_op jit(solution)/shard_map/all_to_all | solution.py:793
  85.7 1.6 slice.64.router_ref
  89.6 6.0 %shard_map.209 = (bf16[320,768]{1,0:T(8,128)(2,1)}, bf16[320,3072]{1,0:T(8,128)(2,1)}) custom-call(bf16[512,768]{1,0:T(8,128)(2,1)} %bitcast.73, bf16[320,512]{1,0:T(8,128)(2,1)} %fusion.25.compact_ref, bf16[1,3072,768]{2,1,0:T(8,128)(2,1)} %weight_out_ref.1), custom_call_target="tpu_custom_call" | custom-call | flops 1509949440 | bytes 9437184 | tf_op jit(solution)/shard_map/pallas_call | solution.py:560
  95.6 9.5 %all-to-all-done.1 = bf16[32,16,768]{2,1,0:T(8,128)(2,1)S(1)} async-done(((bf16[32,16,768]{2,1,0:T(8,128)(2,1)}), bf16[32,16,768]{2,1,0:T(8,128)(2,1)S(1)}, u32[]{:S(2)}, u32[]{:S(2)}) %all-to-all-start.1) | async-done | bytes 786464 | tf_op jit(solution)/shard_map/all_to_all | solution.py:793
  106.0 11.9 %shard_map.210 = (bf16[320,768]{1,0:T(8,128)(2,1)}, bf16[320,768]{1,0:T(8,128)(2,1)}, bf16[320,3072]{1,0:T(8,128)(2,1)}, bf16[320,3072]{1,0:T(8,128)(2,1)}, bf16...) custom-call(s32[5]{0:T(128)} %stack.23.flags_ref, bf16[512,768]{1,0:T(8,128)(2,1)} %bitcast.75, ...), custom_call_target="tpu_custom_call" | custom-call | flops 6039797760 | bytes 18874368 | tf_op jit(solution)/shard_map/pallas_call | solution.py:639
  117.9 4.4 %all-to-all-start.2 = ((bf16[32,16,768]{2,1,0:T(8,128)(2,1)}), bf16[32,16,768]{2,1,0:T(8,128)(2,1)S(1)}, u32[]{:S(2)}, u32[]{:S(2)}) async-start(bf16[32,16,768]{2,1,0:T(8,128)(2,1)} %bitcast.77), calls=%async_computation.2 | async-start | bytes 1572864 | tf_op jit(solution)/shard_map/all_to_all | solution.py:793
  122.7 6.9 %fusion.41 = f32[768,3072]{1,0:T(8,128)} fusion(bf16[320,768]{1,0:T(8,128)(2,1)S(1)} %copy-done.24, bf16[320,3072]{1,0:T(8,128)(2,1)} %get-tuple-element.152), kind=kOutput, calls=%fused_computation.94 | convolution fusion | flops 1509949440 | bytes 11894784 | tf_op jit(solution)/shard_map/dot_general | solution.py:24
  129.6 5.2 %fusion.42 = f32[3072,768]{1,0:T(8,128)} fusion(bf16[320,3072]{1,0:T(8,128)(2,1)S(1)} %copy-done.23, bf16[320,768]{1,0:T(8,128)(2,1)S(1)} %copy-done.34), kind=kOutput, calls=%fused_computation.95 | convolution fusion | flops 1509949440 | bytes 11894784 | tf_op jit(solution)/shard_map/dot_general | solution.py:24
  134.8 5.8 %convolution_convert_fusion = bf16[512,768]{1,0:T(8,128)(2,1)} fusion(bf16[320,3072]{1,0:T(8,128)(2,1)S(1)} %copy-done.23, bf16[1,3072,768]{2,1,0:T(8,128)(2,1)} %weight_out_ref.1, f32[320]{0:T(512)S(1)} %reduce.2, s32[512]{0:T(512)S(1)} %and_select_fusion), kind=kOutput, calls=%fused_computation.7 | convolution fusion | flops 1763147776 | bytes 7474432 | tf_op jit(solution)/shard_map/dot_general | solution.py:20
  140.5 1.3 all-to-all-done.2
  142.8 4.4 %shard_map.211 = (f32[256,768]{1,0:T(8,128)}, bf16[256,768]{1,0:T(8,128)(2,1)}, bf16[128,768]{1,0:T(8,128)(2,1)}, bf16[128,768]{1,0:T(8,128)(2,1)}, bf16[16,768]{1,0:T(8,128)(2,1)}) custom-call(s32[5]{0:T(128)} %stack.23.flags_ref, bf16[512,768]{1,0:T(8,128)(2,1)} %bitcast.74, bf16[256,512]{1,0:T(8,128)(2,1)} %fusion.26.to_tokens_ref, ...), custom_call_target="tpu_custom_call" | custom-call | bytes 1048576 | tf_op jit(solution)/shard_map/pallas_call | solution.py:274
  147.2 1.5 collective-permute-start.23
  152.1 1.8 collective-permute-start.24
  154.7 1.8 collective-permute-start.26
  157.2 6.9 %collective-permute-done.25.refs_2_ = bf16[128,384]{1,0:T(8,128)(2,1)S(1)} collective-permute-done((bf16[128,384]{1,0:T(8,128)(2,1)S(1)}, bf16[128,384]{1,0:T(8,128)(2,1)S(1)}, u32[]{:S(2)}, u32[]{:S(2)}) %collective-permute-start.25) | collective-permute-done | bytes 98336 | tf_op jit(solution)/shard_map/ppermute | solution.py:45
  164.1 3.6 %all-to-all-start.3 = ((bf16[32,16,768]{2,1,0:T(8,128)(2,1)}), bf16[32,16,768]{2,1,0:T(8,128)(2,1)}, u32[]{:S(2)}, u32[]{:S(2)}) async-start(bf16[32,16,768]{2,1,0:T(8,128)(2,1)} %bitcast.21), calls=%async_computation.3 | async-start | bytes 1572864 | tf_op jit(solution)/shard_map/all_to_all | solution.py:793
  167.8 8.9 %shard_map.213 = (bf16[512,384]{1,0:T(8,128)(2,1)}, bf16[2,512,384]{2,1,0:T(8,128)(2,1)}, bf16[2,512,384]{2,1,0:T(8,128)(2,1)}) custom-call(bf16[512,384]{1,0:T(8,128)(2,1)} %get-tuple-element.118.query_ref, bf16[512,768]{1,0:T(8,128)(2,1)} %get-tuple-element.119.key_ref.value_ref, bf16[512,768]{1,0:T(8,128)(2,1)} %get-tuple-element.119.key_ref.value_ref, ...), custom_call_target="tpu_custom_call" | custom-call | flops 20000000000 | bytes 4096 | tf_op jit(solution)/shard_map/pallas_call | solution.py:231
  176.9 2.3 %collective-permute-done.27.got_ref = bf16[2,512,384]{2,1,0:T(8,128)(2,1)S(1)} collective-permute-done((bf16[2,512,384]{2,1,0:T(8,128)(2,1)}, bf16[2,512,384]{2,1,0:T(8,128)(2,1)S(1)}, u32[]{:S(2)}, u32[]{:S(2)}) %collective-permute-start.27) | collective-permute-done | bytes 786464 | tf_op jit(solution)/shard_map/ppermute | solution.py:45
  181.4 4.6 %shard_map.214 = (bf16[512,1152]{1,0:T(8,128)(2,1)S(1)}, f32[384,2048]{1,0:T(8,128)}, bf16[384,2048]{1,0:T(8,128)(2,1)}) custom-call(s32[5]{0:T(128)S(1)} %copy-done.12, bf16[512,768]{1,0:T(8,128)(2,1)S(1)} %copy-done, bf16[512,384]{1,0:T(8,128)(2,1)S(1)} %copy-done.4, bf16[2,512,384]{2,1,0:T(8,128)(2,1)S(1)} %copy-done.1, ...), custom_call_target="tpu_custom_call" | custom-call | bytes 1048576 | tf_op jit(solution)/shard_map/pallas_call | solution.py:274
  187.0 1.5 collective-permute-start.28
  188.7 3.2 %convolution_convert_fusion.2 = bf16[512,768]{1,0:T(8,128)(2,1)S(1)} fusion(bf16[512,1152]{1,0:T(8,128)(2,1)} %copy-done.15, bf16[768,1152]{1,0:T(8,128)(2,1)} %get-tuple-element.176), kind=kOutput, calls=%fused_computation.9 | convolution fusion | flops 906362880 | bytes 3735552 | tf_op jit(solution)/shard_map/dot_general | solution.py:28
  192.8 1.8 collective-permute-start.29
  194.8 1.4 collective-permute-start.33
  196.2 2.0 collective-permute-start.34
  199.9 3.3 %collective-permute-start.31 = (bf16[128,768]{1,0:T(8,128)(2,1)S(1)}, bf16[128,768]{1,0:T(8,128)(2,1)S(1)}, u32[]{:S(2)}, u32[]{:S(2)}) collective-permute-start(bf16[128,768]{1,0:T(8,128)(2,1)S(1)} %get-tuple-element.211), channel_id=1, source_target_pairs={{0,3},{1,2},{2,1},{3,0},{4,7},{5,6},{6,5},{7,4},{8,11},{9,10},{10,... | collective-permute-start | bytes 589832 | tf_op jit(solution)/shard_map/ppermute | solution.py:45
  203.3 2.3 fusion.16
  205.6 7.8 %collective-permute-done.30 = bf16[128,768]{1,0:T(8,128)(2,1)S(1)} collective-permute-done((bf16[128,768]{1,0:T(8,128)(2,1)S(1)}, bf16[128,768]{1,0:T(8,128)(2,1)S(1)}, u32[]{:S(2)}, u32[]{:S(2)}) %collective-permute-start.30) | collective-permute-done | bytes 196640 | tf_op jit(solution)/shard_map/ppermute | solution.py:45
  214.7 3.9 %collective-permute-start.36 = (bf16[24,2048]{1,0:T(8,128)(2,1)S(1)}, bf16[24,2048]{1,0:T(8,128)(2,1)S(1)}, u32[]{:S(2)}, u32[]{:S(2)}) collective-permute-start(bf16[24,2048]{1,0:T(8,128)(2,1)S(1)} %get-tuple-element.210), channel_id=1, source_target_pairs={{0,1},{1,0},{2,3},{3,2},{4,5},{5,4},{6,7},{7,6},{8,9},{9,8},{10,11... | collective-permute-start | bytes 294920 | tf_op jit(solution)/shard_map/ppermute | solution.py:45
  220.3 2.4 %collective-permute-start.38 = (bf16[24,2048]{1,0:T(8,128)(2,1)S(1)}, bf16[24,2048]{1,0:T(8,128)(2,1)S(1)}, u32[]{:S(2)}, u32[]{:S(2)}) collective-permute-start(bf16[24,2048]{1,0:T(8,128)(2,1)S(1)} %get-tuple-element.192), channel_id=1, source_target_pairs={{0,3},{1,2},{2,1},{3,0},{4,7},{5,6},{6,5},{7,4},{8,11},{9,10},{10,... | collective-permute-start | bytes 294920 | tf_op jit(solution)/shard_map/ppermute | solution.py:45
  222.7 6.3 %collective-permute-done.37.two_ref = bf16[24,2048]{1,0:T(8,128)(2,1)S(1)} collective-permute-done((bf16[24,2048]{1,0:T(8,128)(2,1)S(1)}, bf16[24,2048]{1,0:T(8,128)(2,1)S(1)}, u32[]{:S(2)}, u32[]{:S(2)}) %collective-permute-start.37) | collective-permute-done | bytes 98336 | tf_op jit(solution)/shard_map/ppermute | solution.py:45
  229.1 1.4 shard_map.215
  (216 shorter events, 44.2 us)
Async XLA Ops:
  0.6 18.4 %copy-start.17 = (bf16[256,768]{1,0:T(8,128)(2,1)S(1)}, bf16[256,768]{1,0:T(8,128)(2,1)}, u32[]{:S(2)}) copy-start(bf16[256,768]{1,0:T(8,128)(2,1)} %inputs_ref.1) | copy-start | bytes 1179652
  2.9 9.8 %collective-permute-start.4 = (bf16[24,2048]{1,0:T(8,128)(2,1)}, bf16[24,2048]{1,0:T(8,128)(2,1)S(1)}, u32[]{:S(2)}, u32[]{:S(2)}) collective-permute-start(bf16[24,2048]{1,0:T(8,128)(2,1)} %get-tuple-element.108), channel_id=1, source_target_pairs={{0,1},{1,0},{2,3},{3,2},{4,5},{5,4},{6,7},{7,6},{8,9},{9,8},{10,11... | collective-permute-start | bytes 294920 | tf_op jit(solution)/shard_map/ppermute | solution.py:45
  5.9 12.0 %collective-permute-start.6 = (bf16[24,2048]{1,0:T(8,128)(2,1)}, bf16[24,2048]{1,0:T(8,128)(2,1)S(1)}, u32[]{:S(2)}, u32[]{:S(2)}) collective-permute-start(bf16[24,2048]{1,0:T(8,128)(2,1)} %get-tuple-element.108), channel_id=1, source_target_pairs={{0,3},{1,2},{2,1},{3,0},{4,7},{5,6},{6,5},{7,4},{8,11},{9,10},{10,... | collective-permute-start | bytes 294920 | tf_op jit(solution)/shard_map/ppermute | solution.py:45
  9.5 9.5 %collective-permute-start = (bf16[128,768]{1,0:T(8,128)(2,1)S(1)}, bf16[128,768]{1,0:T(8,128)(2,1)S(1)}, u32[]{:S(2)}, u32[]{:S(2)}) collective-permute-start(bf16[128,768]{1,0:T(8,128)(2,1)S(1)} %broadcast_select_fusion.4), channel_id=1, source_target_pairs={{0,4},{1,5},{2,6},{3,7},{4,0},{5,1},{6,2},{7,3},{8,12},{9,13},{10,... | collective-permute-start | bytes 589832 | tf_op jit(solution)/shard_map/ppermute | solution.py:45
  9.5 8.4 %collective-permute-start.5 = (bf16[24,2048]{1,0:T(8,128)(2,1)}, bf16[24,2048]{1,0:T(8,128)(2,1)S(1)}, u32[]{:S(2)}, u32[]{:S(2)}) collective-permute-start(bf16[24,2048]{1,0:T(8,128)(2,1)} %get-tuple-element.107), channel_id=1, source_target_pairs={{0,2},{1,3},{2,0},{3,1},{4,6},{5,7},{6,4},{7,5},{8,10},{9,11},{10,... | collective-permute-start | bytes 294920 | tf_op jit(solution)/shard_map/ppermute | solution.py:45
  12.7 17.3 %copy-start.25 = (bf16[256,768]{1,0:T(8,128)(2,1)S(1)}, bf16[256,768]{1,0:T(8,128)(2,1)}, u32[]{:S(2)}) copy-start(bf16[256,768]{1,0:T(8,128)(2,1)} %cotangent_ref.1) | copy-start | bytes 1179652
  19.1 10.9 %collective-permute-start.2 = (bf16[128,768]{1,0:T(8,128)(2,1)S(1)}, bf16[128,768]{1,0:T(8,128)(2,1)S(1)}, u32[]{:S(2)}, u32[]{:S(2)}) collective-permute-start(bf16[128,768]{1,0:T(8,128)(2,1)S(1)} %get-tuple-element.215), channel_id=1, source_target_pairs={{0,2},{1,3},{2,0},{3,1},{4,6},{5,7},{6,4},{7,5},{8,10},{9,11},{10,... | collective-permute-start | bytes 589832 | tf_op jit(solution)/shard_map/ppermute | solution.py:45
  19.3 19.5 %copy-start.27 = (bf16[96,1152]{1,0:T(8,128)(2,1)}, bf16[96,1152]{1,0:T(8,128)(2,1)S(1)}, u32[]{:S(2)}) copy-start(bf16[96,1152]{1,0:T(8,128)(2,1)S(1)} %fusion.32.refs_0_) | copy-start | bytes 663556
  19.3 11.9 %collective-permute-start.7 = (bf16[96,1152]{1,0:T(8,128)(2,1)S(1)}, bf16[96,1152]{1,0:T(8,128)(2,1)S(1)}, u32[]{:S(2)}, u32[]{:S(2)}) collective-permute-start(bf16[96,1152]{1,0:T(8,128)(2,1)S(1)} %fusion.32.refs_0_), channel_id=1, source_target_pairs={{0,8},{1,9},{2,10},{3,11},{4,12},{5,13},{6,14},{7,15},{8,0},{9,1},... | collective-permute-start | bytes 663560 | tf_op jit(solution)/shard_map/ppermute | solution.py:45
  20.8 11.6 %collective-permute-start.8 = (bf16[96,1152]{1,0:T(8,128)(2,1)S(1)}, bf16[96,1152]{1,0:T(8,128)(2,1)S(1)}, u32[]{:S(2)}, u32[]{:S(2)}) collective-permute-start(bf16[96,1152]{1,0:T(8,128)(2,1)S(1)} %fusion.32.refs_0_), channel_id=1, source_target_pairs={{0,16},{1,17},{2,18},{3,19},{4,20},{5,21},{6,22},{7,23},{8,24},{9,... | collective-permute-start | bytes 663560 | tf_op jit(solution)/shard_map/ppermute | solution.py:45
  22.4 10.1 %collective-permute-start.9 = (bf16[96,1152]{1,0:T(8,128)(2,1)S(1)}, bf16[96,1152]{1,0:T(8,128)(2,1)S(1)}, u32[]{:S(2)}, u32[]{:S(2)}) collective-permute-start(bf16[96,1152]{1,0:T(8,128)(2,1)S(1)} %fusion.32.refs_0_), channel_id=1, source_target_pairs={{0,24},{1,25},{2,26},{3,27},{4,28},{5,29},{6,30},{7,31},{8,16},{9,... | collective-permute-start | bytes 663560 | tf_op jit(solution)/shard_map/ppermute | solution.py:45
  22.8 10.1 %collective-permute-start.1 = (bf16[128,768]{1,0:T(8,128)(2,1)S(1)}, bf16[128,768]{1,0:T(8,128)(2,1)S(1)}, u32[]{:S(2)}, u32[]{:S(2)}) collective-permute-start(bf16[128,768]{1,0:T(8,128)(2,1)S(1)} %get-tuple-element.214), channel_id=1, source_target_pairs={{0,1},{1,0},{2,3},{3,2},{4,5},{5,4},{6,7},{7,6},{8,9},{9,8},{10,11... | collective-permute-start | bytes 589832 | tf_op jit(solution)/shard_map/ppermute | solution.py:45
  30.0 8.6 %collective-permute-start.3 = (bf16[128,768]{1,0:T(8,128)(2,1)S(1)}, bf16[128,768]{1,0:T(8,128)(2,1)S(1)}, u32[]{:S(2)}, u32[]{:S(2)}) collective-permute-start(bf16[128,768]{1,0:T(8,128)(2,1)S(1)} %collective-permute-done.2), channel_id=1, source_target_pairs={{0,1},{1,0},{2,3},{3,2},{4,5},{5,4},{6,7},{7,6},{8,9},{9,8},{10,11... | collective-permute-start | bytes 589832 | tf_op jit(solution)/shard_map/ppermute | solution.py:45
  33.0 6.9 %collective-permute-start.10 = (bf16[96,1152]{1,0:T(8,128)(2,1)S(1)}, bf16[96,1152]{1,0:T(8,128)(2,1)S(1)}, u32[]{:S(2)}, u32[]{:S(2)}) collective-permute-start(bf16[96,1152]{1,0:T(8,128)(2,1)S(1)} %fusion.32.refs_0_), channel_id=1, source_target_pairs={{0,4},{1,5},{2,6},{3,7},{4,0},{5,1},{6,2},{7,3},{8,12},{9,13},{10,... | collective-permute-start | bytes 663560 | tf_op jit(solution)/shard_map/ppermute | solution.py:45
  33.0 6.9 %collective-permute-start.11 = (bf16[96,1152]{1,0:T(8,128)(2,1)S(1)}, bf16[96,1152]{1,0:T(8,128)(2,1)S(1)}, u32[]{:S(2)}, u32[]{:S(2)}) collective-permute-start(bf16[96,1152]{1,0:T(8,128)(2,1)S(1)} %collective-permute-done.7.refs_1_), channel_id=1, source_target_pairs={{0,4},{1,5},{2,6},{3,7},{4,0},{5,1},{6,2},{7,3},{8,12},{9,13},{10,... | collective-permute-start | bytes 663560 | tf_op jit(solution)/shard_map/ppermute | solution.py:45
  33.5 6.4 %collective-permute-start.12 = (bf16[96,1152]{1,0:T(8,128)(2,1)S(1)}, bf16[96,1152]{1,0:T(8,128)(2,1)S(1)}, u32[]{:S(2)}, u32[]{:S(2)}) collective-permute-start(bf16[96,1152]{1,0:T(8,128)(2,1)S(1)} %collective-permute-done.8.refs_2_), channel_id=1, source_target_pairs={{0,4},{1,5},{2,6},{3,7},{4,0},{5,1},{6,2},{7,3},{8,12},{9,13},{10,... | collective-permute-start | bytes 663560 | tf_op jit(solution)/shard_map/ppermute | solution.py:45
  33.5 6.4 %collective-permute-start.13 = (bf16[96,1152]{1,0:T(8,128)(2,1)S(1)}, bf16[96,1152]{1,0:T(8,128)(2,1)}, u32[]{:S(2)}, u32[]{:S(2)}) collective-permute-start(bf16[96,1152]{1,0:T(8,128)(2,1)S(1)} %collective-permute-done.9.refs_3_), channel_id=1, source_target_pairs={{0,4},{1,5},{2,6},{3,7},{4,0},{5,1},{6,2},{7,3},{8,12},{9,13},{10,... | collective-permute-start | bytes 663560 | tf_op jit(solution)/shard_map/ppermute | solution.py:45
  34.0 25.8 %all-to-all-start = ((bf16[32,16,768]{2,1,0:T(8,128)(2,1)}), bf16[32,16,768]{2,1,0:T(8,128)(2,1)S(1)}, u32[]{:S(2)}, u32[]{:S(2)}) async-start(bf16[32,16,768]{2,1,0:T(8,128)(2,1)} %bitcast.11), calls=%async_computation | async-start | bytes 1572864 | tf_op jit(solution)/shard_map/all_to_all | solution.py:793
  45.4 3.8 %collective-permute-start.14 = (bf16[512,768]{1,0:T(8,128)(2,1)}, bf16[512,768]{1,0:T(8,128)(2,1)S(1)}, u32[]{:S(2)}, u32[]{:S(2)}) collective-permute-start(bf16[512,768]{1,0:T(8,128)(2,1)} %get-tuple-element.119.key_ref.value_ref), channel_id=1, source_target_pairs={{0,4},{1,5},{2,6},{3,7},{4,0},{5,1},{6,2},{7,3},{8,12},{9,13},{10,... | collective-permute-start | bytes 2359304 | tf_op jit(solution)/shard_map/ppermute | solution.py:45
  45.7 12.3 %collective-permute-start.15 = (bf16[96,896]{1,0:T(8,128)(2,1)S(1)}, bf16[96,896]{1,0:T(8,128)(2,1)S(1)}, u32[]{:S(2)}, u32[]{:S(2)}) collective-permute-start(bf16[96,896]{1,0:T(8,128)(2,1)S(1)} %fusion.33.refs_0_), channel_id=1, source_target_pairs={{0,8},{1,9},{2,10},{3,11},{4,12},{5,13},{6,14},{7,15},{8,0},{9,1},... | collective-permute-start | bytes 516104 | tf_op jit(solution)/shard_map/ppermute | solution.py:45
  47.4 11.1 %collective-permute-start.16 = (bf16[96,896]{1,0:T(8,128)(2,1)S(1)}, bf16[96,896]{1,0:T(8,128)(2,1)S(1)}, u32[]{:S(2)}, u32[]{:S(2)}) collective-permute-start(bf16[96,896]{1,0:T(8,128)(2,1)S(1)} %fusion.33.refs_0_), channel_id=1, source_target_pairs={{0,16},{1,17},{2,18},{3,19},{4,20},{5,21},{6,22},{7,23},{8,24},{9,... | collective-permute-start | bytes 516104 | tf_op jit(solution)/shard_map/ppermute | solution.py:45
  48.9 10.9 %collective-permute-start.17 = (bf16[96,896]{1,0:T(8,128)(2,1)S(1)}, bf16[96,896]{1,0:T(8,128)(2,1)S(1)}, u32[]{:S(2)}, u32[]{:S(2)}) collective-permute-start(bf16[96,896]{1,0:T(8,128)(2,1)S(1)} %fusion.33.refs_0_), channel_id=1, source_target_pairs={{0,24},{1,25},{2,26},{3,27},{4,28},{5,29},{6,30},{7,31},{8,16},{9,... | collective-permute-start | bytes 516104 | tf_op jit(solution)/shard_map/ppermute | solution.py:45
  59.8 14.8 %copy-start.10 = (bf16[128,384]{1,0:T(8,128)(2,1)S(1)}, bf16[128,384]{1,0:T(8,128)(2,1)}, u32[]{:S(2)}) copy-start(bf16[128,384]{1,0:T(8,128)(2,1)} %get-tuple-element.126.zero_ref.refs_4_) | copy-start | bytes 294916
  59.8 14.8 %copy-start.11 = (s32[5]{0:T(128)S(1)}, s32[5]{0:T(128)}, u32[]{:S(2)}) copy-start(s32[5]{0:T(128)} %stack.23.flags_ref) | copy-start | bytes 64
  59.9 4.7 %collective-permute-start.20 = (bf16[384,896]{1,0:T(8,128)(2,1)S(1)}, bf16[384,896]{1,0:T(8,128)(2,1)S(1)}, u32[]{:S(2)}, u32[]{:S(2)}) collective-permute-start(bf16[384,896]{1,0:T(8,128)(2,1)S(1)} %pad_maximum_fusion.1), channel_id=1, source_target_pairs={{0,4},{1,5},{2,6},{3,7},{4,0},{5,1},{6,2},{7,3},{8,12},{9,13},{10,... | collective-permute-start | bytes 2064392 | tf_op jit(solution)/shard_map/ppermute | solution.py:45
  60.8 9.4 %collective-permute-start.18 = (bf16[128,384]{1,0:T(8,128)(2,1)S(1)}, bf16[128,384]{1,0:T(8,128)(2,1)S(1)}, u32[]{:S(2)}, u32[]{:S(2)}) collective-permute-start(bf16[128,384]{1,0:T(8,128)(2,1)S(1)} %copy-done.46), channel_id=1, source_target_pairs={{0,1},{1,0},{2,3},{3,2},{4,5},{5,4},{6,7},{7,6},{8,9},{9,8},{10,11... | collective-permute-start | bytes 294920 | tf_op jit(solution)/shard_map/ppermute | solution.py:45
  63.5 7.8 %collective-permute-start.19 = (bf16[128,384]{1,0:T(8,128)(2,1)S(1)}, bf16[128,384]{1,0:T(8,128)(2,1)S(1)}, u32[]{:S(2)}, u32[]{:S(2)}) collective-permute-start(bf16[128,384]{1,0:T(8,128)(2,1)S(1)} %copy-done.47), channel_id=1, source_target_pairs={{0,2},{1,3},{2,0},{3,1},{4,6},{5,7},{6,4},{7,5},{8,10},{9,11},{10,... | collective-permute-start | bytes 294920 | tf_op jit(solution)/shard_map/ppermute | solution.py:45
  68.2 6.5 %collective-permute-start.21 = (bf16[128,384]{1,0:T(8,128)(2,1)S(1)}, bf16[128,384]{1,0:T(8,128)(2,1)S(1)}, u32[]{:S(2)}, u32[]{:S(2)}) collective-permute-start(bf16[128,384]{1,0:T(8,128)(2,1)S(1)} %copy-done.48), channel_id=1, source_target_pairs={{0,3},{1,2},{2,1},{3,0},{4,7},{5,6},{6,5},{7,4},{8,11},{9,10},{10,... | collective-permute-start | bytes 294920 | tf_op jit(solution)/shard_map/ppermute | solution.py:45
  75.9 1.4 collective-permute-start.22
  81.7 23.4 %all-to-all-start.1 = ((bf16[32,16,768]{2,1,0:T(8,128)(2,1)}), bf16[32,16,768]{2,1,0:T(8,128)(2,1)S(1)}, u32[]{:S(2)}, u32[]{:S(2)}) async-start(bf16[32,16,768]{2,1,0:T(8,128)(2,1)} %bitcast.76), calls=%async_computation.1 | async-start | bytes 1572864 | tf_op jit(solution)/shard_map/all_to_all | solution.py:793
  117.9 24.0 %all-to-all-start.2 = ((bf16[32,16,768]{2,1,0:T(8,128)(2,1)}), bf16[32,16,768]{2,1,0:T(8,128)(2,1)S(1)}, u32[]{:S(2)}, u32[]{:S(2)}) async-start(bf16[32,16,768]{2,1,0:T(8,128)(2,1)} %bitcast.77), calls=%async_computation.2 | async-start | bytes 1572864 | tf_op jit(solution)/shard_map/all_to_all | solution.py:793
  147.2 2.7 %collective-permute-start.23 = (bf16[128,768]{1,0:T(8,128)(2,1)}, bf16[128,768]{1,0:T(8,128)(2,1)S(1)}, u32[]{:S(2)}, u32[]{:S(2)}) collective-permute-start(bf16[128,768]{1,0:T(8,128)(2,1)} %get-tuple-element.157), channel_id=1, source_target_pairs={{0,4},{1,5},{2,6},{3,7},{4,0},{5,1},{6,2},{7,3},{8,12},{9,13},{10,... | collective-permute-start | bytes 589832 | tf_op jit(solution)/shard_map/ppermute | solution.py:45
  152.1 5.1 %collective-permute-start.24 = (bf16[128,384]{1,0:T(8,128)(2,1)S(1)}, bf16[128,384]{1,0:T(8,128)(2,1)S(1)}, u32[]{:S(2)}, u32[]{:S(2)}) collective-permute-start(bf16[128,384]{1,0:T(8,128)(2,1)S(1)} %get-tuple-element.158), channel_id=1, source_target_pairs={{0,1},{1,0},{2,3},{3,2},{4,5},{5,4},{6,7},{7,6},{8,9},{9,8},{10,11... | collective-permute-start | bytes 294920 | tf_op jit(solution)/shard_map/ppermute | solution.py:45
  154.0 10.1 %collective-permute-start.25 = (bf16[128,384]{1,0:T(8,128)(2,1)S(1)}, bf16[128,384]{1,0:T(8,128)(2,1)S(1)}, u32[]{:S(2)}, u32[]{:S(2)}) collective-permute-start(bf16[128,384]{1,0:T(8,128)(2,1)S(1)} %get-tuple-element.159), channel_id=1, source_target_pairs={{0,2},{1,3},{2,0},{3,1},{4,6},{5,7},{6,4},{7,5},{8,10},{9,11},{10,... | collective-permute-start | bytes 294920 | tf_op jit(solution)/shard_map/ppermute | solution.py:45
  154.7 9.4 %collective-permute-start.26 = (bf16[128,384]{1,0:T(8,128)(2,1)S(1)}, bf16[128,384]{1,0:T(8,128)(2,1)S(1)}, u32[]{:S(2)}, u32[]{:S(2)}) collective-permute-start(bf16[128,384]{1,0:T(8,128)(2,1)S(1)} %get-tuple-element.160), channel_id=1, source_target_pairs={{0,3},{1,2},{2,1},{3,0},{4,7},{5,6},{6,5},{7,4},{8,11},{9,10},{10,... | collective-permute-start | bytes 294920 | tf_op jit(solution)/shard_map/ppermute | solution.py:45
  164.1 22.9 %all-to-all-start.3 = ((bf16[32,16,768]{2,1,0:T(8,128)(2,1)}), bf16[32,16,768]{2,1,0:T(8,128)(2,1)}, u32[]{:S(2)}, u32[]{:S(2)}) async-start(bf16[32,16,768]{2,1,0:T(8,128)(2,1)} %bitcast.21), calls=%async_computation.3 | async-start | bytes 1572864 | tf_op jit(solution)/shard_map/all_to_all | solution.py:793
  176.7 2.6 %collective-permute-start.27 = (bf16[2,512,384]{2,1,0:T(8,128)(2,1)}, bf16[2,512,384]{2,1,0:T(8,128)(2,1)S(1)}, u32[]{:S(2)}, u32[]{:S(2)}) collective-permute-start(bf16[2,512,384]{2,1,0:T(8,128)(2,1)} %get-tuple-element.171), channel_id=1, source_target_pairs={{0,4},{1,5},{2,6},{3,7},{4,0},{5,1},{6,2},{7,3},{8,12},{9,13},{10,... | collective-permute-start | bytes 2359304 | tf_op jit(solution)/shard_map/ppermute | solution.py:45
  187.0 4.8 %collective-permute-start.28 = (bf16[384,2048]{1,0:T(8,128)(2,1)}, bf16[384,2048]{1,0:T(8,128)(2,1)S(1)}, u32[]{:S(2)}, u32[]{:S(2)}) collective-permute-start(bf16[384,2048]{1,0:T(8,128)(2,1)} %get-tuple-element.179), channel_id=1, source_target_pairs={{0,4},{1,5},{2,6},{3,7},{4,0},{5,1},{6,2},{7,3},{8,12},{9,13},{10,... | collective-permute-start | bytes 4718600 | tf_op jit(solution)/shard_map/ppermute | solution.py:45
  192.8 7.1 %collective-permute-start.29 = (bf16[128,768]{1,0:T(8,128)(2,1)S(1)}, bf16[128,768]{1,0:T(8,128)(2,1)S(1)}, u32[]{:S(2)}, u32[]{:S(2)}) collective-permute-start(bf16[128,768]{1,0:T(8,128)(2,1)S(1)} %get-tuple-element.213), channel_id=1, source_target_pairs={{0,1},{1,0},{2,3},{3,2},{4,5},{5,4},{6,7},{7,6},{8,9},{9,8},{10,11... | collective-permute-start | bytes 589832 | tf_op jit(solution)/shard_map/ppermute | solution.py:45
  194.7 18.7 %collective-permute-start.32 = (bf16[96,2048]{1,0:T(8,128)(2,1)S(1)}, bf16[96,2048]{1,0:T(8,128)(2,1)S(1)}, u32[]{:S(2)}, u32[]{:S(2)}) collective-permute-start(bf16[96,2048]{1,0:T(8,128)(2,1)S(1)} %get-tuple-element.207), channel_id=1, source_target_pairs={{0,8},{1,9},{2,10},{3,11},{4,12},{5,13},{6,14},{7,15},{8,0},{9,1},... | collective-permute-start | bytes 1179656 | tf_op jit(solution)/shard_map/ppermute | solution.py:45
  194.8 19.5 %collective-permute-start.33 = (bf16[96,2048]{1,0:T(8,128)(2,1)S(1)}, bf16[96,2048]{1,0:T(8,128)(2,1)S(1)}, u32[]{:S(2)}, u32[]{:S(2)}) collective-permute-start(bf16[96,2048]{1,0:T(8,128)(2,1)S(1)} %get-tuple-element.206), channel_id=1, source_target_pairs={{0,16},{1,17},{2,18},{3,19},{4,20},{5,21},{6,22},{7,23},{8,24},{9,... | collective-permute-start | bytes 1179656 | tf_op jit(solution)/shard_map/ppermute | solution.py:45
  196.2 18.1 %collective-permute-start.34 = (bf16[96,2048]{1,0:T(8,128)(2,1)S(1)}, bf16[96,2048]{1,0:T(8,128)(2,1)S(1)}, u32[]{:S(2)}, u32[]{:S(2)}) collective-permute-start(bf16[96,2048]{1,0:T(8,128)(2,1)S(1)} %get-tuple-element.205), channel_id=1, source_target_pairs={{0,24},{1,25},{2,26},{3,27},{4,28},{5,29},{6,30},{7,31},{8,16},{9,... | collective-permute-start | bytes 1179656 | tf_op jit(solution)/shard_map/ppermute | solution.py:45
  198.3 15.1 %collective-permute-start.30 = (bf16[128,768]{1,0:T(8,128)(2,1)S(1)}, bf16[128,768]{1,0:T(8,128)(2,1)S(1)}, u32[]{:S(2)}, u32[]{:S(2)}) collective-permute-start(bf16[128,768]{1,0:T(8,128)(2,1)S(1)} %get-tuple-element.212), channel_id=1, source_target_pairs={{0,2},{1,3},{2,0},{3,1},{4,6},{5,7},{6,4},{7,5},{8,10},{9,11},{10,... | collective-permute-start | bytes 589832 | tf_op jit(solution)/shard_map/ppermute | solution.py:45
  199.9 13.5 %collective-permute-start.31 = (bf16[128,768]{1,0:T(8,128)(2,1)S(1)}, bf16[128,768]{1,0:T(8,128)(2,1)S(1)}, u32[]{:S(2)}, u32[]{:S(2)}) collective-permute-start(bf16[128,768]{1,0:T(8,128)(2,1)S(1)} %get-tuple-element.211), channel_id=1, source_target_pairs={{0,3},{1,2},{2,1},{3,0},{4,7},{5,6},{6,5},{7,4},{8,11},{9,10},{10,... | collective-permute-start | bytes 589832 | tf_op jit(solution)/shard_map/ppermute | solution.py:45
  214.6 4.0 %collective-permute-start.35 = (bf16[128,768]{1,0:T(8,128)(2,1)S(1)}, bf16[128,768]{1,0:T(8,128)(2,1)S(1)}, u32[]{:S(2)}, u32[]{:S(2)}) collective-permute-start(bf16[128,768]{1,0:T(8,128)(2,1)S(1)} %broadcast_select_fusion.6), channel_id=1, source_target_pairs={{0,4},{1,5},{2,6},{3,7},{4,0},{5,1},{6,2},{7,3},{8,12},{9,13},{10,... | collective-permute-start | bytes 589832 | tf_op jit(solution)/shard_map/ppermute | solution.py:45
  214.7 8.0 %collective-permute-start.36 = (bf16[24,2048]{1,0:T(8,128)(2,1)S(1)}, bf16[24,2048]{1,0:T(8,128)(2,1)S(1)}, u32[]{:S(2)}, u32[]{:S(2)}) collective-permute-start(bf16[24,2048]{1,0:T(8,128)(2,1)S(1)} %get-tuple-element.210), channel_id=1, source_target_pairs={{0,1},{1,0},{2,3},{3,2},{4,5},{5,4},{6,7},{7,6},{8,9},{9,8},{10,11... | collective-permute-start | bytes 294920 | tf_op jit(solution)/shard_map/ppermute | solution.py:45
  218.6 10.5 %collective-permute-start.37 = (bf16[24,2048]{1,0:T(8,128)(2,1)S(1)}, bf16[24,2048]{1,0:T(8,128)(2,1)S(1)}, u32[]{:S(2)}, u32[]{:S(2)}) collective-permute-start(bf16[24,2048]{1,0:T(8,128)(2,1)S(1)} %get-tuple-element.209), channel_id=1, source_target_pairs={{0,2},{1,3},{2,0},{3,1},{4,6},{5,7},{6,4},{7,5},{8,10},{9,11},{10,... | collective-permute-start | bytes 294920 | tf_op jit(solution)/shard_map/ppermute | solution.py:45
  220.3 8.8 %collective-permute-start.38 = (bf16[24,2048]{1,0:T(8,128)(2,1)S(1)}, bf16[24,2048]{1,0:T(8,128)(2,1)S(1)}, u32[]{:S(2)}, u32[]{:S(2)}) collective-permute-start(bf16[24,2048]{1,0:T(8,128)(2,1)S(1)} %get-tuple-element.192), channel_id=1, source_target_pairs={{0,3},{1,2},{2,1},{3,0},{4,7},{5,6},{6,5},{7,4},{8,11},{9,10},{10,... | collective-permute-start | bytes 294920 | tf_op jit(solution)/shard_map/ppermute | solution.py:45
  (47 other events, 269.8 us)

commit v4 on v3

--- a/solution.py
+++ b/solution.py
@@ -114,7 +114,7 @@
     rows = block.shape[0] // links.levels
     parts = [rows_of(block, links.level ^ b, rows) for b in range(links.levels)]
     sent = [part.astype(BF) for part in parts[1:]]
-    sent[-1] = gate(sent[-1], before_last)
+    sent[0] = gate(sent[0], before_last)
     got = tie(*[links.swap_level(part, b + 1) for b, part in enumerate(sent)])
     return [parts[0], *got]
 
@@ -878,9 +878,9 @@
         full_extra = in_order(links, own_extra, other_parts)
         gain_two = full_extra[:, width + 2 * experts].astype(F32)[None]
     full_router = full_extra[:, width : width + experts]
-    last_part = gate(mixed_parts[3], gain_two)
-    back = [links.swap_level(mixed_parts[1], 1), links.swap_level(mixed_parts[2], 2)]
-    back = tie(*back, links.swap_level(last_part, 3))
+    last_part = gate(mixed_parts[1], gain_two)
+    back = [links.swap_level(mixed_parts[2], 2), links.swap_level(mixed_parts[3], 3)]
+    back = tie(links.swap_level(last_part, 1), *back)
     tallies = full_extra[::own_rows, width + experts : width + 2 * experts].astype(F32)
     mine_only = (jnp.arange(experts, dtype=jnp.int32) == device).astype(F32)[None, :]
     counts = jnp.sum(tallies * mine_only, axis=1).astype(jnp.int32)

time: 232 us -> 230 us (level)
  transfers between devices with their start and end apart: 43 -> 43, of which waited for: 19 -> 20; matrix products, arithmetic and copies ran while one was open for 17% -> 17% of each run, Pallas kernels for 15% -> 15%
where the time goes in v4:
time: 230 us; the launch traced here: 229 us
  starting transfers between devices  62 us (27%)
  Pallas kernels  58.8 us (26%)
  waiting for transfers between devices  54.7 us (24%)
  matrix products  24.8 us (11%)
  local copies, waits for them, and re-layouts  14.6 us (6%)
  other arithmetic  13.1 us (6%)
    ppermute x39, starting transfers between devices, permute(): return lax.ppermute(array, AXES, pairs)  45.4 us
    ppermute x39, waiting for transfers between devices, permute(): return lax.ppermute(array, AXES, pairs)  43.9 us
    pallas_call x9, Pallas kernels, one_step(): pl.pallas_call(kernel, grid=(1,), in_specs=[FLAGS] + [whole(operand.shape...  24.3 us
    all_to_all x4, starting transfers between devices, all_to_all(): return lax.all_to_all(array, AXES, split_axis=0, concat_axis=0, tiled=True)  16.6 us
    dot_general x3, matrix products, dot_tn(): lax.dot_general(left, right, (((0,), (0,)), ((), ())), preferred_element_...  12.3 us
    pallas_call x1, Pallas kernels, expert_layer(): pl.pallas_call(expert_kernel, grid=(hidden_width // TILE,), in_specs=[FLA...  11.9 us
    all_to_all x4, waiting for transfers between devices, all_to_all(): return lax.all_to_all(array, AXES, split_axis=0, concat_axis=0, tiled=True)  10.8 us
    unnamed x104, local copies, waits for them, and re-layouts  10.5 us
  transfers between devices with their start and end apart: 43, of which 20 were waited for; matrix products, arithmetic and copies ran while one was open for 17% of the time, Pallas kernels for 15%

profile of v4, /device:TPU:0, one launch (start us, length us, event | category | flops | bytes accessed | tf_op | source)
XLA Modules:
  0.0 229.4 jit_solution(5447260484895623483)
XLA Ops:
  1.3 1.7 shard_map.203
  2.9 3.0 %collective-permute-start.4 = (bf16[24,2048]{1,0:T(8,128)(2,1)}, bf16[24,2048]{1,0:T(8,128)(2,1)S(1)}, u32[]{:S(2)}, u32[]{:S(2)}) collective-permute-start(bf16[24,2048]{1,0:T(8,128)(2,1)} %get-tuple-element.108), channel_id=1, source_target_pairs={{0,1},{1,0},{2,3},{3,2},{4,5},{5,4},{6,7},{7,6},{8,9},{9,8},{10,11... | collective-permute-start | bytes 294920 | tf_op jit(solution)/shard_map/ppermute | solution.py:45
  5.9 2.5 %collective-permute-start.6 = (bf16[24,2048]{1,0:T(8,128)(2,1)}, bf16[24,2048]{1,0:T(8,128)(2,1)S(1)}, u32[]{:S(2)}, u32[]{:S(2)}) collective-permute-start(bf16[24,2048]{1,0:T(8,128)(2,1)} %get-tuple-element.108), channel_id=1, source_target_pairs={{0,3},{1,2},{2,1},{3,0},{4,7},{5,6},{6,5},{7,4},{8,11},{9,10},{10,... | collective-permute-start | bytes 294920 | tf_op jit(solution)/shard_map/ppermute | solution.py:45
  12.7 5.3 %collective-permute-done.5 = bf16[24,2048]{1,0:T(8,128)(2,1)S(1)} collective-permute-done((bf16[24,2048]{1,0:T(8,128)(2,1)}, bf16[24,2048]{1,0:T(8,128)(2,1)S(1)}, u32[]{:S(2)}, u32[]{:S(2)}) %collective-permute-start.5) | collective-permute-done | bytes 98336 | tf_op jit(solution)/shard_map/ppermute | solution.py:45
  19.3 1.6 collective-permute-start.7
  20.8 1.5 collective-permute-start.8
  22.8 2.7 %collective-permute-start.1 = (bf16[128,768]{1,0:T(8,128)(2,1)S(1)}, bf16[128,768]{1,0:T(8,128)(2,1)S(1)}, u32[]{:S(2)}, u32[]{:S(2)}) collective-permute-start(bf16[128,768]{1,0:T(8,128)(2,1)S(1)} %get-tuple-element.214), channel_id=1, source_target_pairs={{0,1},{1,0},{2,3},{3,2},{4,5},{5,4},{6,7},{7,6},{8,9},{9,8},{10,11... | collective-permute-start | bytes 589832 | tf_op jit(solution)/shard_map/ppermute | solution.py:45
  25.5 4.4 %collective-permute-done.2 = bf16[128,768]{1,0:T(8,128)(2,1)S(1)} collective-permute-done((bf16[128,768]{1,0:T(8,128)(2,1)S(1)}, bf16[128,768]{1,0:T(8,128)(2,1)S(1)}, u32[]{:S(2)}, u32[]{:S(2)}) %collective-permute-start.2) | collective-permute-done | bytes 196640 | tf_op jit(solution)/shard_map/ppermute | solution.py:45
  34.0 4.5 %all-to-all-start = ((bf16[32,16,768]{2,1,0:T(8,128)(2,1)}), bf16[32,16,768]{2,1,0:T(8,128)(2,1)S(1)}, u32[]{:S(2)}, u32[]{:S(2)}) async-start(bf16[32,16,768]{2,1,0:T(8,128)(2,1)} %bitcast.11), calls=%async_computation | async-start | bytes 1572864 | tf_op jit(solution)/shard_map/all_to_all | solution.py:793
  40.7 4.7 %shard_map.204 = (bf16[512,384]{1,0:T(8,128)(2,1)}, bf16[512,768]{1,0:T(8,128)(2,1)}, bf16[768,1152]{1,0:T(8,128)(2,1)}) custom-call(s32[5]{0:T(128)} %stack.23.flags_ref, bf16[512,768]{1,0:T(8,128)(2,1)} %fusion.3.normed_ref, bf16[96,1152]{1,0:T(8,128)(2,1)} %copy-done.27, bf16[96,1152]{1,0:T(8,128)(2,1)} %copy-done.35, bf16[96,1152]{1,0:T(8,128)(2,1)} %copy-done.36, ...), custom_call_target="tpu_custom_call" | custom-call | bytes 1048576 | tf_op jit(solution)/shard_map/pallas_call | solution.py:274
  45.7 1.7 collective-permute-start.15
  47.4 1.5 collective-permute-start.16
  50.1 7.8 %shard_map.205 = (bf16[128,384]{1,0:T(8,128)(2,1)}, bf16[128,384]{1,0:T(8,128)(2,1)}, bf16[128,384]{1,0:T(8,128)(2,1)}, bf16[128,384]{1,0:T(8,128)(2,1)}, bf16[6...) custom-call(bf16[512,384]{1,0:T(8,128)(2,1)} %get-tuple-element.118.query_ref, ...), custom_call_target="tpu_custom_call" | custom-call | flops 2000000000 | bytes 4096 | tf_op jit(solution)/shard_map/pallas_call | solution.py:180
  60.8 3.5 %collective-permute-start.20 = (bf16[128,384]{1,0:T(8,128)(2,1)S(1)}, bf16[128,384]{1,0:T(8,128)(2,1)S(1)}, u32[]{:S(2)}, u32[]{:S(2)}) collective-permute-start(bf16[128,384]{1,0:T(8,128)(2,1)S(1)} %copy-done.47), channel_id=1, source_target_pairs={{0,2},{1,3},{2,0},{3,1},{4,6},{5,7},{6,4},{7,5},{8,10},{9,11},{10,... | collective-permute-start | bytes 294920 | tf_op jit(solution)/shard_map/ppermute | solution.py:45
  64.3 1.5 collective-permute-start.21
  66.7 2.7 %shard_map.206 = (bf16[768,896]{1,0:T(8,128)(2,1)}, f32[1,768]{1,0:T(1,128)}) custom-call(s32[5]{0:T(128)} %stack.23.flags_ref, bf16[96,896]{1,0:T(8,128)(2,1)} %copy-done.26, bf16[96,896]{1,0:T(8,128)(2,1)} %copy-done.31, bf16[96,896]{1,0:T(8,128)(2,1)} %copy-done.32, bf16[96,896]{1,0:T(8,128)(2,1)} %copy-done.33, bf16[384,896]{1,0:T(8,128)(2,1)} %copy-done.30), custom_call_target="tpu_custom_call" | custom-call | bytes 1048576 | tf_op jit(solution)/shard_map/pallas_call | solution.py:274
  70.2 2.0 collective-permute-done.20.two_ref
  72.2 1.9 collective-permute-done.19.one_ref
  77.5 3.6 %shard_map.208 = (bf16[256,768]{1,0:T(8,128)(2,1)}, f32[256,768]{1,0:T(8,128)}, bf16[512,768]{1,0:T(8,128)(2,1)}) custom-call(s32[5]{0:T(128)} %stack.23.flags_ref, bf16[128,768]{1,0:T(8,128)(2,1)} %copy-done.5, bf16[128,768]{1,0:T(8,128)(2,1)} %copy-done.41, bf16[256,768]{1,0:T(8,128)(2,1)} %inputs_ref.1, bf16[768,896]{1,0:T(8,128)(2,1)} %get-tuple-element.141.weight_ref, ...), custom_call_target="tpu_custom_call" | custom-call | bytes 1048576 | tf_op jit(solution)/shard_map/pallas_call | solution.py:274
  81.1 4.1 %all-to-all-start.1 = ((bf16[32,16,768]{2,1,0:T(8,128)(2,1)}), bf16[32,16,768]{2,1,0:T(8,128)(2,1)S(1)}, u32[]{:S(2)}, u32[]{:S(2)}) async-start(bf16[32,16,768]{2,1,0:T(8,128)(2,1)} %bitcast.76), calls=%async_computation.1 | async-start | bytes 1572864 | tf_op jit(solution)/shard_map/all_to_all | solution.py:793
  85.3 1.6 slice.64.router_ref
  89.2 6.0 %shard_map.209 = (bf16[320,768]{1,0:T(8,128)(2,1)}, bf16[320,3072]{1,0:T(8,128)(2,1)}) custom-call(bf16[512,768]{1,0:T(8,128)(2,1)} %bitcast.73, bf16[320,512]{1,0:T(8,128)(2,1)} %fusion.25.compact_ref, bf16[1,3072,768]{2,1,0:T(8,128)(2,1)} %weight_out_ref.1), custom_call_target="tpu_custom_call" | custom-call | flops 1509949440 | bytes 9437184 | tf_op jit(solution)/shard_map/pallas_call | solution.py:560
  95.2 9.5 %all-to-all-done.1 = bf16[32,16,768]{2,1,0:T(8,128)(2,1)S(1)} async-done(((bf16[32,16,768]{2,1,0:T(8,128)(2,1)}), bf16[32,16,768]{2,1,0:T(8,128)(2,1)S(1)}, u32[]{:S(2)}, u32[]{:S(2)}) %all-to-all-start.1) | async-done | bytes 786464 | tf_op jit(solution)/shard_map/all_to_all | solution.py:793
  105.6 11.9 %shard_map.210 = (bf16[320,768]{1,0:T(8,128)(2,1)}, bf16[320,768]{1,0:T(8,128)(2,1)}, bf16[320,3072]{1,0:T(8,128)(2,1)}, bf16[320,3072]{1,0:T(8,128)(2,1)}, bf16...) custom-call(s32[5]{0:T(128)} %stack.23.flags_ref, bf16[512,768]{1,0:T(8,128)(2,1)} %bitcast.75, ...), custom_call_target="tpu_custom_call" | custom-call | flops 6039797760 | bytes 18874368 | tf_op jit(solution)/shard_map/pallas_call | solution.py:639
  117.5 4.4 %all-to-all-start.2 = ((bf16[32,16,768]{2,1,0:T(8,128)(2,1)}), bf16[32,16,768]{2,1,0:T(8,128)(2,1)S(1)}, u32[]{:S(2)}, u32[]{:S(2)}) async-start(bf16[32,16,768]{2,1,0:T(8,128)(2,1)} %bitcast.77), calls=%async_computation.2 | async-start | bytes 1572864 | tf_op jit(solution)/shard_map/all_to_all | solution.py:793
  122.3 6.9 %fusion.41 = f32[768,3072]{1,0:T(8,128)} fusion(bf16[320,768]{1,0:T(8,128)(2,1)S(1)} %copy-done.24, bf16[320,3072]{1,0:T(8,128)(2,1)} %get-tuple-element.152), kind=kOutput, calls=%fused_computation.94 | convolution fusion | flops 1509949440 | bytes 11894784 | tf_op jit(solution)/shard_map/dot_general | solution.py:24
  129.2 5.2 %fusion.42 = f32[3072,768]{1,0:T(8,128)} fusion(bf16[320,3072]{1,0:T(8,128)(2,1)S(1)} %copy-done.23, bf16[320,768]{1,0:T(8,128)(2,1)S(1)} %copy-done.34), kind=kOutput, calls=%fused_computation.95 | convolution fusion | flops 1509949440 | bytes 11894784 | tf_op jit(solution)/shard_map/dot_general | solution.py:24
  134.4 5.8 %convolution_convert_fusion = bf16[512,768]{1,0:T(8,128)(2,1)} fusion(bf16[320,3072]{1,0:T(8,128)(2,1)S(1)} %copy-done.23, bf16[1,3072,768]{2,1,0:T(8,128)(2,1)} %weight_out_ref.1, f32[320]{0:T(512)S(1)} %reduce.2, s32[512]{0:T(512)S(1)} %and_select_fusion), kind=kOutput, calls=%fused_computation.7 | convolution fusion | flops 1763147776 | bytes 7474432 | tf_op jit(solution)/shard_map/dot_general | solution.py:20
  142.3 4.4 %shard_map.211 = (f32[256,768]{1,0:T(8,128)}, bf16[256,768]{1,0:T(8,128)(2,1)}, bf16[128,768]{1,0:T(8,128)(2,1)}, bf16[128,768]{1,0:T(8,128)(2,1)}, bf16[16,768]{1,0:T(8,128)(2,1)}) custom-call(s32[5]{0:T(128)} %stack.23.flags_ref, bf16[512,768]{1,0:T(8,128)(2,1)} %bitcast.74, bf16[256,512]{1,0:T(8,128)(2,1)} %fusion.26.to_tokens_ref, ...), custom_call_target="tpu_custom_call" | custom-call | bytes 1048576 | tf_op jit(solution)/shard_map/pallas_call | solution.py:274
  146.8 1.5 collective-permute-start.23
  151.7 1.8 collective-permute-start.24
  154.3 1.8 collective-permute-start.26
  156.8 6.9 %collective-permute-done.25.refs_2_ = bf16[128,384]{1,0:T(8,128)(2,1)S(1)} collective-permute-done((bf16[128,384]{1,0:T(8,128)(2,1)S(1)}, bf16[128,384]{1,0:T(8,128)(2,1)S(1)}, u32[]{:S(2)}, u32[]{:S(2)}) %collective-permute-start.25) | collective-permute-done | bytes 98336 | tf_op jit(solution)/shard_map/ppermute | solution.py:45
  163.7 3.6 %all-to-all-start.3 = ((bf16[32,16,768]{2,1,0:T(8,128)(2,1)}), bf16[32,16,768]{2,1,0:T(8,128)(2,1)}, u32[]{:S(2)}, u32[]{:S(2)}) async-start(bf16[32,16,768]{2,1,0:T(8,128)(2,1)} %bitcast.21), calls=%async_computation.3 | async-start | bytes 1572864 | tf_op jit(solution)/shard_map/all_to_all | solution.py:793
  167.3 8.9 %shard_map.213 = (bf16[512,384]{1,0:T(8,128)(2,1)}, bf16[2,512,384]{2,1,0:T(8,128)(2,1)}, bf16[2,512,384]{2,1,0:T(8,128)(2,1)}) custom-call(bf16[512,384]{1,0:T(8,128)(2,1)} %get-tuple-element.118.query_ref, bf16[512,768]{1,0:T(8,128)(2,1)} %get-tuple-element.119.key_ref.value_ref, bf16[512,768]{1,0:T(8,128)(2,1)} %get-tuple-element.119.key_ref.value_ref, ...), custom_call_target="tpu_custom_call" | custom-call | flops 20000000000 | bytes 4096 | tf_op jit(solution)/shard_map/pallas_call | solution.py:231
  176.5 2.3 %collective-permute-done.27.got_ref = bf16[2,512,384]{2,1,0:T(8,128)(2,1)S(1)} collective-permute-done((bf16[2,512,384]{2,1,0:T(8,128)(2,1)}, bf16[2,512,384]{2,1,0:T(8,128)(2,1)S(1)}, u32[]{:S(2)}, u32[]{:S(2)}) %collective-permute-start.27) | collective-permute-done | bytes 786464 | tf_op jit(solution)/shard_map/ppermute | solution.py:45
  181.0 4.6 %shard_map.214 = (bf16[512,1152]{1,0:T(8,128)(2,1)S(1)}, f32[384,2048]{1,0:T(8,128)}, bf16[384,2048]{1,0:T(8,128)(2,1)}) custom-call(s32[5]{0:T(128)S(1)} %copy-done.12, bf16[512,768]{1,0:T(8,128)(2,1)S(1)} %copy-done, bf16[512,384]{1,0:T(8,128)(2,1)S(1)} %copy-done.4, bf16[2,512,384]{2,1,0:T(8,128)(2,1)S(1)} %copy-done.1, ...), custom_call_target="tpu_custom_call" | custom-call | bytes 1048576 | tf_op jit(solution)/shard_map/pallas_call | solution.py:274
  186.6 1.5 collective-permute-start.28
  188.3 3.2 %convolution_convert_fusion.2 = bf16[512,768]{1,0:T(8,128)(2,1)S(1)} fusion(bf16[512,1152]{1,0:T(8,128)(2,1)} %copy-done.15, bf16[768,1152]{1,0:T(8,128)(2,1)} %get-tuple-element.176), kind=kOutput, calls=%fused_computation.9 | convolution fusion | flops 906362880 | bytes 3735552 | tf_op jit(solution)/shard_map/dot_general | solution.py:28
  192.4 1.8 collective-permute-start.29
  195.8 2.0 collective-permute-start.34
  199.5 3.3 %collective-permute-start.31 = (bf16[128,768]{1,0:T(8,128)(2,1)S(1)}, bf16[128,768]{1,0:T(8,128)(2,1)S(1)}, u32[]{:S(2)}, u32[]{:S(2)}) collective-permute-start(bf16[128,768]{1,0:T(8,128)(2,1)S(1)} %get-tuple-element.211), channel_id=1, source_target_pairs={{0,3},{1,2},{2,1},{3,0},{4,7},{5,6},{6,5},{7,4},{8,11},{9,10},{10,... | collective-permute-start | bytes 589832 | tf_op jit(solution)/shard_map/ppermute | solution.py:45
  202.8 2.3 %fusion.16 = bf16[256,768]{1,0:T(8,128)(2,1)} fusion(f32[256,768]{1,0:T(8,128)S(1)} %copy-done.20, bf16[512,768]{1,0:T(8,128)(2,1)} %bitcast.22, s32[256]{0:T(256)S(1)} %bitcast.83), kind=kOutput, calls=%fused_computation.15 | convolution fusion | flops 201850880 | bytes 1967104 | tf_op jit(solution)/shard_map/dot_general | solution.py:20
  205.1 7.8 %collective-permute-done.30 = bf16[128,768]{1,0:T(8,128)(2,1)S(1)} collective-permute-done((bf16[128,768]{1,0:T(8,128)(2,1)S(1)}, bf16[128,768]{1,0:T(8,128)(2,1)S(1)}, u32[]{:S(2)}, u32[]{:S(2)}) %collective-permute-start.30) | collective-permute-done | bytes 196640 | tf_op jit(solution)/shard_map/ppermute | solution.py:45
  214.3 3.6 %collective-permute-start.37 = (bf16[24,2048]{1,0:T(8,128)(2,1)S(1)}, bf16[24,2048]{1,0:T(8,128)(2,1)S(1)}, u32[]{:S(2)}, u32[]{:S(2)}) collective-permute-start(bf16[24,2048]{1,0:T(8,128)(2,1)S(1)} %get-tuple-element.209), channel_id=1, source_target_pairs={{0,2},{1,3},{2,0},{3,1},{4,6},{5,7},{6,4},{7,5},{8,10},{9,11},{10,... | collective-permute-start | bytes 294920 | tf_op jit(solution)/shard_map/ppermute | solution.py:45
  217.9 2.6 %collective-permute-start.38 = (bf16[24,2048]{1,0:T(8,128)(2,1)S(1)}, bf16[24,2048]{1,0:T(8,128)(2,1)S(1)}, u32[]{:S(2)}, u32[]{:S(2)}) collective-permute-start(bf16[24,2048]{1,0:T(8,128)(2,1)S(1)} %get-tuple-element.208), channel_id=1, source_target_pairs={{0,3},{1,2},{2,1},{3,0},{4,7},{5,6},{6,5},{7,4},{8,11},{9,10},{10,... | collective-permute-start | bytes 294920 | tf_op jit(solution)/shard_map/ppermute | solution.py:45
  222.2 4.0 %collective-permute-done.38.three_ref = bf16[24,2048]{1,0:T(8,128)(2,1)S(1)} collective-permute-done((bf16[24,2048]{1,0:T(8,128)(2,1)S(1)}, bf16[24,2048]{1,0:T(8,128)(2,1)S(1)}, u32[]{:S(2)}, u32[]{:S(2)}) %collective-permute-start.38) | collective-permute-done | bytes 98336 | tf_op jit(solution)/shard_map/ppermute | solution.py:45
  226.3 1.7 collective-permute-done.36.one_ref
  (216 shorter events, 44.9 us)
Async XLA Ops:
  0.6 18.4 %copy-start.17 = (bf16[256,768]{1,0:T(8,128)(2,1)S(1)}, bf16[256,768]{1,0:T(8,128)(2,1)}, u32[]{:S(2)}) copy-start(bf16[256,768]{1,0:T(8,128)(2,1)} %inputs_ref.1) | copy-start | bytes 1179652
  2.9 9.8 %collective-permute-start.4 = (bf16[24,2048]{1,0:T(8,128)(2,1)}, bf16[24,2048]{1,0:T(8,128)(2,1)S(1)}, u32[]{:S(2)}, u32[]{:S(2)}) collective-permute-start(bf16[24,2048]{1,0:T(8,128)(2,1)} %get-tuple-element.108), channel_id=1, source_target_pairs={{0,1},{1,0},{2,3},{3,2},{4,5},{5,4},{6,7},{7,6},{8,9},{9,8},{10,11... | collective-permute-start | bytes 294920 | tf_op jit(solution)/shard_map/ppermute | solution.py:45
  5.9 12.0 %collective-permute-start.6 = (bf16[24,2048]{1,0:T(8,128)(2,1)}, bf16[24,2048]{1,0:T(8,128)(2,1)S(1)}, u32[]{:S(2)}, u32[]{:S(2)}) collective-permute-start(bf16[24,2048]{1,0:T(8,128)(2,1)} %get-tuple-element.108), channel_id=1, source_target_pairs={{0,3},{1,2},{2,1},{3,0},{4,7},{5,6},{6,5},{7,4},{8,11},{9,10},{10,... | collective-permute-start | bytes 294920 | tf_op jit(solution)/shard_map/ppermute | solution.py:45
  9.5 9.5 %collective-permute-start = (bf16[128,768]{1,0:T(8,128)(2,1)S(1)}, bf16[128,768]{1,0:T(8,128)(2,1)S(1)}, u32[]{:S(2)}, u32[]{:S(2)}) collective-permute-start(bf16[128,768]{1,0:T(8,128)(2,1)S(1)} %broadcast_select_fusion.4), channel_id=1, source_target_pairs={{0,4},{1,5},{2,6},{3,7},{4,0},{5,1},{6,2},{7,3},{8,12},{9,13},{10,... | collective-permute-start | bytes 589832 | tf_op jit(solution)/shard_map/ppermute | solution.py:45
  9.5 8.4 %collective-permute-start.5 = (bf16[24,2048]{1,0:T(8,128)(2,1)}, bf16[24,2048]{1,0:T(8,128)(2,1)S(1)}, u32[]{:S(2)}, u32[]{:S(2)}) collective-permute-start(bf16[24,2048]{1,0:T(8,128)(2,1)} %get-tuple-element.107), channel_id=1, source_target_pairs={{0,2},{1,3},{2,0},{3,1},{4,6},{5,7},{6,4},{7,5},{8,10},{9,11},{10,... | collective-permute-start | bytes 294920 | tf_op jit(solution)/shard_map/ppermute | solution.py:45
  12.7 17.3 %copy-start.25 = (bf16[256,768]{1,0:T(8,128)(2,1)S(1)}, bf16[256,768]{1,0:T(8,128)(2,1)}, u32[]{:S(2)}) copy-start(bf16[256,768]{1,0:T(8,128)(2,1)} %cotangent_ref.1) | copy-start | bytes 1179652
  19.1 10.9 %collective-permute-start.2 = (bf16[128,768]{1,0:T(8,128)(2,1)S(1)}, bf16[128,768]{1,0:T(8,128)(2,1)S(1)}, u32[]{:S(2)}, u32[]{:S(2)}) collective-permute-start(bf16[128,768]{1,0:T(8,128)(2,1)S(1)} %get-tuple-element.215), channel_id=1, source_target_pairs={{0,2},{1,3},{2,0},{3,1},{4,6},{5,7},{6,4},{7,5},{8,10},{9,11},{10,... | collective-permute-start | bytes 589832 | tf_op jit(solution)/shard_map/ppermute | solution.py:45
  19.3 19.5 %copy-start.27 = (bf16[96,1152]{1,0:T(8,128)(2,1)}, bf16[96,1152]{1,0:T(8,128)(2,1)S(1)}, u32[]{:S(2)}) copy-start(bf16[96,1152]{1,0:T(8,128)(2,1)S(1)} %fusion.32.refs_0_) | copy-start | bytes 663556
  19.3 11.9 %collective-permute-start.7 = (bf16[96,1152]{1,0:T(8,128)(2,1)S(1)}, bf16[96,1152]{1,0:T(8,128)(2,1)S(1)}, u32[]{:S(2)}, u32[]{:S(2)}) collective-permute-start(bf16[96,1152]{1,0:T(8,128)(2,1)S(1)} %fusion.32.refs_0_), channel_id=1, source_target_pairs={{0,8},{1,9},{2,10},{3,11},{4,12},{5,13},{6,14},{7,15},{8,0},{9,1},... | collective-permute-start | bytes 663560 | tf_op jit(solution)/shard_map/ppermute | solution.py:45
  20.8 11.6 %collective-permute-start.8 = (bf16[96,1152]{1,0:T(8,128)(2,1)S(1)}, bf16[96,1152]{1,0:T(8,128)(2,1)S(1)}, u32[]{:S(2)}, u32[]{:S(2)}) collective-permute-start(bf16[96,1152]{1,0:T(8,128)(2,1)S(1)} %fusion.32.refs_0_), channel_id=1, source_target_pairs={{0,16},{1,17},{2,18},{3,19},{4,20},{5,21},{6,22},{7,23},{8,24},{9,... | collective-permute-start | bytes 663560 | tf_op jit(solution)/shard_map/ppermute | solution.py:45
  22.4 10.1 %collective-permute-start.9 = (bf16[96,1152]{1,0:T(8,128)(2,1)S(1)}, bf16[96,1152]{1,0:T(8,128)(2,1)S(1)}, u32[]{:S(2)}, u32[]{:S(2)}) collective-permute-start(bf16[96,1152]{1,0:T(8,128)(2,1)S(1)} %fusion.32.refs_0_), channel_id=1, source_target_pairs={{0,24},{1,25},{2,26},{3,27},{4,28},{5,29},{6,30},{7,31},{8,16},{9,... | collective-permute-start | bytes 663560 | tf_op jit(solution)/shard_map/ppermute | solution.py:45
  22.8 10.1 %collective-permute-start.1 = (bf16[128,768]{1,0:T(8,128)(2,1)S(1)}, bf16[128,768]{1,0:T(8,128)(2,1)S(1)}, u32[]{:S(2)}, u32[]{:S(2)}) collective-permute-start(bf16[128,768]{1,0:T(8,128)(2,1)S(1)} %get-tuple-element.214), channel_id=1, source_target_pairs={{0,1},{1,0},{2,3},{3,2},{4,5},{5,4},{6,7},{7,6},{8,9},{9,8},{10,11... | collective-permute-start | bytes 589832 | tf_op jit(solution)/shard_map/ppermute | solution.py:45
  30.0 8.6 %collective-permute-start.3 = (bf16[128,768]{1,0:T(8,128)(2,1)S(1)}, bf16[128,768]{1,0:T(8,128)(2,1)S(1)}, u32[]{:S(2)}, u32[]{:S(2)}) collective-permute-start(bf16[128,768]{1,0:T(8,128)(2,1)S(1)} %collective-permute-done.2), channel_id=1, source_target_pairs={{0,1},{1,0},{2,3},{3,2},{4,5},{5,4},{6,7},{7,6},{8,9},{9,8},{10,11... | collective-permute-start | bytes 589832 | tf_op jit(solution)/shard_map/ppermute | solution.py:45
  33.0 6.9 %collective-permute-start.10 = (bf16[96,1152]{1,0:T(8,128)(2,1)S(1)}, bf16[96,1152]{1,0:T(8,128)(2,1)S(1)}, u32[]{:S(2)}, u32[]{:S(2)}) collective-permute-start(bf16[96,1152]{1,0:T(8,128)(2,1)S(1)} %fusion.32.refs_0_), channel_id=1, source_target_pairs={{0,4},{1,5},{2,6},{3,7},{4,0},{5,1},{6,2},{7,3},{8,12},{9,13},{10,... | collective-permute-start | bytes 663560 | tf_op jit(solution)/shard_map/ppermute | solution.py:45
  33.0 6.9 %collective-permute-start.11 = (bf16[96,1152]{1,0:T(8,128)(2,1)S(1)}, bf16[96,1152]{1,0:T(8,128)(2,1)S(1)}, u32[]{:S(2)}, u32[]{:S(2)}) collective-permute-start(bf16[96,1152]{1,0:T(8,128)(2,1)S(1)} %collective-permute-done.7.refs_1_), channel_id=1, source_target_pairs={{0,4},{1,5},{2,6},{3,7},{4,0},{5,1},{6,2},{7,3},{8,12},{9,13},{10,... | collective-permute-start | bytes 663560 | tf_op jit(solution)/shard_map/ppermute | solution.py:45
  33.5 6.4 %collective-permute-start.12 = (bf16[96,1152]{1,0:T(8,128)(2,1)S(1)}, bf16[96,1152]{1,0:T(8,128)(2,1)S(1)}, u32[]{:S(2)}, u32[]{:S(2)}) collective-permute-start(bf16[96,1152]{1,0:T(8,128)(2,1)S(1)} %collective-permute-done.8.refs_2_), channel_id=1, source_target_pairs={{0,4},{1,5},{2,6},{3,7},{4,0},{5,1},{6,2},{7,3},{8,12},{9,13},{10,... | collective-permute-start | bytes 663560 | tf_op jit(solution)/shard_map/ppermute | solution.py:45
  33.5 6.4 %collective-permute-start.13 = (bf16[96,1152]{1,0:T(8,128)(2,1)S(1)}, bf16[96,1152]{1,0:T(8,128)(2,1)}, u32[]{:S(2)}, u32[]{:S(2)}) collective-permute-start(bf16[96,1152]{1,0:T(8,128)(2,1)S(1)} %collective-permute-done.9.refs_3_), channel_id=1, source_target_pairs={{0,4},{1,5},{2,6},{3,7},{4,0},{5,1},{6,2},{7,3},{8,12},{9,13},{10,... | collective-permute-start | bytes 663560 | tf_op jit(solution)/shard_map/ppermute | solution.py:45
  34.0 25.8 %all-to-all-start = ((bf16[32,16,768]{2,1,0:T(8,128)(2,1)}), bf16[32,16,768]{2,1,0:T(8,128)(2,1)S(1)}, u32[]{:S(2)}, u32[]{:S(2)}) async-start(bf16[32,16,768]{2,1,0:T(8,128)(2,1)} %bitcast.11), calls=%async_computation | async-start | bytes 1572864 | tf_op jit(solution)/shard_map/all_to_all | solution.py:793
  45.4 3.8 %collective-permute-start.14 = (bf16[512,768]{1,0:T(8,128)(2,1)}, bf16[512,768]{1,0:T(8,128)(2,1)S(1)}, u32[]{:S(2)}, u32[]{:S(2)}) collective-permute-start(bf16[512,768]{1,0:T(8,128)(2,1)} %get-tuple-element.119.key_ref.value_ref), channel_id=1, source_target_pairs={{0,4},{1,5},{2,6},{3,7},{4,0},{5,1},{6,2},{7,3},{8,12},{9,13},{10,... | collective-permute-start | bytes 2359304 | tf_op jit(solution)/shard_map/ppermute | solution.py:45
  45.7 12.3 %collective-permute-start.15 = (bf16[96,896]{1,0:T(8,128)(2,1)S(1)}, bf16[96,896]{1,0:T(8,128)(2,1)S(1)}, u32[]{:S(2)}, u32[]{:S(2)}) collective-permute-start(bf16[96,896]{1,0:T(8,128)(2,1)S(1)} %fusion.33.refs_0_), channel_id=1, source_target_pairs={{0,8},{1,9},{2,10},{3,11},{4,12},{5,13},{6,14},{7,15},{8,0},{9,1},... | collective-permute-start | bytes 516104 | tf_op jit(solution)/shard_map/ppermute | solution.py:45
  47.4 11.1 %collective-permute-start.16 = (bf16[96,896]{1,0:T(8,128)(2,1)S(1)}, bf16[96,896]{1,0:T(8,128)(2,1)S(1)}, u32[]{:S(2)}, u32[]{:S(2)}) collective-permute-start(bf16[96,896]{1,0:T(8,128)(2,1)S(1)} %fusion.33.refs_0_), channel_id=1, source_target_pairs={{0,16},{1,17},{2,18},{3,19},{4,20},{5,21},{6,22},{7,23},{8,24},{9,... | collective-permute-start | bytes 516104 | tf_op jit(solution)/shard_map/ppermute | solution.py:45
  48.9 10.9 %collective-permute-start.17 = (bf16[96,896]{1,0:T(8,128)(2,1)S(1)}, bf16[96,896]{1,0:T(8,128)(2,1)S(1)}, u32[]{:S(2)}, u32[]{:S(2)}) collective-permute-start(bf16[96,896]{1,0:T(8,128)(2,1)S(1)} %fusion.33.refs_0_), channel_id=1, source_target_pairs={{0,24},{1,25},{2,26},{3,27},{4,28},{5,29},{6,30},{7,31},{8,16},{9,... | collective-permute-start | bytes 516104 | tf_op jit(solution)/shard_map/ppermute | solution.py:45
  59.8 14.3 %copy-start.10 = (bf16[128,384]{1,0:T(8,128)(2,1)S(1)}, bf16[128,384]{1,0:T(8,128)(2,1)}, u32[]{:S(2)}) copy-start(bf16[128,384]{1,0:T(8,128)(2,1)} %get-tuple-element.126.zero_ref.refs_4_) | copy-start | bytes 294916
  59.8 14.3 %copy-start.11 = (s32[5]{0:T(128)S(1)}, s32[5]{0:T(128)}, u32[]{:S(2)}) copy-start(s32[5]{0:T(128)} %stack.23.flags_ref) | copy-start | bytes 64
  59.9 6.0 %collective-permute-start.18 = (bf16[384,896]{1,0:T(8,128)(2,1)S(1)}, bf16[384,896]{1,0:T(8,128)(2,1)S(1)}, u32[]{:S(2)}, u32[]{:S(2)}) collective-permute-start(bf16[384,896]{1,0:T(8,128)(2,1)S(1)} %pad_maximum_fusion.1), channel_id=1, source_target_pairs={{0,4},{1,5},{2,6},{3,7},{4,0},{5,1},{6,2},{7,3},{8,12},{9,13},{10,... | collective-permute-start | bytes 2064392 | tf_op jit(solution)/shard_map/ppermute | solution.py:45
  60.8 11.3 %collective-permute-start.20 = (bf16[128,384]{1,0:T(8,128)(2,1)S(1)}, bf16[128,384]{1,0:T(8,128)(2,1)S(1)}, u32[]{:S(2)}, u32[]{:S(2)}) collective-permute-start(bf16[128,384]{1,0:T(8,128)(2,1)S(1)} %copy-done.47), channel_id=1, source_target_pairs={{0,2},{1,3},{2,0},{3,1},{4,6},{5,7},{6,4},{7,5},{8,10},{9,11},{10,... | collective-permute-start | bytes 294920 | tf_op jit(solution)/shard_map/ppermute | solution.py:45
  64.3 7.9 %collective-permute-start.21 = (bf16[128,384]{1,0:T(8,128)(2,1)S(1)}, bf16[128,384]{1,0:T(8,128)(2,1)S(1)}, u32[]{:S(2)}, u32[]{:S(2)}) collective-permute-start(bf16[128,384]{1,0:T(8,128)(2,1)S(1)} %copy-done.48), channel_id=1, source_target_pairs={{0,3},{1,2},{2,1},{3,0},{4,7},{5,6},{6,5},{7,4},{8,11},{9,10},{10,... | collective-permute-start | bytes 294920 | tf_op jit(solution)/shard_map/ppermute | solution.py:45
  69.4 4.7 %collective-permute-start.19 = (bf16[128,384]{1,0:T(8,128)(2,1)S(1)}, bf16[128,384]{1,0:T(8,128)(2,1)S(1)}, u32[]{:S(2)}, u32[]{:S(2)}) collective-permute-start(bf16[128,384]{1,0:T(8,128)(2,1)S(1)} %copy-done.46), channel_id=1, source_target_pairs={{0,1},{1,0},{2,3},{3,2},{4,5},{5,4},{6,7},{7,6},{8,9},{9,8},{10,11... | collective-permute-start | bytes 294920 | tf_op jit(solution)/shard_map/ppermute | solution.py:45
  75.4 1.4 collective-permute-start.22
  81.1 23.6 %all-to-all-start.1 = ((bf16[32,16,768]{2,1,0:T(8,128)(2,1)}), bf16[32,16,768]{2,1,0:T(8,128)(2,1)S(1)}, u32[]{:S(2)}, u32[]{:S(2)}) async-start(bf16[32,16,768]{2,1,0:T(8,128)(2,1)} %bitcast.76), calls=%async_computation.1 | async-start | bytes 1572864 | tf_op jit(solution)/shard_map/all_to_all | solution.py:793
  117.5 24.0 %all-to-all-start.2 = ((bf16[32,16,768]{2,1,0:T(8,128)(2,1)}), bf16[32,16,768]{2,1,0:T(8,128)(2,1)S(1)}, u32[]{:S(2)}, u32[]{:S(2)}) async-start(bf16[32,16,768]{2,1,0:T(8,128)(2,1)} %bitcast.77), calls=%async_computation.2 | async-start | bytes 1572864 | tf_op jit(solution)/shard_map/all_to_all | solution.py:793
  146.8 2.7 %collective-permute-start.23 = (bf16[128,768]{1,0:T(8,128)(2,1)}, bf16[128,768]{1,0:T(8,128)(2,1)S(1)}, u32[]{:S(2)}, u32[]{:S(2)}) collective-permute-start(bf16[128,768]{1,0:T(8,128)(2,1)} %get-tuple-element.157), channel_id=1, source_target_pairs={{0,4},{1,5},{2,6},{3,7},{4,0},{5,1},{6,2},{7,3},{8,12},{9,13},{10,... | collective-permute-start | bytes 589832 | tf_op jit(solution)/shard_map/ppermute | solution.py:45
  151.7 5.1 %collective-permute-start.24 = (bf16[128,384]{1,0:T(8,128)(2,1)S(1)}, bf16[128,384]{1,0:T(8,128)(2,1)S(1)}, u32[]{:S(2)}, u32[]{:S(2)}) collective-permute-start(bf16[128,384]{1,0:T(8,128)(2,1)S(1)} %get-tuple-element.158), channel_id=1, source_target_pairs={{0,1},{1,0},{2,3},{3,2},{4,5},{5,4},{6,7},{7,6},{8,9},{9,8},{10,11... | collective-permute-start | bytes 294920 | tf_op jit(solution)/shard_map/ppermute | solution.py:45
  153.5 10.1 %collective-permute-start.25 = (bf16[128,384]{1,0:T(8,128)(2,1)S(1)}, bf16[128,384]{1,0:T(8,128)(2,1)S(1)}, u32[]{:S(2)}, u32[]{:S(2)}) collective-permute-start(bf16[128,384]{1,0:T(8,128)(2,1)S(1)} %get-tuple-element.159), channel_id=1, source_target_pairs={{0,2},{1,3},{2,0},{3,1},{4,6},{5,7},{6,4},{7,5},{8,10},{9,11},{10,... | collective-permute-start | bytes 294920 | tf_op jit(solution)/shard_map/ppermute | solution.py:45
  154.3 9.4 %collective-permute-start.26 = (bf16[128,384]{1,0:T(8,128)(2,1)S(1)}, bf16[128,384]{1,0:T(8,128)(2,1)S(1)}, u32[]{:S(2)}, u32[]{:S(2)}) collective-permute-start(bf16[128,384]{1,0:T(8,128)(2,1)S(1)} %get-tuple-element.160), channel_id=1, source_target_pairs={{0,3},{1,2},{2,1},{3,0},{4,7},{5,6},{6,5},{7,4},{8,11},{9,10},{10,... | collective-permute-start | bytes 294920 | tf_op jit(solution)/shard_map/ppermute | solution.py:45
  163.7 22.9 %all-to-all-start.3 = ((bf16[32,16,768]{2,1,0:T(8,128)(2,1)}), bf16[32,16,768]{2,1,0:T(8,128)(2,1)}, u32[]{:S(2)}, u32[]{:S(2)}) async-start(bf16[32,16,768]{2,1,0:T(8,128)(2,1)} %bitcast.21), calls=%async_computation.3 | async-start | bytes 1572864 | tf_op jit(solution)/shard_map/all_to_all | solution.py:793
  176.2 2.6 %collective-permute-start.27 = (bf16[2,512,384]{2,1,0:T(8,128)(2,1)}, bf16[2,512,384]{2,1,0:T(8,128)(2,1)S(1)}, u32[]{:S(2)}, u32[]{:S(2)}) collective-permute-start(bf16[2,512,384]{2,1,0:T(8,128)(2,1)} %get-tuple-element.171), channel_id=1, source_target_pairs={{0,4},{1,5},{2,6},{3,7},{4,0},{5,1},{6,2},{7,3},{8,12},{9,13},{10,... | collective-permute-start | bytes 2359304 | tf_op jit(solution)/shard_map/ppermute | solution.py:45
  186.6 4.8 %collective-permute-start.28 = (bf16[384,2048]{1,0:T(8,128)(2,1)}, bf16[384,2048]{1,0:T(8,128)(2,1)S(1)}, u32[]{:S(2)}, u32[]{:S(2)}) collective-permute-start(bf16[384,2048]{1,0:T(8,128)(2,1)} %get-tuple-element.179), channel_id=1, source_target_pairs={{0,4},{1,5},{2,6},{3,7},{4,0},{5,1},{6,2},{7,3},{8,12},{9,13},{10,... | collective-permute-start | bytes 4718600 | tf_op jit(solution)/shard_map/ppermute | solution.py:45
  192.4 7.1 %collective-permute-start.29 = (bf16[128,768]{1,0:T(8,128)(2,1)S(1)}, bf16[128,768]{1,0:T(8,128)(2,1)S(1)}, u32[]{:S(2)}, u32[]{:S(2)}) collective-permute-start(bf16[128,768]{1,0:T(8,128)(2,1)S(1)} %get-tuple-element.213), channel_id=1, source_target_pairs={{0,1},{1,0},{2,3},{3,2},{4,5},{5,4},{6,7},{7,6},{8,9},{9,8},{10,11... | collective-permute-start | bytes 589832 | tf_op jit(solution)/shard_map/ppermute | solution.py:45
  194.3 18.7 %collective-permute-start.32 = (bf16[96,2048]{1,0:T(8,128)(2,1)S(1)}, bf16[96,2048]{1,0:T(8,128)(2,1)S(1)}, u32[]{:S(2)}, u32[]{:S(2)}) collective-permute-start(bf16[96,2048]{1,0:T(8,128)(2,1)S(1)} %get-tuple-element.207), channel_id=1, source_target_pairs={{0,8},{1,9},{2,10},{3,11},{4,12},{5,13},{6,14},{7,15},{8,0},{9,1},... | collective-permute-start | bytes 1179656 | tf_op jit(solution)/shard_map/ppermute | solution.py:45
  194.4 19.5 %collective-permute-start.33 = (bf16[96,2048]{1,0:T(8,128)(2,1)S(1)}, bf16[96,2048]{1,0:T(8,128)(2,1)S(1)}, u32[]{:S(2)}, u32[]{:S(2)}) collective-permute-start(bf16[96,2048]{1,0:T(8,128)(2,1)S(1)} %get-tuple-element.206), channel_id=1, source_target_pairs={{0,16},{1,17},{2,18},{3,19},{4,20},{5,21},{6,22},{7,23},{8,24},{9,... | collective-permute-start | bytes 1179656 | tf_op jit(solution)/shard_map/ppermute | solution.py:45
  195.8 18.1 %collective-permute-start.34 = (bf16[96,2048]{1,0:T(8,128)(2,1)S(1)}, bf16[96,2048]{1,0:T(8,128)(2,1)S(1)}, u32[]{:S(2)}, u32[]{:S(2)}) collective-permute-start(bf16[96,2048]{1,0:T(8,128)(2,1)S(1)} %get-tuple-element.205), channel_id=1, source_target_pairs={{0,24},{1,25},{2,26},{3,27},{4,28},{5,29},{6,30},{7,31},{8,16},{9,... | collective-permute-start | bytes 1179656 | tf_op jit(solution)/shard_map/ppermute | solution.py:45
  197.8 15.1 %collective-permute-start.30 = (bf16[128,768]{1,0:T(8,128)(2,1)S(1)}, bf16[128,768]{1,0:T(8,128)(2,1)S(1)}, u32[]{:S(2)}, u32[]{:S(2)}) collective-permute-start(bf16[128,768]{1,0:T(8,128)(2,1)S(1)} %get-tuple-element.212), channel_id=1, source_target_pairs={{0,2},{1,3},{2,0},{3,1},{4,6},{5,7},{6,4},{7,5},{8,10},{9,11},{10,... | collective-permute-start | bytes 589832 | tf_op jit(solution)/shard_map/ppermute | solution.py:45
  199.5 13.5 %collective-permute-start.31 = (bf16[128,768]{1,0:T(8,128)(2,1)S(1)}, bf16[128,768]{1,0:T(8,128)(2,1)S(1)}, u32[]{:S(2)}, u32[]{:S(2)}) collective-permute-start(bf16[128,768]{1,0:T(8,128)(2,1)S(1)} %get-tuple-element.211), channel_id=1, source_target_pairs={{0,3},{1,2},{2,1},{3,0},{4,7},{5,6},{6,5},{7,4},{8,11},{9,10},{10,... | collective-permute-start | bytes 589832 | tf_op jit(solution)/shard_map/ppermute | solution.py:45
  214.2 6.3 %collective-permute-start.35 = (bf16[128,768]{1,0:T(8,128)(2,1)S(1)}, bf16[128,768]{1,0:T(8,128)(2,1)S(1)}, u32[]{:S(2)}, u32[]{:S(2)}) collective-permute-start(bf16[128,768]{1,0:T(8,128)(2,1)S(1)} %broadcast_select_fusion.6), channel_id=1, source_target_pairs={{0,4},{1,5},{2,6},{3,7},{4,0},{5,1},{6,2},{7,3},{8,12},{9,13},{10,... | collective-permute-start | bytes 589832 | tf_op jit(solution)/shard_map/ppermute | solution.py:45
  214.3 7.9 %collective-permute-start.37 = (bf16[24,2048]{1,0:T(8,128)(2,1)S(1)}, bf16[24,2048]{1,0:T(8,128)(2,1)S(1)}, u32[]{:S(2)}, u32[]{:S(2)}) collective-permute-start(bf16[24,2048]{1,0:T(8,128)(2,1)S(1)} %get-tuple-element.209), channel_id=1, source_target_pairs={{0,2},{1,3},{2,0},{3,1},{4,6},{5,7},{6,4},{7,5},{8,10},{9,11},{10,... | collective-permute-start | bytes 294920 | tf_op jit(solution)/shard_map/ppermute | solution.py:45
  217.9 8.3 %collective-permute-start.38 = (bf16[24,2048]{1,0:T(8,128)(2,1)S(1)}, bf16[24,2048]{1,0:T(8,128)(2,1)S(1)}, u32[]{:S(2)}, u32[]{:S(2)}) collective-permute-start(bf16[24,2048]{1,0:T(8,128)(2,1)S(1)} %get-tuple-element.208), channel_id=1, source_target_pairs={{0,3},{1,2},{2,1},{3,0},{4,7},{5,6},{6,5},{7,4},{8,11},{9,10},{10,... | collective-permute-start | bytes 294920 | tf_op jit(solution)/shard_map/ppermute | solution.py:45
  222.2 5.8 %collective-permute-start.36 = (bf16[24,2048]{1,0:T(8,128)(2,1)S(1)}, bf16[24,2048]{1,0:T(8,128)(2,1)S(1)}, u32[]{:S(2)}, u32[]{:S(2)}) collective-permute-start(bf16[24,2048]{1,0:T(8,128)(2,1)S(1)} %get-tuple-element.192), channel_id=1, source_target_pairs={{0,1},{1,0},{2,3},{3,2},{4,5},{5,4},{6,7},{7,6},{8,9},{9,8},{10,11... | collective-permute-start | bytes 294920 | tf_op jit(solution)/shard_map/ppermute | solution.py:45
  (47 other events, 265.7 us)

commit v5 on v4

--- a/solution.py
+++ b/solution.py
@@ -785,7 +785,7 @@
         operands,
         [low_shape(work_rows, 3 * part)] + dealt(width, columns),
         [pltpu.VMEM((width, columns), F32)],
-        2 * SMALL_BYTES,
+        VMEM_BYTES,
     )
 
 

time: 230 us -> 230 us (level)
    unnamed x104 -> x94, local copies, waits for them, and re-layouts: 10.5 us -> 8.26 us
  transfers between devices with their start and end apart: 43 -> 43, of which waited for: 20 -> 21; matrix products, arithmetic and copies ran while one was open for 17% -> 17% of each run, Pallas kernels for 15% -> 16%
where the time goes in v5:
time: 230 us; the launch traced here: 229 us
  starting transfers between devices  61 us (27%)
  Pallas kernels  60.8 us (26%)
  waiting for transfers between devices  56 us (24%)
  matrix products  23.6 us (10%)
  local copies, waits for them, and re-layouts  13.1 us (6%)
  other arithmetic  13.1 us (6%)
    ppermute x39, starting transfers between devices, permute(): return lax.ppermute(array, AXES, pairs)  45 us
    ppermute x39, waiting for transfers between devices, permute(): return lax.ppermute(array, AXES, pairs)  44.6 us
    pallas_call x9, Pallas kernels, one_step(): pl.pallas_call(kernel, grid=(1,), in_specs=[FLAGS] + [whole(operand.shape...  26.2 us
    all_to_all x4, starting transfers between devices, all_to_all(): return lax.all_to_all(array, AXES, split_axis=0, concat_axis=0, tiled=True)  16.1 us
    dot_general x3, matrix products, dot_tn(): lax.dot_general(left, right, (((0,), (0,)), ((), ())), preferred_element_...  12.3 us
    pallas_call x1, Pallas kernels, expert_layer(): pl.pallas_call(expert_kernel, grid=(hidden_width // TILE,), in_specs=[FLA...  11.9 us
    all_to_all x4, waiting for transfers between devices, all_to_all(): return lax.all_to_all(array, AXES, split_axis=0, concat_axis=0, tiled=True)  11.4 us
    pallas_call x1, Pallas kernels, attention_backward(): pl.pallas_call(backward_kernel, grid=(pairs,), in_specs=[pair_column(rows...  8.84 us
  transfers between devices with their start and end apart: 43, of which 21 were waited for; matrix products, arithmetic and copies ran while one was open for 17% of the time, Pallas kernels for 16%

profile of v5, /device:TPU:0, one launch (start us, length us, event | category | flops | bytes accessed | tf_op | source)
XLA Modules:
  0.0 229.0 jit_solution(13266500901286192920)
XLA Ops:
  1.3 1.7 shard_map.203
  2.9 3.0 %collective-permute-start.4 = (bf16[24,2048]{1,0:T(8,128)(2,1)}, bf16[24,2048]{1,0:T(8,128)(2,1)S(1)}, u32[]{:S(2)}, u32[]{:S(2)}) collective-permute-start(bf16[24,2048]{1,0:T(8,128)(2,1)} %get-tuple-element.108), channel_id=1, source_target_pairs={{0,1},{1,0},{2,3},{3,2},{4,5},{5,4},{6,7},{7,6},{8,9},{9,8},{10,11... | collective-permute-start | bytes 294920 | tf_op jit(solution)/shard_map/ppermute | solution.py:45
  5.9 2.5 %collective-permute-start.6 = (bf16[24,2048]{1,0:T(8,128)(2,1)}, bf16[24,2048]{1,0:T(8,128)(2,1)S(1)}, u32[]{:S(2)}, u32[]{:S(2)}) collective-permute-start(bf16[24,2048]{1,0:T(8,128)(2,1)} %get-tuple-element.108), channel_id=1, source_target_pairs={{0,3},{1,2},{2,1},{3,0},{4,7},{5,6},{6,5},{7,4},{8,11},{9,10},{10,... | collective-permute-start | bytes 294920 | tf_op jit(solution)/shard_map/ppermute | solution.py:45
  12.7 5.3 %collective-permute-done.5 = bf16[24,2048]{1,0:T(8,128)(2,1)S(1)} collective-permute-done((bf16[24,2048]{1,0:T(8,128)(2,1)}, bf16[24,2048]{1,0:T(8,128)(2,1)S(1)}, u32[]{:S(2)}, u32[]{:S(2)}) %collective-permute-start.5) | collective-permute-done | bytes 98336 | tf_op jit(solution)/shard_map/ppermute | solution.py:45
  19.3 1.6 collective-permute-start.7
  20.8 1.5 collective-permute-start.8
  22.8 2.7 %collective-permute-start.1 = (bf16[128,768]{1,0:T(8,128)(2,1)S(1)}, bf16[128,768]{1,0:T(8,128)(2,1)S(1)}, u32[]{:S(2)}, u32[]{:S(2)}) collective-permute-start(bf16[128,768]{1,0:T(8,128)(2,1)S(1)} %get-tuple-element.214), channel_id=1, source_target_pairs={{0,1},{1,0},{2,3},{3,2},{4,5},{5,4},{6,7},{7,6},{8,9},{9,8},{10,11... | collective-permute-start | bytes 589832 | tf_op jit(solution)/shard_map/ppermute | solution.py:45
  25.5 4.4 %collective-permute-done.2 = bf16[128,768]{1,0:T(8,128)(2,1)S(1)} collective-permute-done((bf16[128,768]{1,0:T(8,128)(2,1)S(1)}, bf16[128,768]{1,0:T(8,128)(2,1)S(1)}, u32[]{:S(2)}, u32[]{:S(2)}) %collective-permute-start.2) | collective-permute-done | bytes 196640 | tf_op jit(solution)/shard_map/ppermute | solution.py:45
  34.0 4.5 %all-to-all-start = ((bf16[32,16,768]{2,1,0:T(8,128)(2,1)}), bf16[32,16,768]{2,1,0:T(8,128)(2,1)S(1)}, u32[]{:S(2)}, u32[]{:S(2)}) async-start(bf16[32,16,768]{2,1,0:T(8,128)(2,1)} %bitcast.11), calls=%async_computation | async-start | bytes 1572864 | tf_op jit(solution)/shard_map/all_to_all | solution.py:793
  40.7 4.7 %shard_map.204 = (bf16[512,384]{1,0:T(8,128)(2,1)}, bf16[512,768]{1,0:T(8,128)(2,1)}, bf16[768,1152]{1,0:T(8,128)(2,1)}) custom-call(s32[5]{0:T(128)} %stack.23.flags_ref, bf16[512,768]{1,0:T(8,128)(2,1)} %fusion.3.normed_ref, bf16[96,1152]{1,0:T(8,128)(2,1)} %copy-done.21, bf16[96,1152]{1,0:T(8,128)(2,1)} %copy-done.30, bf16[96,1152]{1,0:T(8,128)(2,1)} %copy-done.31, ...), custom_call_target="tpu_custom_call" | custom-call | bytes 1048576 | tf_op jit(solution)/shard_map/pallas_call | solution.py:274
  45.7 1.7 collective-permute-start.15
  47.4 1.5 collective-permute-start.16
  50.1 7.8 %shard_map.205 = (bf16[128,384]{1,0:T(8,128)(2,1)}, bf16[128,384]{1,0:T(8,128)(2,1)}, bf16[128,384]{1,0:T(8,128)(2,1)}, bf16[128,384]{1,0:T(8,128)(2,1)}, bf16[6...) custom-call(bf16[512,384]{1,0:T(8,128)(2,1)} %get-tuple-element.118.query_ref, ...), custom_call_target="tpu_custom_call" | custom-call | flops 2000000000 | bytes 4096 | tf_op jit(solution)/shard_map/pallas_call | solution.py:180
  60.8 3.5 %collective-permute-start.20 = (bf16[128,384]{1,0:T(8,128)(2,1)S(1)}, bf16[128,384]{1,0:T(8,128)(2,1)S(1)}, u32[]{:S(2)}, u32[]{:S(2)}) collective-permute-start(bf16[128,384]{1,0:T(8,128)(2,1)S(1)} %copy-done.42), channel_id=1, source_target_pairs={{0,2},{1,3},{2,0},{3,1},{4,6},{5,7},{6,4},{7,5},{8,10},{9,11},{10,... | collective-permute-start | bytes 294920 | tf_op jit(solution)/shard_map/ppermute | solution.py:45
  64.3 1.5 collective-permute-start.21
  66.7 2.6 %shard_map.206 = (bf16[768,896]{1,0:T(8,128)(2,1)}, f32[1,768]{1,0:T(1,128)}) custom-call(s32[5]{0:T(128)} %stack.23.flags_ref, bf16[96,896]{1,0:T(8,128)(2,1)} %copy-done.20, bf16[96,896]{1,0:T(8,128)(2,1)} %copy-done.26, bf16[96,896]{1,0:T(8,128)(2,1)} %copy-done.27, bf16[96,896]{1,0:T(8,128)(2,1)} %copy-done.28, bf16[384,896]{1,0:T(8,128)(2,1)} %copy-done.25), custom_call_target="tpu_custom_call" | custom-call | bytes 1048576 | tf_op jit(solution)/shard_map/pallas_call | solution.py:274
  70.2 2.0 collective-permute-done.20.two_ref
  72.2 1.9 collective-permute-done.19.one_ref
  77.5 3.6 %shard_map.208 = (bf16[256,768]{1,0:T(8,128)(2,1)}, f32[256,768]{1,0:T(8,128)}, bf16[512,768]{1,0:T(8,128)(2,1)}) custom-call(s32[5]{0:T(128)} %stack.23.flags_ref, bf16[128,768]{1,0:T(8,128)(2,1)} %copy-done, bf16[128,768]{1,0:T(8,128)(2,1)} %copy-done.36, bf16[256,768]{1,0:T(8,128)(2,1)} %inputs_ref.1, bf16[768,896]{1,0:T(8,128)(2,1)} %get-tuple-element.141.weight_ref, ...), custom_call_target="tpu_custom_call" | custom-call | bytes 1048576 | tf_op jit(solution)/shard_map/pallas_call | solution.py:274
  81.1 4.1 %all-to-all-start.1 = ((bf16[32,16,768]{2,1,0:T(8,128)(2,1)}), bf16[32,16,768]{2,1,0:T(8,128)(2,1)S(1)}, u32[]{:S(2)}, u32[]{:S(2)}) async-start(bf16[32,16,768]{2,1,0:T(8,128)(2,1)} %bitcast.77), calls=%async_computation.1 | async-start | bytes 1572864 | tf_op jit(solution)/shard_map/all_to_all | solution.py:793
  85.3 1.6 slice.64.router_ref
  89.2 6.0 %shard_map.209 = (bf16[320,768]{1,0:T(8,128)(2,1)}, bf16[320,3072]{1,0:T(8,128)(2,1)}) custom-call(bf16[512,768]{1,0:T(8,128)(2,1)} %bitcast.74, bf16[320,512]{1,0:T(8,128)(2,1)} %fusion.25.compact_ref, bf16[1,3072,768]{2,1,0:T(8,128)(2,1)} %weight_out_ref.1), custom_call_target="tpu_custom_call" | custom-call | flops 1509949440 | bytes 9437184 | tf_op jit(solution)/shard_map/pallas_call | solution.py:560
  95.2 9.5 %all-to-all-done.1 = bf16[32,16,768]{2,1,0:T(8,128)(2,1)S(1)} async-done(((bf16[32,16,768]{2,1,0:T(8,128)(2,1)}), bf16[32,16,768]{2,1,0:T(8,128)(2,1)S(1)}, u32[]{:S(2)}, u32[]{:S(2)}) %all-to-all-start.1) | async-done | bytes 786464 | tf_op jit(solution)/shard_map/all_to_all | solution.py:793
  105.6 11.9 %shard_map.210 = (bf16[320,768]{1,0:T(8,128)(2,1)}, bf16[320,768]{1,0:T(8,128)(2,1)}, bf16[320,3072]{1,0:T(8,128)(2,1)}, bf16[320,3072]{1,0:T(8,128)(2,1)}, bf16...) custom-call(s32[5]{0:T(128)} %stack.23.flags_ref, bf16[512,768]{1,0:T(8,128)(2,1)} %bitcast.76, ...), custom_call_target="tpu_custom_call" | custom-call | flops 6039797760 | bytes 18874368 | tf_op jit(solution)/shard_map/pallas_call | solution.py:639
  117.5 4.4 %all-to-all-start.2 = ((bf16[32,16,768]{2,1,0:T(8,128)(2,1)}), bf16[32,16,768]{2,1,0:T(8,128)(2,1)S(1)}, u32[]{:S(2)}, u32[]{:S(2)}) async-start(bf16[32,16,768]{2,1,0:T(8,128)(2,1)} %bitcast.78), calls=%async_computation.2 | async-start | bytes 1572864 | tf_op jit(solution)/shard_map/all_to_all | solution.py:793
  122.3 6.9 %fusion.41 = f32[768,3072]{1,0:T(8,128)} fusion(bf16[320,768]{1,0:T(8,128)(2,1)S(1)} %copy-done.18, bf16[320,3072]{1,0:T(8,128)(2,1)} %get-tuple-element.152), kind=kOutput, calls=%fused_computation.94 | convolution fusion | flops 1509949440 | bytes 11894784 | tf_op jit(solution)/shard_map/dot_general | solution.py:24
  129.2 5.2 %fusion.42 = f32[3072,768]{1,0:T(8,128)} fusion(bf16[320,3072]{1,0:T(8,128)(2,1)S(1)} %copy-done.17, bf16[320,768]{1,0:T(8,128)(2,1)S(1)} %copy-done.29), kind=kOutput, calls=%fused_computation.95 | convolution fusion | flops 1509949440 | bytes 11894784 | tf_op jit(solution)/shard_map/dot_general | solution.py:24
  134.4 5.7 %convolution_convert_fusion = bf16[512,768]{1,0:T(8,128)(2,1)} fusion(bf16[320,3072]{1,0:T(8,128)(2,1)S(1)} %copy-done.17, bf16[1,3072,768]{2,1,0:T(8,128)(2,1)} %weight_out_ref.1, f32[320]{0:T(512)S(1)} %reduce.2, s32[512]{0:T(512)S(1)} %and_select_fusion), kind=kOutput, calls=%fused_computation.7 | convolution fusion | flops 1763147776 | bytes 7474432 | tf_op jit(solution)/shard_map/dot_general | solution.py:20
  140.1 1.4 all-to-all-done.2
  142.4 4.5 %shard_map.211 = (f32[256,768]{1,0:T(8,128)}, bf16[256,768]{1,0:T(8,128)(2,1)}, bf16[128,768]{1,0:T(8,128)(2,1)}, bf16[128,768]{1,0:T(8,128)(2,1)}, bf16[16,768]{1,0:T(8,128)(2,1)}) custom-call(s32[5]{0:T(128)} %stack.23.flags_ref, bf16[512,768]{1,0:T(8,128)(2,1)} %bitcast.75, bf16[256,512]{1,0:T(8,128)(2,1)} %fusion.26.to_tokens_ref, ...), custom_call_target="tpu_custom_call" | custom-call | bytes 1048576 | tf_op jit(solution)/shard_map/pallas_call | solution.py:274
  146.9 1.5 collective-permute-start.23
  151.8 1.8 collective-permute-start.24
  154.4 1.8 collective-permute-start.26
  156.9 6.9 %collective-permute-done.25.refs_2_ = bf16[128,384]{1,0:T(8,128)(2,1)S(1)} collective-permute-done((bf16[128,384]{1,0:T(8,128)(2,1)S(1)}, bf16[128,384]{1,0:T(8,128)(2,1)S(1)}, u32[]{:S(2)}, u32[]{:S(2)}) %collective-permute-start.25) | collective-permute-done | bytes 98336 | tf_op jit(solution)/shard_map/ppermute | solution.py:45
  163.8 3.0 %all-to-all-start.3 = ((bf16[32,16,768]{2,1,0:T(8,128)(2,1)}), bf16[32,16,768]{2,1,0:T(8,128)(2,1)S(1)}, u32[]{:S(2)}, u32[]{:S(2)}) async-start(bf16[32,16,768]{2,1,0:T(8,128)(2,1)} %bitcast.21), calls=%async_computation.3 | async-start | bytes 1572864 | tf_op jit(solution)/shard_map/all_to_all | solution.py:793
  166.8 8.8 %shard_map.213 = (bf16[512,384]{1,0:T(8,128)(2,1)}, bf16[2,512,384]{2,1,0:T(8,128)(2,1)}, bf16[2,512,384]{2,1,0:T(8,128)(2,1)}) custom-call(bf16[512,384]{1,0:T(8,128)(2,1)} %get-tuple-element.118.query_ref, bf16[512,768]{1,0:T(8,128)(2,1)} %get-tuple-element.119.key_ref.value_ref, bf16[512,768]{1,0:T(8,128)(2,1)} %get-tuple-element.119.key_ref.value_ref, ...), custom_call_target="tpu_custom_call" | custom-call | flops 20000000000 | bytes 4096 | tf_op jit(solution)/shard_map/pallas_call | solution.py:231
  176.7 1.5 collective-permute-done.27.got_ref
  179.1 6.5 %shard_map.214 = (bf16[512,1152]{1,0:T(8,128)(2,1)}, f32[384,2048]{1,0:T(8,128)}, bf16[384,2048]{1,0:T(8,128)(2,1)}) custom-call(s32[5]{0:T(128)} %stack.23.flags_ref, bf16[512,768]{1,0:T(8,128)(2,1)} %fusion.3.normed_ref, bf16[512,384]{1,0:T(8,128)(2,1)} %get-tuple-element.169.query_ref, bf16[2,512,384]{2,1,0:T(8,128)(2,1)} %get-tuple-element.170.near_ref, ...), custom_call_target="tpu_custom_call" | custom-call | bytes 1048576 | tf_op jit(solution)/shard_map/pallas_call | solution.py:274
  186.2 1.5 collective-permute-start.28
  187.8 3.2 %convolution_convert_fusion.2 = bf16[512,768]{1,0:T(8,128)(2,1)S(1)} fusion(bf16[512,1152]{1,0:T(8,128)(2,1)} %get-tuple-element.175, bf16[768,1152]{1,0:T(8,128)(2,1)} %get-tuple-element.176), kind=kOutput, calls=%fused_computation.9 | convolution fusion | flops 906362880 | bytes 3735552 | tf_op jit(solution)/shard_map/dot_general | solution.py:28
  192.0 1.8 collective-permute-start.29
  195.1 2.3 %collective-permute-start.34 = (bf16[96,2048]{1,0:T(8,128)(2,1)S(1)}, bf16[96,2048]{1,0:T(8,128)(2,1)S(1)}, u32[]{:S(2)}, u32[]{:S(2)}) collective-permute-start(bf16[96,2048]{1,0:T(8,128)(2,1)S(1)} %get-tuple-element.205), channel_id=1, source_target_pairs={{0,24},{1,25},{2,26},{3,27},{4,28},{5,29},{6,30},{7,31},{8,16},{9,... | collective-permute-start | bytes 1179656 | tf_op jit(solution)/shard_map/ppermute | solution.py:45
  199.1 3.1 %collective-permute-start.31 = (bf16[128,768]{1,0:T(8,128)(2,1)S(1)}, bf16[128,768]{1,0:T(8,128)(2,1)S(1)}, u32[]{:S(2)}, u32[]{:S(2)}) collective-permute-start(bf16[128,768]{1,0:T(8,128)(2,1)S(1)} %get-tuple-element.211), channel_id=1, source_target_pairs={{0,3},{1,2},{2,1},{3,0},{4,7},{5,6},{6,5},{7,4},{8,11},{9,10},{10,... | collective-permute-start | bytes 589832 | tf_op jit(solution)/shard_map/ppermute | solution.py:45
  203.4 9.1 %collective-permute-done.30 = bf16[128,768]{1,0:T(8,128)(2,1)S(1)} collective-permute-done((bf16[128,768]{1,0:T(8,128)(2,1)S(1)}, bf16[128,768]{1,0:T(8,128)(2,1)S(1)}, u32[]{:S(2)}, u32[]{:S(2)}) %collective-permute-start.30) | collective-permute-done | bytes 196640 | tf_op jit(solution)/shard_map/ppermute | solution.py:45
  213.9 3.5 %collective-permute-start.37 = (bf16[24,2048]{1,0:T(8,128)(2,1)S(1)}, bf16[24,2048]{1,0:T(8,128)(2,1)S(1)}, u32[]{:S(2)}, u32[]{:S(2)}) collective-permute-start(bf16[24,2048]{1,0:T(8,128)(2,1)S(1)} %get-tuple-element.209), channel_id=1, source_target_pairs={{0,2},{1,3},{2,0},{3,1},{4,6},{5,7},{6,4},{7,5},{8,10},{9,11},{10,... | collective-permute-start | bytes 294920 | tf_op jit(solution)/shard_map/ppermute | solution.py:45
  217.3 2.8 %collective-permute-start.38 = (bf16[24,2048]{1,0:T(8,128)(2,1)S(1)}, bf16[24,2048]{1,0:T(8,128)(2,1)S(1)}, u32[]{:S(2)}, u32[]{:S(2)}) collective-permute-start(bf16[24,2048]{1,0:T(8,128)(2,1)S(1)} %get-tuple-element.208), channel_id=1, source_target_pairs={{0,3},{1,2},{2,1},{3,0},{4,7},{5,6},{6,5},{7,4},{8,11},{9,10},{10,... | collective-permute-start | bytes 294920 | tf_op jit(solution)/shard_map/ppermute | solution.py:45
  221.8 4.0 %collective-permute-done.38.three_ref = bf16[24,2048]{1,0:T(8,128)(2,1)S(1)} collective-permute-done((bf16[24,2048]{1,0:T(8,128)(2,1)S(1)}, bf16[24,2048]{1,0:T(8,128)(2,1)S(1)}, u32[]{:S(2)}, u32[]{:S(2)}) %collective-permute-start.38) | collective-permute-done | bytes 98336 | tf_op jit(solution)/shard_map/ppermute | solution.py:45
  225.8 1.7 collective-permute-done.36.one_ref
  (206 shorter events, 43.5 us)
Async XLA Ops:
  0.6 18.4 %copy-start.11 = (bf16[256,768]{1,0:T(8,128)(2,1)S(1)}, bf16[256,768]{1,0:T(8,128)(2,1)}, u32[]{:S(2)}) copy-start(bf16[256,768]{1,0:T(8,128)(2,1)} %inputs_ref.1) | copy-start | bytes 1179652
  2.9 9.8 %collective-permute-start.4 = (bf16[24,2048]{1,0:T(8,128)(2,1)}, bf16[24,2048]{1,0:T(8,128)(2,1)S(1)}, u32[]{:S(2)}, u32[]{:S(2)}) collective-permute-start(bf16[24,2048]{1,0:T(8,128)(2,1)} %get-tuple-element.108), channel_id=1, source_target_pairs={{0,1},{1,0},{2,3},{3,2},{4,5},{5,4},{6,7},{7,6},{8,9},{9,8},{10,11... | collective-permute-start | bytes 294920 | tf_op jit(solution)/shard_map/ppermute | solution.py:45
  5.9 12.0 %collective-permute-start.6 = (bf16[24,2048]{1,0:T(8,128)(2,1)}, bf16[24,2048]{1,0:T(8,128)(2,1)S(1)}, u32[]{:S(2)}, u32[]{:S(2)}) collective-permute-start(bf16[24,2048]{1,0:T(8,128)(2,1)} %get-tuple-element.108), channel_id=1, source_target_pairs={{0,3},{1,2},{2,1},{3,0},{4,7},{5,6},{6,5},{7,4},{8,11},{9,10},{10,... | collective-permute-start | bytes 294920 | tf_op jit(solution)/shard_map/ppermute | solution.py:45
  9.5 9.5 %collective-permute-start = (bf16[128,768]{1,0:T(8,128)(2,1)S(1)}, bf16[128,768]{1,0:T(8,128)(2,1)S(1)}, u32[]{:S(2)}, u32[]{:S(2)}) collective-permute-start(bf16[128,768]{1,0:T(8,128)(2,1)S(1)} %broadcast_select_fusion.4), channel_id=1, source_target_pairs={{0,4},{1,5},{2,6},{3,7},{4,0},{5,1},{6,2},{7,3},{8,12},{9,13},{10,... | collective-permute-start | bytes 589832 | tf_op jit(solution)/shard_map/ppermute | solution.py:45
  9.5 8.4 %collective-permute-start.5 = (bf16[24,2048]{1,0:T(8,128)(2,1)}, bf16[24,2048]{1,0:T(8,128)(2,1)S(1)}, u32[]{:S(2)}, u32[]{:S(2)}) collective-permute-start(bf16[24,2048]{1,0:T(8,128)(2,1)} %get-tuple-element.107), channel_id=1, source_target_pairs={{0,2},{1,3},{2,0},{3,1},{4,6},{5,7},{6,4},{7,5},{8,10},{9,11},{10,... | collective-permute-start | bytes 294920 | tf_op jit(solution)/shard_map/ppermute | solution.py:45
  12.7 17.3 %copy-start.19 = (bf16[256,768]{1,0:T(8,128)(2,1)S(1)}, bf16[256,768]{1,0:T(8,128)(2,1)}, u32[]{:S(2)}) copy-start(bf16[256,768]{1,0:T(8,128)(2,1)} %cotangent_ref.1) | copy-start | bytes 1179652
  19.1 10.9 %collective-permute-start.2 = (bf16[128,768]{1,0:T(8,128)(2,1)S(1)}, bf16[128,768]{1,0:T(8,128)(2,1)S(1)}, u32[]{:S(2)}, u32[]{:S(2)}) collective-permute-start(bf16[128,768]{1,0:T(8,128)(2,1)S(1)} %get-tuple-element.215), channel_id=1, source_target_pairs={{0,2},{1,3},{2,0},{3,1},{4,6},{5,7},{6,4},{7,5},{8,10},{9,11},{10,... | collective-permute-start | bytes 589832 | tf_op jit(solution)/shard_map/ppermute | solution.py:45
  19.3 19.5 %copy-start.21 = (bf16[96,1152]{1,0:T(8,128)(2,1)}, bf16[96,1152]{1,0:T(8,128)(2,1)S(1)}, u32[]{:S(2)}) copy-start(bf16[96,1152]{1,0:T(8,128)(2,1)S(1)} %fusion.32.refs_0_) | copy-start | bytes 663556
  19.3 11.9 %collective-permute-start.7 = (bf16[96,1152]{1,0:T(8,128)(2,1)S(1)}, bf16[96,1152]{1,0:T(8,128)(2,1)S(1)}, u32[]{:S(2)}, u32[]{:S(2)}) collective-permute-start(bf16[96,1152]{1,0:T(8,128)(2,1)S(1)} %fusion.32.refs_0_), channel_id=1, source_target_pairs={{0,8},{1,9},{2,10},{3,11},{4,12},{5,13},{6,14},{7,15},{8,0},{9,1},... | collective-permute-start | bytes 663560 | tf_op jit(solution)/shard_map/ppermute | solution.py:45
  20.8 11.6 %collective-permute-start.8 = (bf16[96,1152]{1,0:T(8,128)(2,1)S(1)}, bf16[96,1152]{1,0:T(8,128)(2,1)S(1)}, u32[]{:S(2)}, u32[]{:S(2)}) collective-permute-start(bf16[96,1152]{1,0:T(8,128)(2,1)S(1)} %fusion.32.refs_0_), channel_id=1, source_target_pairs={{0,16},{1,17},{2,18},{3,19},{4,20},{5,21},{6,22},{7,23},{8,24},{9,... | collective-permute-start | bytes 663560 | tf_op jit(solution)/shard_map/ppermute | solution.py:45
  22.4 10.1 %collective-permute-start.9 = (bf16[96,1152]{1,0:T(8,128)(2,1)S(1)}, bf16[96,1152]{1,0:T(8,128)(2,1)S(1)}, u32[]{:S(2)}, u32[]{:S(2)}) collective-permute-start(bf16[96,1152]{1,0:T(8,128)(2,1)S(1)} %fusion.32.refs_0_), channel_id=1, source_target_pairs={{0,24},{1,25},{2,26},{3,27},{4,28},{5,29},{6,30},{7,31},{8,16},{9,... | collective-permute-start | bytes 663560 | tf_op jit(solution)/shard_map/ppermute | solution.py:45
  22.8 10.1 %collective-permute-start.1 = (bf16[128,768]{1,0:T(8,128)(2,1)S(1)}, bf16[128,768]{1,0:T(8,128)(2,1)S(1)}, u32[]{:S(2)}, u32[]{:S(2)}) collective-permute-start(bf16[128,768]{1,0:T(8,128)(2,1)S(1)} %get-tuple-element.214), channel_id=1, source_target_pairs={{0,1},{1,0},{2,3},{3,2},{4,5},{5,4},{6,7},{7,6},{8,9},{9,8},{10,11... | collective-permute-start | bytes 589832 | tf_op jit(solution)/shard_map/ppermute | solution.py:45
  30.0 8.6 %collective-permute-start.3 = (bf16[128,768]{1,0:T(8,128)(2,1)S(1)}, bf16[128,768]{1,0:T(8,128)(2,1)S(1)}, u32[]{:S(2)}, u32[]{:S(2)}) collective-permute-start(bf16[128,768]{1,0:T(8,128)(2,1)S(1)} %collective-permute-done.2), channel_id=1, source_target_pairs={{0,1},{1,0},{2,3},{3,2},{4,5},{5,4},{6,7},{7,6},{8,9},{9,8},{10,11... | collective-permute-start | bytes 589832 | tf_op jit(solution)/shard_map/ppermute | solution.py:45
  33.0 6.9 %collective-permute-start.10 = (bf16[96,1152]{1,0:T(8,128)(2,1)S(1)}, bf16[96,1152]{1,0:T(8,128)(2,1)S(1)}, u32[]{:S(2)}, u32[]{:S(2)}) collective-permute-start(bf16[96,1152]{1,0:T(8,128)(2,1)S(1)} %fusion.32.refs_0_), channel_id=1, source_target_pairs={{0,4},{1,5},{2,6},{3,7},{4,0},{5,1},{6,2},{7,3},{8,12},{9,13},{10,... | collective-permute-start | bytes 663560 | tf_op jit(solution)/shard_map/ppermute | solution.py:45
  33.0 6.9 %collective-permute-start.11 = (bf16[96,1152]{1,0:T(8,128)(2,1)S(1)}, bf16[96,1152]{1,0:T(8,128)(2,1)S(1)}, u32[]{:S(2)}, u32[]{:S(2)}) collective-permute-start(bf16[96,1152]{1,0:T(8,128)(2,1)S(1)} %collective-permute-done.7.refs_1_), channel_id=1, source_target_pairs={{0,4},{1,5},{2,6},{3,7},{4,0},{5,1},{6,2},{7,3},{8,12},{9,13},{10,... | collective-permute-start | bytes 663560 | tf_op jit(solution)/shard_map/ppermute | solution.py:45
  33.5 6.4 %collective-permute-start.12 = (bf16[96,1152]{1,0:T(8,128)(2,1)S(1)}, bf16[96,1152]{1,0:T(8,128)(2,1)S(1)}, u32[]{:S(2)}, u32[]{:S(2)}) collective-permute-start(bf16[96,1152]{1,0:T(8,128)(2,1)S(1)} %collective-permute-done.8.refs_2_), channel_id=1, source_target_pairs={{0,4},{1,5},{2,6},{3,7},{4,0},{5,1},{6,2},{7,3},{8,12},{9,13},{10,... | collective-permute-start | bytes 663560 | tf_op jit(solution)/shard_map/ppermute | solution.py:45
  33.5 6.4 %collective-permute-start.13 = (bf16[96,1152]{1,0:T(8,128)(2,1)S(1)}, bf16[96,1152]{1,0:T(8,128)(2,1)}, u32[]{:S(2)}, u32[]{:S(2)}) collective-permute-start(bf16[96,1152]{1,0:T(8,128)(2,1)S(1)} %collective-permute-done.9.refs_3_), channel_id=1, source_target_pairs={{0,4},{1,5},{2,6},{3,7},{4,0},{5,1},{6,2},{7,3},{8,12},{9,13},{10,... | collective-permute-start | bytes 663560 | tf_op jit(solution)/shard_map/ppermute | solution.py:45
  34.0 25.8 %all-to-all-start = ((bf16[32,16,768]{2,1,0:T(8,128)(2,1)}), bf16[32,16,768]{2,1,0:T(8,128)(2,1)S(1)}, u32[]{:S(2)}, u32[]{:S(2)}) async-start(bf16[32,16,768]{2,1,0:T(8,128)(2,1)} %bitcast.11), calls=%async_computation | async-start | bytes 1572864 | tf_op jit(solution)/shard_map/all_to_all | solution.py:793
  45.4 3.8 %collective-permute-start.14 = (bf16[512,768]{1,0:T(8,128)(2,1)}, bf16[512,768]{1,0:T(8,128)(2,1)S(1)}, u32[]{:S(2)}, u32[]{:S(2)}) collective-permute-start(bf16[512,768]{1,0:T(8,128)(2,1)} %get-tuple-element.119.key_ref.value_ref), channel_id=1, source_target_pairs={{0,4},{1,5},{2,6},{3,7},{4,0},{5,1},{6,2},{7,3},{8,12},{9,13},{10,... | collective-permute-start | bytes 2359304 | tf_op jit(solution)/shard_map/ppermute | solution.py:45
  45.7 12.3 %collective-permute-start.15 = (bf16[96,896]{1,0:T(8,128)(2,1)S(1)}, bf16[96,896]{1,0:T(8,128)(2,1)S(1)}, u32[]{:S(2)}, u32[]{:S(2)}) collective-permute-start(bf16[96,896]{1,0:T(8,128)(2,1)S(1)} %fusion.33.refs_0_), channel_id=1, source_target_pairs={{0,8},{1,9},{2,10},{3,11},{4,12},{5,13},{6,14},{7,15},{8,0},{9,1},... | collective-permute-start | bytes 516104 | tf_op jit(solution)/shard_map/ppermute | solution.py:45
  47.4 11.1 %collective-permute-start.16 = (bf16[96,896]{1,0:T(8,128)(2,1)S(1)}, bf16[96,896]{1,0:T(8,128)(2,1)S(1)}, u32[]{:S(2)}, u32[]{:S(2)}) collective-permute-start(bf16[96,896]{1,0:T(8,128)(2,1)S(1)} %fusion.33.refs_0_), channel_id=1, source_target_pairs={{0,16},{1,17},{2,18},{3,19},{4,20},{5,21},{6,22},{7,23},{8,24},{9,... | collective-permute-start | bytes 516104 | tf_op jit(solution)/shard_map/ppermute | solution.py:45
  48.9 10.9 %collective-permute-start.17 = (bf16[96,896]{1,0:T(8,128)(2,1)S(1)}, bf16[96,896]{1,0:T(8,128)(2,1)S(1)}, u32[]{:S(2)}, u32[]{:S(2)}) collective-permute-start(bf16[96,896]{1,0:T(8,128)(2,1)S(1)} %fusion.33.refs_0_), channel_id=1, source_target_pairs={{0,24},{1,25},{2,26},{3,27},{4,28},{5,29},{6,30},{7,31},{8,16},{9,... | collective-permute-start | bytes 516104 | tf_op jit(solution)/shard_map/ppermute | solution.py:45
  59.8 14.3 %copy-start.5 = (bf16[128,384]{1,0:T(8,128)(2,1)S(1)}, bf16[128,384]{1,0:T(8,128)(2,1)}, u32[]{:S(2)}) copy-start(bf16[128,384]{1,0:T(8,128)(2,1)} %get-tuple-element.126.zero_ref.refs_4_) | copy-start | bytes 294916
  59.8 14.3 %copy-start.6 = (s32[5]{0:T(128)S(1)}, s32[5]{0:T(128)}, u32[]{:S(2)}) copy-start(s32[5]{0:T(128)} %stack.23.flags_ref) | copy-start | bytes 64
  59.9 5.9 %collective-permute-start.18 = (bf16[384,896]{1,0:T(8,128)(2,1)S(1)}, bf16[384,896]{1,0:T(8,128)(2,1)S(1)}, u32[]{:S(2)}, u32[]{:S(2)}) collective-permute-start(bf16[384,896]{1,0:T(8,128)(2,1)S(1)} %pad_maximum_fusion.1), channel_id=1, source_target_pairs={{0,4},{1,5},{2,6},{3,7},{4,0},{5,1},{6,2},{7,3},{8,12},{9,13},{10,... | collective-permute-start | bytes 2064392 | tf_op jit(solution)/shard_map/ppermute | solution.py:45
  60.8 11.3 %collective-permute-start.20 = (bf16[128,384]{1,0:T(8,128)(2,1)S(1)}, bf16[128,384]{1,0:T(8,128)(2,1)S(1)}, u32[]{:S(2)}, u32[]{:S(2)}) collective-permute-start(bf16[128,384]{1,0:T(8,128)(2,1)S(1)} %copy-done.42), channel_id=1, source_target_pairs={{0,2},{1,3},{2,0},{3,1},{4,6},{5,7},{6,4},{7,5},{8,10},{9,11},{10,... | collective-permute-start | bytes 294920 | tf_op jit(solution)/shard_map/ppermute | solution.py:45
  64.3 7.9 %collective-permute-start.21 = (bf16[128,384]{1,0:T(8,128)(2,1)S(1)}, bf16[128,384]{1,0:T(8,128)(2,1)S(1)}, u32[]{:S(2)}, u32[]{:S(2)}) collective-permute-start(bf16[128,384]{1,0:T(8,128)(2,1)S(1)} %copy-done.43), channel_id=1, source_target_pairs={{0,3},{1,2},{2,1},{3,0},{4,7},{5,6},{6,5},{7,4},{8,11},{9,10},{10,... | collective-permute-start | bytes 294920 | tf_op jit(solution)/shard_map/ppermute | solution.py:45
  69.3 4.7 %collective-permute-start.19 = (bf16[128,384]{1,0:T(8,128)(2,1)S(1)}, bf16[128,384]{1,0:T(8,128)(2,1)S(1)}, u32[]{:S(2)}, u32[]{:S(2)}) collective-permute-start(bf16[128,384]{1,0:T(8,128)(2,1)S(1)} %copy-done.41), channel_id=1, source_target_pairs={{0,1},{1,0},{2,3},{3,2},{4,5},{5,4},{6,7},{7,6},{8,9},{9,8},{10,11... | collective-permute-start | bytes 294920 | tf_op jit(solution)/shard_map/ppermute | solution.py:45
  75.4 1.4 collective-permute-start.22
  81.1 23.6 %all-to-all-start.1 = ((bf16[32,16,768]{2,1,0:T(8,128)(2,1)}), bf16[32,16,768]{2,1,0:T(8,128)(2,1)S(1)}, u32[]{:S(2)}, u32[]{:S(2)}) async-start(bf16[32,16,768]{2,1,0:T(8,128)(2,1)} %bitcast.77), calls=%async_computation.1 | async-start | bytes 1572864 | tf_op jit(solution)/shard_map/all_to_all | solution.py:793
  117.5 24.0 %all-to-all-start.2 = ((bf16[32,16,768]{2,1,0:T(8,128)(2,1)}), bf16[32,16,768]{2,1,0:T(8,128)(2,1)S(1)}, u32[]{:S(2)}, u32[]{:S(2)}) async-start(bf16[32,16,768]{2,1,0:T(8,128)(2,1)} %bitcast.78), calls=%async_computation.2 | async-start | bytes 1572864 | tf_op jit(solution)/shard_map/all_to_all | solution.py:793
  146.9 2.7 %collective-permute-start.23 = (bf16[128,768]{1,0:T(8,128)(2,1)}, bf16[128,768]{1,0:T(8,128)(2,1)S(1)}, u32[]{:S(2)}, u32[]{:S(2)}) collective-permute-start(bf16[128,768]{1,0:T(8,128)(2,1)} %get-tuple-element.157), channel_id=1, source_target_pairs={{0,4},{1,5},{2,6},{3,7},{4,0},{5,1},{6,2},{7,3},{8,12},{9,13},{10,... | collective-permute-start | bytes 589832 | tf_op jit(solution)/shard_map/ppermute | solution.py:45
  151.8 5.1 %collective-permute-start.24 = (bf16[128,384]{1,0:T(8,128)(2,1)S(1)}, bf16[128,384]{1,0:T(8,128)(2,1)S(1)}, u32[]{:S(2)}, u32[]{:S(2)}) collective-permute-start(bf16[128,384]{1,0:T(8,128)(2,1)S(1)} %get-tuple-element.158), channel_id=1, source_target_pairs={{0,1},{1,0},{2,3},{3,2},{4,5},{5,4},{6,7},{7,6},{8,9},{9,8},{10,11... | collective-permute-start | bytes 294920 | tf_op jit(solution)/shard_map/ppermute | solution.py:45
  153.6 10.1 %collective-permute-start.25 = (bf16[128,384]{1,0:T(8,128)(2,1)S(1)}, bf16[128,384]{1,0:T(8,128)(2,1)S(1)}, u32[]{:S(2)}, u32[]{:S(2)}) collective-permute-start(bf16[128,384]{1,0:T(8,128)(2,1)S(1)} %get-tuple-element.159), channel_id=1, source_target_pairs={{0,2},{1,3},{2,0},{3,1},{4,6},{5,7},{6,4},{7,5},{8,10},{9,11},{10,... | collective-permute-start | bytes 294920 | tf_op jit(solution)/shard_map/ppermute | solution.py:45
  154.4 9.4 %collective-permute-start.26 = (bf16[128,384]{1,0:T(8,128)(2,1)S(1)}, bf16[128,384]{1,0:T(8,128)(2,1)S(1)}, u32[]{:S(2)}, u32[]{:S(2)}) collective-permute-start(bf16[128,384]{1,0:T(8,128)(2,1)S(1)} %get-tuple-element.160), channel_id=1, source_target_pairs={{0,3},{1,2},{2,1},{3,0},{4,7},{5,6},{6,5},{7,4},{8,11},{9,10},{10,... | collective-permute-start | bytes 294920 | tf_op jit(solution)/shard_map/ppermute | solution.py:45
  163.8 22.4 %all-to-all-start.3 = ((bf16[32,16,768]{2,1,0:T(8,128)(2,1)}), bf16[32,16,768]{2,1,0:T(8,128)(2,1)S(1)}, u32[]{:S(2)}, u32[]{:S(2)}) async-start(bf16[32,16,768]{2,1,0:T(8,128)(2,1)} %bitcast.21), calls=%async_computation.3 | async-start | bytes 1572864 | tf_op jit(solution)/shard_map/all_to_all | solution.py:793
  175.7 2.6 %collective-permute-start.27 = (bf16[2,512,384]{2,1,0:T(8,128)(2,1)}, bf16[2,512,384]{2,1,0:T(8,128)(2,1)S(1)}, u32[]{:S(2)}, u32[]{:S(2)}) collective-permute-start(bf16[2,512,384]{2,1,0:T(8,128)(2,1)} %get-tuple-element.171), channel_id=1, source_target_pairs={{0,4},{1,5},{2,6},{3,7},{4,0},{5,1},{6,2},{7,3},{8,12},{9,13},{10,... | collective-permute-start | bytes 2359304 | tf_op jit(solution)/shard_map/ppermute | solution.py:45
  186.2 4.8 %collective-permute-start.28 = (bf16[384,2048]{1,0:T(8,128)(2,1)}, bf16[384,2048]{1,0:T(8,128)(2,1)S(1)}, u32[]{:S(2)}, u32[]{:S(2)}) collective-permute-start(bf16[384,2048]{1,0:T(8,128)(2,1)} %get-tuple-element.179), channel_id=1, source_target_pairs={{0,4},{1,5},{2,6},{3,7},{4,0},{5,1},{6,2},{7,3},{8,12},{9,13},{10,... | collective-permute-start | bytes 4718600 | tf_op jit(solution)/shard_map/ppermute | solution.py:45
  192.0 7.1 %collective-permute-start.29 = (bf16[128,768]{1,0:T(8,128)(2,1)S(1)}, bf16[128,768]{1,0:T(8,128)(2,1)S(1)}, u32[]{:S(2)}, u32[]{:S(2)}) collective-permute-start(bf16[128,768]{1,0:T(8,128)(2,1)S(1)} %get-tuple-element.213), channel_id=1, source_target_pairs={{0,1},{1,0},{2,3},{3,2},{4,5},{5,4},{6,7},{7,6},{8,9},{9,8},{10,11... | collective-permute-start | bytes 589832 | tf_op jit(solution)/shard_map/ppermute | solution.py:45
  193.9 18.7 %collective-permute-start.32 = (bf16[96,2048]{1,0:T(8,128)(2,1)S(1)}, bf16[96,2048]{1,0:T(8,128)(2,1)S(1)}, u32[]{:S(2)}, u32[]{:S(2)}) collective-permute-start(bf16[96,2048]{1,0:T(8,128)(2,1)S(1)} %get-tuple-element.207), channel_id=1, source_target_pairs={{0,8},{1,9},{2,10},{3,11},{4,12},{5,13},{6,14},{7,15},{8,0},{9,1},... | collective-permute-start | bytes 1179656 | tf_op jit(solution)/shard_map/ppermute | solution.py:45
  193.9 19.5 %collective-permute-start.33 = (bf16[96,2048]{1,0:T(8,128)(2,1)S(1)}, bf16[96,2048]{1,0:T(8,128)(2,1)S(1)}, u32[]{:S(2)}, u32[]{:S(2)}) collective-permute-start(bf16[96,2048]{1,0:T(8,128)(2,1)S(1)} %get-tuple-element.206), channel_id=1, source_target_pairs={{0,16},{1,17},{2,18},{3,19},{4,20},{5,21},{6,22},{7,23},{8,24},{9,... | collective-permute-start | bytes 1179656 | tf_op jit(solution)/shard_map/ppermute | solution.py:45
  195.1 18.3 %collective-permute-start.34 = (bf16[96,2048]{1,0:T(8,128)(2,1)S(1)}, bf16[96,2048]{1,0:T(8,128)(2,1)S(1)}, u32[]{:S(2)}, u32[]{:S(2)}) collective-permute-start(bf16[96,2048]{1,0:T(8,128)(2,1)S(1)} %get-tuple-element.205), channel_id=1, source_target_pairs={{0,24},{1,25},{2,26},{3,27},{4,28},{5,29},{6,30},{7,31},{8,16},{9,... | collective-permute-start | bytes 1179656 | tf_op jit(solution)/shard_map/ppermute | solution.py:45
  197.4 15.1 %collective-permute-start.30 = (bf16[128,768]{1,0:T(8,128)(2,1)S(1)}, bf16[128,768]{1,0:T(8,128)(2,1)S(1)}, u32[]{:S(2)}, u32[]{:S(2)}) collective-permute-start(bf16[128,768]{1,0:T(8,128)(2,1)S(1)} %get-tuple-element.212), channel_id=1, source_target_pairs={{0,2},{1,3},{2,0},{3,1},{4,6},{5,7},{6,4},{7,5},{8,10},{9,11},{10,... | collective-permute-start | bytes 589832 | tf_op jit(solution)/shard_map/ppermute | solution.py:45
  199.1 13.5 %collective-permute-start.31 = (bf16[128,768]{1,0:T(8,128)(2,1)S(1)}, bf16[128,768]{1,0:T(8,128)(2,1)S(1)}, u32[]{:S(2)}, u32[]{:S(2)}) collective-permute-start(bf16[128,768]{1,0:T(8,128)(2,1)S(1)} %get-tuple-element.211), channel_id=1, source_target_pairs={{0,3},{1,2},{2,1},{3,0},{4,7},{5,6},{6,5},{7,4},{8,11},{9,10},{10,... | collective-permute-start | bytes 589832 | tf_op jit(solution)/shard_map/ppermute | solution.py:45
  213.8 6.3 %collective-permute-start.35 = (bf16[128,768]{1,0:T(8,128)(2,1)S(1)}, bf16[128,768]{1,0:T(8,128)(2,1)S(1)}, u32[]{:S(2)}, u32[]{:S(2)}) collective-permute-start(bf16[128,768]{1,0:T(8,128)(2,1)S(1)} %broadcast_select_fusion.6), channel_id=1, source_target_pairs={{0,4},{1,5},{2,6},{3,7},{4,0},{5,1},{6,2},{7,3},{8,12},{9,13},{10,... | collective-permute-start | bytes 589832 | tf_op jit(solution)/shard_map/ppermute | solution.py:45
  213.9 7.9 %collective-permute-start.37 = (bf16[24,2048]{1,0:T(8,128)(2,1)S(1)}, bf16[24,2048]{1,0:T(8,128)(2,1)S(1)}, u32[]{:S(2)}, u32[]{:S(2)}) collective-permute-start(bf16[24,2048]{1,0:T(8,128)(2,1)S(1)} %get-tuple-element.209), channel_id=1, source_target_pairs={{0,2},{1,3},{2,0},{3,1},{4,6},{5,7},{6,4},{7,5},{8,10},{9,11},{10,... | collective-permute-start | bytes 294920 | tf_op jit(solution)/shard_map/ppermute | solution.py:45
  217.3 8.5 %collective-permute-start.38 = (bf16[24,2048]{1,0:T(8,128)(2,1)S(1)}, bf16[24,2048]{1,0:T(8,128)(2,1)S(1)}, u32[]{:S(2)}, u32[]{:S(2)}) collective-permute-start(bf16[24,2048]{1,0:T(8,128)(2,1)S(1)} %get-tuple-element.208), channel_id=1, source_target_pairs={{0,3},{1,2},{2,1},{3,0},{4,7},{5,6},{6,5},{7,4},{8,11},{9,10},{10,... | collective-permute-start | bytes 294920 | tf_op jit(solution)/shard_map/ppermute | solution.py:45
  221.8 5.8 %collective-permute-start.36 = (bf16[24,2048]{1,0:T(8,128)(2,1)S(1)}, bf16[24,2048]{1,0:T(8,128)(2,1)S(1)}, u32[]{:S(2)}, u32[]{:S(2)}) collective-permute-start(bf16[24,2048]{1,0:T(8,128)(2,1)S(1)} %get-tuple-element.192), channel_id=1, source_target_pairs={{0,1},{1,0},{2,3},{3,2},{4,5},{5,4},{6,7},{7,6},{8,9},{9,8},{10,11... | collective-permute-start | bytes 294920 | tf_op jit(solution)/shard_map/ppermute | solution.py:45
  (42 other events, 223.7 us)
